TPU v7x, 32 devices: a whole 2x2x4 slice. The times are simulated.
32 devices in a mesh: parts: 2 (over x), tm: 16 (over z, y, core).
Axes of the slice: x: 2, y: 2, z: 4, core: 2. Of those that a mesh axis runs over, the one named last changes fastest.
Arguments:
- query_states: bfloat16 [32, 384, 768], P(('parts', 'tm')), parts along dimension 0, may hold values from -88 to 88
- key_states: bfloat16 [32, 384, 768], P(('parts', 'tm')), parts along dimension 0, may hold values from -4 to 4
- value_states: bfloat16 [32, 384, 768], P(('parts', 'tm')), parts along dimension 0, may hold values from -40 to 40
- out_weight: bfloat16 [1536, 3072], replicated, may hold values from -0.15625 to 0.15625
Outputs:
- mixed: bfloat16 [6144, 3072], P(('parts', 'tm')), parts along dimension 0
There are 2 independent parts, one for each index of `parts`. A program takes and returns all parts, laid end to end along the dimension named above; an argument that names none is the same for every part. Nothing has to cross between parts.
All inputs are finite; a program needn't handle non-finite values.
Results may differ from a plain program's by a relative error of at most 0.0058.
Values may be sent and summed in bfloat16 or wider, within the bound.
No kernel may reach another device: no remote copies, remote signals or barrier semaphores. Data moves between devices by JAX's collectives and lax.ppermute only.
A program may use at most 128 MiB of HBM per device.

v0:
```python
import jax
import jax.numpy as jnp
from jax import lax
from jax.sharding import PartitionSpec as P

TCOLS = 4
HD = 128


masked_score = -1e30


def from_behind(block, axis, distance):
    devices = range(lax.axis_size(axis))
    route = [(i - distance, i) for i in devices if i - distance in devices]
    return lax.ppermute(block, axis, route)


def swapped(shard, axis, bit):
    return lax.ppermute(shard, axis, [(i, i ^ 1 << bit) for i in range(lax.axis_size(axis))])


def tile_from(stacked, offset):
    return from_behind(stacked, "tm", -2 * offset)


def window_direct(stacked):
    blocks = []
    for time_step in (-1, 0, 1):
        for col_step in (-1, 0, 1):
            if time_step == 0 and col_step == 0:
                blocks.append(stacked)
            else:
                blocks.append(tile_from(stacked, time_step * TCOLS + col_step))
    return jnp.concatenate(blocks, axis=1)


def window_attention(query_tile, key_window, value_window, key_ok):
    score_scale = HD ** (-0.5)
    tile_rows = query_tile.shape[0]
    key_rows = key_window.shape[0]
    heads_here = query_tile.shape[1] // HD
    per_step = 2
    pieces = []
    for head_start in range(0, heads_here, per_step):
        first_col = head_start * HD
        last_col = first_col + per_step * HD
        query_part = query_tile[:, first_col:last_col].reshape(tile_rows, per_step, HD)
        key_part = key_window[:, first_col:last_col].reshape(key_rows, per_step, HD)
        value_part = value_window[:, first_col:last_col].reshape(key_rows, per_step, HD)
        scores = (
            lax.dot_general(
                query_part,
                key_part,
                (((2,), (2,)), ((1,), (1,))),
                preferred_element_type=jnp.float32,
            )
            * score_scale
        )
        scores = jnp.where(key_ok[None, None, :], scores, masked_score)
        row_max = jnp.max(scores, axis=2, keepdims=True)
        exp_scores = jnp.exp(scores - row_max)
        denominator = jnp.sum(exp_scores, axis=2, keepdims=True)
        weights = (exp_scores / denominator).astype(jnp.bfloat16)
        result = lax.dot_general(
            weights, value_part, (((2,), (0,)), ((0,), (1,))), preferred_element_type=jnp.float32
        )
        result = result.astype(jnp.bfloat16).transpose(1, 0, 2).reshape(tile_rows, per_step * HD)
        pieces.append(result)
    return jnp.concatenate(pieces, axis=1)


def per_device(query_states, key_states, value_states, out_weight):
    query_tile = query_states[0]
    key_tile = key_states[0]
    value_tile = value_states[0]
    tile_rows = query_tile.shape[0]
    half_width = query_tile.shape[1]
    half_rows = tile_rows // 2
    position = lax.axis_index("tm")
    device_count = lax.axis_size("tm")
    head_group = position % 2
    other_group = 1 - head_group
    tile_index = position // 2
    col_tile = tile_index % TCOLS
    time_tile = tile_index // TCOLS
    time_count = device_count // (2 * TCOLS)
    stacked = jnp.stack((key_tile, value_tile))
    window_stack = window_direct(stacked)
    tile_steps = jnp.arange(3, dtype=jnp.int32) - 1
    time_ok = (time_tile + tile_steps >= 0) & (time_tile + tile_steps < time_count)
    col_ok = (col_tile + tile_steps >= 0) & (col_tile + tile_steps < TCOLS)
    tile_ok = (time_ok[:, None] & col_ok[None, :]).reshape(9)
    key_ok = jnp.repeat(tile_ok, tile_rows)
    attended = window_attention(query_tile, window_stack[0], window_stack[1], key_ok)
    weight_own = lax.dynamic_slice_in_dim(out_weight, head_group * half_width, half_width, 0)
    own_attended = lax.dynamic_slice_in_dim(attended, head_group * half_rows, half_rows, 0)
    other_attended = lax.dynamic_slice_in_dim(attended, other_group * half_rows, half_rows, 0)
    received = swapped(other_attended, "tm", 0)
    weight_other = lax.dynamic_slice_in_dim(out_weight, other_group * half_width, half_width, 0)
    mixed_rows = jnp.dot(own_attended, weight_own, preferred_element_type=jnp.float32) + jnp.dot(
        received, weight_other, preferred_element_type=jnp.float32
    )
    return mixed_rows.astype(jnp.bfloat16)


def solution(mesh):
    in_specs = (
        P(("parts", "tm"), None, None),
        P(("parts", "tm"), None, None),
        P(("parts", "tm"), None, None),
        P(),
    )
    out_specs = P(("parts", "tm"), None)
    return jax.shard_map(
        per_device, mesh=mesh, in_specs=in_specs, out_specs=out_specs, check_vma=False
    )
```

profile of v0, /device:TPU:1, one launch (start us, length us, event | category | flops | bytes accessed | tf_op | source)
XLA Modules:
  0.0 298.3 jit_solution(15766207930555600884)
XLA Ops:
  0.0 1.4 copy.11
  1.4 1.4 copy.12
  2.7 0.1 pad_maximum_fusion
  2.9 7.0 %collective-permute-start = (bf16[2,384,768]{1,2,0:T(8,128)(2,1)S(1)}, bf16[2,384,768]{1,2,0:T(8,128)(2,1)}, u32[]{:S(2)}, u32[]{:S(2)}) collective-permute-start(bf16[2,384,768]{1,2,0:T(8,128)(2,1)S(1)} %pad_maximum_fusion), channel_id=1, source_target_pairs={{0,10},{1,11},{2,12},{3,13},{4,14},{5,15},{16,26},{17,27},{18,28},... | collective-permute-start | bytes 3538952 | tf_op jit(solution)/shard_map/ppermute | solution.py:16
  9.9 2.4 collective-permute-start.1
  12.3 3.2 %collective-permute-start.2 = (bf16[2,384,768]{1,2,0:T(8,128)(2,1)S(1)}, bf16[2,384,768]{1,2,0:T(8,128)(2,1)}, u32[]{:S(2)}, u32[]{:S(2)}) collective-permute-start(bf16[2,384,768]{1,2,0:T(8,128)(2,1)S(1)} %pad_maximum_fusion), channel_id=1, source_target_pairs={{0,6},{1,7},{2,8},{3,9},{4,10},{5,11},{6,12},{7,13},{8,14},{9,15},... | collective-permute-start | bytes 3538952 | tf_op jit(solution)/shard_map/ppermute | solution.py:16
  15.5 3.3 %collective-permute-start.3 = (bf16[2,384,768]{1,2,0:T(8,128)(2,1)S(1)}, bf16[2,384,768]{1,2,0:T(8,128)(2,1)}, u32[]{:S(2)}, u32[]{:S(2)}) collective-permute-start(bf16[2,384,768]{1,2,0:T(8,128)(2,1)S(1)} %pad_maximum_fusion), channel_id=1, source_target_pairs={{0,2},{1,3},{2,4},{3,5},{4,6},{5,7},{6,8},{7,9},{8,10},{9,11},{10,... | collective-permute-start | bytes 3538952 | tf_op jit(solution)/shard_map/ppermute | solution.py:16
  18.8 1.3 collective-permute-start.4
  20.1 1.4 copy.13
  21.5 0.8 fusion.57
  22.3 24.5 %collective-permute-done = bf16[2,384,768]{1,2,0:T(8,128)(2,1)} collective-permute-done((bf16[2,384,768]{1,2,0:T(8,128)(2,1)S(1)}, bf16[2,384,768]{1,2,0:T(8,128)(2,1)}, u32[]{:S(2)}, u32[]{:S(2)}) %collective-permute-start) | collective-permute-done | bytes 1179680 | tf_op jit(solution)/shard_map/ppermute | solution.py:16
  46.8 1.3 collective-permute-start.5
  48.1 24.7 %collective-permute-done.1 = bf16[2,384,768]{1,2,0:T(8,128)(2,1)} collective-permute-done((bf16[2,384,768]{1,2,0:T(8,128)(2,1)S(1)}, bf16[2,384,768]{1,2,0:T(8,128)(2,1)}, u32[]{:S(2)}, u32[]{:S(2)}) %collective-permute-start.1) | collective-permute-done | bytes 1179680 | tf_op jit(solution)/shard_map/ppermute | solution.py:16
  72.8 1.3 collective-permute-start.6
  74.1 36.4 %collective-permute-done.2 = bf16[2,384,768]{1,2,0:T(8,128)(2,1)} collective-permute-done((bf16[2,384,768]{1,2,0:T(8,128)(2,1)S(1)}, bf16[2,384,768]{1,2,0:T(8,128)(2,1)}, u32[]{:S(2)}, u32[]{:S(2)}) %collective-permute-start.2) | collective-permute-done | bytes 1179680 | tf_op jit(solution)/shard_map/ppermute | solution.py:16
  110.5 1.3 collective-permute-start.7
  111.8 0.1 broadcast_and_fusion
  111.8 0.1 and.58
  111.9 0.1 broadcast_in_dim.33
  112.1 2.5 constant_dynamic-update-slice_fusion.8
  114.5 2.4 constant_dynamic-update-slice_fusion.7
  116.9 2.5 constant_dynamic-update-slice_fusion.6
  119.4 0.0 collective-permute-done.3
  119.4 2.5 constant_dynamic-update-slice_fusion.5
  121.9 1.2 constant_dynamic-update-slice_fusion.4
  123.1 2.4 constant_dynamic-update-slice_fusion.3
  125.5 0.0 collective-permute-done.5
  125.5 2.5 constant_dynamic-update-slice_fusion.2
  128.0 43.2 %collective-permute-done.6 = bf16[2,384,768]{1,2,0:T(8,128)(2,1)} collective-permute-done((bf16[2,384,768]{1,2,0:T(8,128)(2,1)S(1)}, bf16[2,384,768]{1,2,0:T(8,128)(2,1)}, u32[]{:S(2)}, u32[]{:S(2)}) %collective-permute-start.6) | collective-permute-done | bytes 1179680 | tf_op jit(solution)/shard_map/ppermute | solution.py:16
  171.2 2.5 constant_dynamic-update-slice_fusion.1
  173.6 56.1 %collective-permute-done.7 = bf16[2,384,768]{1,2,0:T(8,128)(2,1)} collective-permute-done((bf16[2,384,768]{1,2,0:T(8,128)(2,1)S(1)}, bf16[2,384,768]{1,2,0:T(8,128)(2,1)}, u32[]{:S(2)}, u32[]{:S(2)}) %collective-permute-start.7) | collective-permute-done | bytes 1179680 | tf_op jit(solution)/shard_map/ppermute | solution.py:16
  229.7 2.5 constant_dynamic-update-slice_fusion
  232.2 8.7 %slice_bitcast_fusion = (bf16[3456,768]{0,1:T(8,128)(2,1)}, bf16[3456,768]{0,1:T(8,128)(2,1)}) fusion(bf16[2,3456,768]{1,2,0:T(8,128)(2,1)} %constant_dynamic-update-slice_fusion), kind=kLoop, calls=%fused_computation.21 | loop fusion | bytes 21233664 | tf_op jit(solution)/shard_map/squeeze | solution.py:95
  240.9 7.3 %fusion.55 = (bf16[3456,256]{0,1:T(8,128)(2,1)}, bf16[3456,256]{0,1:T(8,128)(2,1)}, bf16[3456,256]{0,1:T(8,128)(2,1)}, bf16[3456,256]{0,1:T(8,128)(2,1)S(1)}, bf...) fusion(bf16[3456,768]{0,1:T(8,128)(2,1)} %get-tuple-element.5, bf16[3456,768]{0,1:T(8,128)(2,1)} %get-tuple-element.6), kind=kLoop, calls=%fused_computation.72 | loop fusion | bytes 21233664 | tf_op jit(solution)/shard_map/slice | solution.py:49
  248.2 9.4 %fusion.60 = (f32[2,384]{1,0:T(2,128)S(1)}, f32[2,384,3456]{1,2,0:T(8,128)}) fusion(pred[3456]{0:T(1024)(128)(4,1)S(1)} %broadcast_in_dim.34, bf16[3456,2,128]{0,2,1:T(8,128)(2,1)} %bitcast.78, bf16[384,2,128]{0,2,1:T(8,128)(2,1)} %bitcast.81), kind=kOutput, calls=%fused_computation.77 | convolution fusion | flops 690097536 | bytes 12589440 | tf_op jit(solution)/shard_map/sub | solution.py:62
  257.6 9.2 %fusion.59 = (f32[2,384]{1,0:T(2,128)S(1)}, f32[2,384,3456]{1,2,0:T(8,128)}) fusion(pred[3456]{0:T(1024)(128)(4,1)S(1)} %broadcast_in_dim.34, bf16[3456,2,128]{0,2,1:T(8,128)(2,1)} %bitcast.77, bf16[384,2,128]{0,2,1:T(8,128)(2,1)} %bitcast.80), kind=kOutput, calls=%fused_computation.76 | convolution fusion | flops 690097536 | bytes 12589440 | tf_op jit(solution)/shard_map/sub | solution.py:62
  266.8 9.6 %fusion.58 = (f32[2,384]{1,0:T(2,128)S(1)}, f32[2,384,3456]{1,2,0:T(8,128)}) fusion(pred[3456]{0:T(1024)(128)(4,1)S(1)} %broadcast_in_dim.34, bf16[3456,2,128]{0,2,1:T(8,128)(2,1)} %bitcast.76, bf16[384,2,128]{0,2,1:T(8,128)(2,1)} %bitcast.79), kind=kOutput, calls=%fused_computation.75 | convolution fusion | flops 690097536 | bytes 12589440 | tf_op jit(solution)/shard_map/sub | solution.py:62
  276.4 5.8 %fusion.39 = bf16[2,384,128]{1,2,0:T(8,128)(2,1)S(1)} fusion(bf16[3456,2,128]{0,2,1:T(8,128)(2,1)} %bitcast.75, f32[2,384,3456]{1,2,0:T(8,128)} %get-tuple-element.21, f32[2,384]{1,0:T(2,128)S(1)} %get-tuple-element.20), kind=kOutput, calls=%fused_computation.44 | convolution fusion | flops 684883968 | bytes 12585984 | tf_op jit(solution)/shard_map/dot_general | solution.py:65
  282.2 1.7 copy-done
  284.0 1.2 fusion.38
  285.2 1.2 slice-done.1
  286.3 0.9 slice-done.2
  287.2 1.2 fusion.37
  288.4 0.1 pad_maximum_fusion.1
  288.5 0.2 constant_dynamic-slice_fusion
  288.7 1.5 collective-permute-start.8
  290.2 3.5 %fusion.29 = f32[192,3072]{1,0:T(8,128)S(1)} fusion(bf16[1536,3072]{1,0:T(8,128)(2,1)} %param.7, s32[]{:T(128)S(6)} %select_n.60, bf16[384,768]{0,1:T(8,128)(2,1)S(1)} %pad_maximum_fusion.1, s32[]{:T(128)S(6)} %select_n.59), kind=kOutput, calls=%fused_computation.37 | convolution fusion | flops 905969664 | bytes 7471112 | tf_op jit(solution)/shard_map/dot_general | solution.py:101
  293.8 4.5 %fusion.34 = bf16[192,3072]{1,0:T(8,128)(2,1)} fusion(f32[192,3072]{1,0:T(8,128)S(1)} %fusion.29, bf16[192,768]{0,1:T(8,128)(2,1)S(1)} %collective-permute-done.8, bf16[1536,3072]{1,0:T(8,128)(2,1)} %param.7, s32[]{:T(128)S(6)} %select_n.62), kind=kOutput, calls=%fused_computation.40 | convolution fusion | flops 907149312 | bytes 8552452 | tf_op jit(solution)/shard_map/dot_general | solution.py:101
  (10 shorter events, 0.0 us)
Async XLA Ops:
  2.9 43.9 %collective-permute-start = (bf16[2,384,768]{1,2,0:T(8,128)(2,1)S(1)}, bf16[2,384,768]{1,2,0:T(8,128)(2,1)}, u32[]{:S(2)}, u32[]{:S(2)}) collective-permute-start(bf16[2,384,768]{1,2,0:T(8,128)(2,1)S(1)} %pad_maximum_fusion), channel_id=1, source_target_pairs={{0,10},{1,11},{2,12},{3,13},{4,14},{5,15},{16,26},{17,27},{18,28},... | collective-permute-start | bytes 3538952 | tf_op jit(solution)/shard_map/ppermute | solution.py:16
  9.9 62.9 %collective-permute-start.1 = (bf16[2,384,768]{1,2,0:T(8,128)(2,1)S(1)}, bf16[2,384,768]{1,2,0:T(8,128)(2,1)}, u32[]{:S(2)}, u32[]{:S(2)}) collective-permute-start(bf16[2,384,768]{1,2,0:T(8,128)(2,1)S(1)} %pad_maximum_fusion), channel_id=1, source_target_pairs={{0,8},{1,9},{2,10},{3,11},{4,12},{5,13},{6,14},{7,15},{16,24},{17,... | collective-permute-start | bytes 3538952 | tf_op jit(solution)/shard_map/ppermute | solution.py:16
  12.3 98.2 %collective-permute-start.2 = (bf16[2,384,768]{1,2,0:T(8,128)(2,1)S(1)}, bf16[2,384,768]{1,2,0:T(8,128)(2,1)}, u32[]{:S(2)}, u32[]{:S(2)}) collective-permute-start(bf16[2,384,768]{1,2,0:T(8,128)(2,1)S(1)} %pad_maximum_fusion), channel_id=1, source_target_pairs={{0,6},{1,7},{2,8},{3,9},{4,10},{5,11},{6,12},{7,13},{8,14},{9,15},... | collective-permute-start | bytes 3538952 | tf_op jit(solution)/shard_map/ppermute | solution.py:16
  15.5 103.9 %collective-permute-start.3 = (bf16[2,384,768]{1,2,0:T(8,128)(2,1)S(1)}, bf16[2,384,768]{1,2,0:T(8,128)(2,1)}, u32[]{:S(2)}, u32[]{:S(2)}) collective-permute-start(bf16[2,384,768]{1,2,0:T(8,128)(2,1)S(1)} %pad_maximum_fusion), channel_id=1, source_target_pairs={{0,2},{1,3},{2,4},{3,5},{4,6},{5,7},{6,8},{7,9},{8,10},{9,11},{10,... | collective-permute-start | bytes 3538952 | tf_op jit(solution)/shard_map/ppermute | solution.py:16
  18.8 104.3 %collective-permute-start.4 = (bf16[2,384,768]{1,2,0:T(8,128)(2,1)S(1)}, bf16[2,384,768]{1,2,0:T(8,128)(2,1)}, u32[]{:S(2)}, u32[]{:S(2)}) collective-permute-start(bf16[2,384,768]{1,2,0:T(8,128)(2,1)S(1)} %pad_maximum_fusion), channel_id=1, source_target_pairs={{2,0},{3,1},{4,2},{5,3},{6,4},{7,5},{8,6},{9,7},{10,8},{11,9},{12,... | collective-permute-start | bytes 3538952 | tf_op jit(solution)/shard_map/ppermute | solution.py:16
  46.8 78.7 %collective-permute-start.5 = (bf16[2,384,768]{1,2,0:T(8,128)(2,1)S(1)}, bf16[2,384,768]{1,2,0:T(8,128)(2,1)}, u32[]{:S(2)}, u32[]{:S(2)}) collective-permute-start(bf16[2,384,768]{1,2,0:T(8,128)(2,1)S(1)} %pad_maximum_fusion), channel_id=1, source_target_pairs={{6,0},{7,1},{8,2},{9,3},{10,4},{11,5},{12,6},{13,7},{14,8},{15,9},... | collective-permute-start | bytes 3538952 | tf_op jit(solution)/shard_map/ppermute | solution.py:16
  72.8 98.3 %collective-permute-start.6 = (bf16[2,384,768]{1,2,0:T(8,128)(2,1)S(1)}, bf16[2,384,768]{1,2,0:T(8,128)(2,1)}, u32[]{:S(2)}, u32[]{:S(2)}) collective-permute-start(bf16[2,384,768]{1,2,0:T(8,128)(2,1)S(1)} %pad_maximum_fusion), channel_id=1, source_target_pairs={{8,0},{9,1},{10,2},{11,3},{12,4},{13,5},{14,6},{15,7},{24,16},{25,... | collective-permute-start | bytes 3538952 | tf_op jit(solution)/shard_map/ppermute | solution.py:16
  110.5 119.3 %collective-permute-start.7 = (bf16[2,384,768]{1,2,0:T(8,128)(2,1)S(1)}, bf16[2,384,768]{1,2,0:T(8,128)(2,1)}, u32[]{:S(2)}, u32[]{:S(2)}) collective-permute-start(bf16[2,384,768]{1,2,0:T(8,128)(2,1)S(1)} %pad_maximum_fusion), channel_id=1, source_target_pairs={{10,0},{11,1},{12,2},{13,3},{14,4},{15,5},{26,16},{27,17},{28,18},... | collective-permute-start | bytes 3538952 | tf_op jit(solution)/shard_map/ppermute | solution.py:16
  276.4 7.6 %copy-start = (f32[2,384,3456]{1,2,0:T(8,128)S(1)}, f32[2,384,3456]{1,2,0:T(8,128)}, u32[]{:S(2)}) copy-start(f32[2,384,3456]{1,2,0:T(8,128)} %get-tuple-element.19) | copy-start | bytes 31850500
  276.4 8.8 %slice-start = ((s8[10616832]{0:T(1024)(128)(4,1)}), s8[4194304]{0:T(1024)(128)(4,1)S(1)}, s32[]{:S(2)}) async-start(s8[10616832]{0:T(1024)(128)(4,1)} %bitcast.85), calls=%async_computation | async-start | bytes 8388608
  276.4 9.9 %slice-start.1 = ((s8[10616832]{0:T(1024)(128)(4,1)}), s8[4194304]{0:T(1024)(128)(4,1)S(1)}, s32[]{:S(2)}) async-start(s8[10616832]{0:T(1024)(128)(4,1)} %bitcast.85), calls=%async_computation.1 | async-start | bytes 8388608
  284.0 3.3 %slice-start.2 = ((s8[10616832]{0:T(1024)(128)(4,1)}), s8[2228224]{0:T(1024)(128)(4,1)S(1)}, s32[]{:S(2)}) async-start(s8[10616832]{0:T(1024)(128)(4,1)} %bitcast.85), calls=%async_computation.2 | async-start | bytes 4456448
  288.7 5.0 %collective-permute-start.8 = (bf16[192,768]{0,1:T(8,128)(2,1)S(1)}, bf16[192,768]{0,1:T(8,128)(2,1)S(1)}, u32[]{:S(2)}, u32[]{:S(2)}) collective-permute-start(bf16[192,768]{0,1:T(8,128)(2,1)S(1)} %constant_dynamic-slice_fusion), channel_id=1, source_target_pairs={{0,1},{1,0},{2,3},{3,2},{4,5},{5,4},{6,7},{7,6},{8,9},{9,8},{10,11... | collective-permute-start | bytes 884744 | tf_op jit(solution)/shard_map/ppermute | solution.py:20
where the time goes:
time: 299 us; the launch traced here: 298 us
  waiting for transfers between devices  185 us (62%)
  local copies, waits for them, and re-layouts  44.8 us (15%)
  matrix products  44.5 us (15%)
  starting transfers between devices  22.5 us (8%)
    ppermute x8, waiting for transfers between devices, from_behind(): return lax.ppermute(block, axis, route)  185 us
    sub x3, matrix products, window_attention(): exp_scores = jnp.exp(scores - row_max)  28.2 us
    unnamed x18, local copies, waits for them, and re-layouts  25.1 us
    ppermute x8, starting transfers between devices, from_behind(): return lax.ppermute(block, axis, route)  21 us
    squeeze x1, local copies, waits for them, and re-layouts, per_device(): window_stack[0]  8.69 us
    dot_general x3, matrix products, window_attention(): lax.dot_general(weights, value_part, (((2,), (0,)), ((0,), (1,))), prefer...  8.23 us
    slice x1, local copies, waits for them, and re-layouts, window_attention(): key_part = key_window[:, first_col:last_col].reshape(key_rows, per_step, HD)  7.32 us
  transfers between devices with their start and end apart: 9, of which 5 were waited for; matrix products, arithmetic and copies ran while one was open for 8% of the time, Pallas kernels for 0%

commit v1 on v0

v1 whole, which is shorter than its diff:
```python
import functools
import math

import jax
import jax.numpy as jnp
from jax import lax
from jax.experimental import pallas as pl
from jax.experimental.pallas import tpu as pltpu
from jax.sharding import PartitionSpec as P

TCOLS = 4
HD = 128
CHUNK_HEADS = 2
STAT_ROWS = 16
EXP2_SCALE = HD ** (-0.5) * math.log2(math.e)
MASKED = -1e30
VMEM_BYTES = 48 * 1024 * 1024


def dot_rows(a, b):
    return lax.dot_general(a, b, (((1,), (1,)), ((), ())), preferred_element_type=jnp.float32)


def attend_kernel(q_ref, own_ref, next_ref, far_ref, same_ref, cross_ref):
    position = lax.axis_index("tm")
    group = position % 2
    col = (position // 2) % TCOLS
    far_ok = (col == 1) | (col == 2)
    rows = q_ref.shape[0]
    half = rows // 2
    width = q_ref.shape[1]
    stats = []
    outs = []
    for head in range(width // HD):
        cols = slice(head * HD, (head + 1) * HD)
        query = q_ref[:, cols]
        s_own = dot_rows(own_ref[0, :, cols], query)
        s_next = dot_rows(next_ref[0, :, cols], query)
        s_far = dot_rows(far_ref[0, :, cols], query)
        s_far = jnp.where(far_ok, s_far, MASKED)
        top = jnp.maximum(jnp.maximum(s_own, s_next), s_far)
        top = jnp.max(top, axis=0, keepdims=True).astype(jnp.bfloat16).astype(jnp.float32)
        total = jnp.zeros((1, rows), jnp.float32)
        out = jnp.zeros((HD, rows), jnp.float32)
        for scores, ref in ((s_own, own_ref), (s_next, next_ref), (s_far, far_ref)):
            probs = jnp.exp2((scores - top) * EXP2_SCALE)
            total += jnp.sum(probs, axis=0, keepdims=True)
            out += lax.dot_general(
                ref[1, :, cols],
                probs.astype(jnp.bfloat16),
                (((0,), (0,)), ((), ())),
                preferred_element_type=jnp.float32,
            )
        high = total.astype(jnp.bfloat16).astype(jnp.float32)
        stats += [top, high, total - high]
        outs.append(out.T.astype(jnp.bfloat16))
    stats.append(jnp.zeros((STAT_ROWS - len(stats), rows), jnp.float32))
    stats = jnp.concatenate(stats, axis=0).astype(jnp.bfloat16)
    out = jnp.concatenate(outs, axis=1)

    def put(ref, part):
        ref[:half, :] = out[part * half : (part + 1) * half]
        first = part * (rows - width)
        ref[half:, :] = stats[:, first : first + width]

    @pl.when(group == 0)
    def _():
        put(same_ref, 0)
        put(cross_ref, 1)

    @pl.when(group == 1)
    def _():
        put(same_ref, 1)
        put(cross_ref, 0)


def attend(query, own, nxt, far):
    rows, width = query.shape
    keys = 3 * own.shape[1]
    out = jax.ShapeDtypeStruct((rows // 2 + STAT_ROWS, width), jnp.bfloat16)
    return pl.pallas_call(
        attend_kernel,
        out_shape=(out, out),
        compiler_params=pltpu.CompilerParams(vmem_limit_bytes=VMEM_BYTES),
        cost_estimate=pl.CostEstimate(
            flops=4 * rows * keys * width,
            bytes_accessed=2 * width * (2 * rows + 2 * keys),
            transcendentals=rows * keys * width // HD,
        ),
        name="attend",
    )(query, own, nxt, far)


def merge(refs, oks, half, width, part):
    shift = width - half
    parts = []
    for ref, ok in zip(refs, oks):
        stats = ref[half:, :].astype(jnp.float32).T
        stats = jnp.where(part == 0, stats[:half], stats[shift:])
        parts.append((ref[:half, :].astype(jnp.float32), stats, ok))
    heads = []
    for head in range(width // HD):
        cols = slice(head * HD, (head + 1) * HD)
        tops, sums = [], []
        for _, stats, ok in parts:
            top = stats[:, 3 * head : 3 * head + 1]
            tops.append(top if ok is None else jnp.where(ok, top, MASKED))
            sums.append(stats[:, 3 * head + 1 : 3 * head + 2] + stats[:, 3 * head + 2 : 3 * head + 3])
        top = functools.reduce(jnp.maximum, tops)
        weights = [jnp.exp2((t - top) * EXP2_SCALE) for t in tops]
        total = sum(w * s for w, s in zip(weights, sums))
        value = sum(w * p[0][:, cols] for w, p in zip(weights, parts))
        heads.append((value / total).astype(jnp.bfloat16))
    return jnp.concatenate(heads, axis=1)


def project_kernel(steps, time_count, has_total, *refs):
    count = len(steps) + 1
    mine, other = refs[:count], refs[count : 2 * count]
    w_ref = refs[2 * count]
    total_ref = refs[2 * count + 1] if has_total else None
    out_ref, held = refs[-2:]
    position = lax.axis_index("tm")
    group = position % 2
    time_tile = position // (2 * TCOLS)
    width = held.shape[2]
    half = held.shape[1]

    @pl.when(pl.program_id(0) == 0)
    def _():
        oks = [None]
        for step in steps:
            source = time_tile + step
            oks.append(None if time_count == 2 else (source >= 0) & (source < time_count))
        held[0] = merge(mine, oks, half, width, group)
        held[1] = merge(other, oks, half, width, group)

    result = jnp.dot(held[0], w_ref[group], preferred_element_type=jnp.float32)
    result += jnp.dot(held[1], w_ref[1 - group], preferred_element_type=jnp.float32)
    if has_total:
        result += total_ref[...]
    out_ref[...] = result.astype(out_ref.dtype)


def project(mine, other, weight, chunk, total, steps, time_count, dtype):
    tall, width = mine[0].shape
    half = tall - STAT_ROWS
    model = weight.shape[2]
    block = 512 if model % 512 == 0 else model
    whole = pl.BlockSpec((tall, width), lambda n: (0, 0))
    tile = pl.BlockSpec((half, block), lambda n: (0, n))
    in_specs = [whole] * (2 * len(mine)) + [pl.BlockSpec((2, width, block), lambda n: (0, chunk, n))]
    args = [*mine, *other, weight]
    if total is not None:
        in_specs.append(tile)
        args.append(total)
    return pl.pallas_call(
        functools.partial(project_kernel, steps, time_count, total is not None),
        grid=(model // block,),
        in_specs=in_specs,
        out_specs=tile,
        out_shape=jax.ShapeDtypeStruct((half, model), dtype),
        scratch_shapes=[pltpu.VMEM((2, half, width), jnp.bfloat16)],
        compiler_params=pltpu.CompilerParams(vmem_limit_bytes=VMEM_BYTES),
        cost_estimate=pl.CostEstimate(
            flops=4 * half * width * model,
            bytes_accessed=4 * width * model + 4 * half * model,
            transcendentals=0,
        ),
        name="project",
    )(*args)


def per_device(query_states, key_states, value_states, out_weight):
    query, key, value = query_states[0], key_states[0], value_states[0]
    half_width = query.shape[1]
    devices = lax.axis_size("tm")
    time_count = devices // (2 * TCOLS)
    places = range(devices)
    row = 2 * TCOLS
    width = CHUNK_HEADS * HD
    chunks = half_width // width

    next_route = [(p, p ^ 2) for p in places]
    far_route = [(p, p ^ 4) for p in places if (p // 2) % TCOLS in (0, 3)]
    if time_count == 2:
        steps = (1,)
        ask_routes = [[(p, p ^ row) for p in places]]
    else:
        steps = (1, -1)
        ask_routes = [[(p, p + s * row) for p in places if 0 <= p + s * row < devices] for s in steps]
    same_routes = [[(b, a) for a, b in route] for route in ask_routes]
    cross_routes = [[(b, a ^ 1) for a, b in route] for route in ask_routes]
    core_route = [(p, p ^ 1) for p in places]

    weight = out_weight.reshape(2, half_width, out_weight.shape[1])
    cuts = [slice(c * width, (c + 1) * width) for c in range(chunks)]
    total = None
    for c in range(chunks):
        q_part = query[:, cuts[c]]
        asked = [lax.ppermute(q_part, "tm", route) for route in ask_routes]
        own = jnp.stack((key[:, cuts[c]], value[:, cuts[c]]))
        nxt = lax.ppermute(own, "tm", next_route)
        far = lax.ppermute(nxt, "tm", far_route)
        mine, other = [], []
        for q, same_route, cross_route in zip(asked, same_routes, cross_routes):
            same, cross = attend(q, own, nxt, far)
            mine.append(lax.ppermute(same, "tm", same_route))
            other.append(lax.ppermute(cross, "tm", cross_route))
        same, cross = attend(q_part, own, nxt, far)
        mine.insert(0, same)
        other.insert(0, lax.ppermute(cross, "tm", core_route))
        last = c == chunks - 1
        total = project(
            mine, other, weight, c, total, steps, time_count, jnp.bfloat16 if last else jnp.float32
        )
    return total


def solution(mesh):
    in_specs = (
        P(("parts", "tm"), None, None),
        P(("parts", "tm"), None, None),
        P(("parts", "tm"), None, None),
        P(),
    )
    out_specs = P(("parts", "tm"), None)
    return jax.shard_map(
        per_device, mesh=mesh, in_specs=in_specs, out_specs=out_specs, check_vma=False
    )
```

time: 299 us -> 90.5 us (0.30)
  the two profiles are of different devices: /device:TPU:1 before, /device:TPU:7 now
where the time goes in v1:
time: 90.5 us; the launch traced here: 89 us
  waiting for transfers between devices  31.5 us (35%)
  Pallas kernels  28.5 us (31%)
  starting transfers between devices  27.1 us (30%)
  local copies, waits for them, and re-layouts  1.53 us (2%)
    ppermute x3, waiting for transfers between devices, per_device(): nxt = lax.ppermute(own, 'tm', next_route)  19.9 us
    pallas_call x3, Pallas kernels, project(): pl.pallas_call(functools.partial(project_kernel, steps, time_count, total...  17 us
    pallas_call x6, Pallas kernels, attend(): pl.pallas_call(attend_kernel, out_shape=(out, out), compiler_params=pltpu...  11.6 us
    ppermute x3, starting transfers between devices, per_device(): other.append(lax.ppermute(cross, 'tm', cross_route))  9.59 us
    ppermute x3, waiting for transfers between devices, per_device(): other.append(lax.ppermute(cross, 'tm', cross_route))  7.04 us
    ppermute x3, starting transfers between devices, per_device(): asked = [lax.ppermute(q_part, 'tm', route) for route in ask_routes]  4.83 us
    ppermute x3, starting transfers between devices, per_device(): other.insert(0, lax.ppermute(cross, 'tm', core_route))  4.5 us
    ppermute x3, starting transfers between devices, per_device(): far = lax.ppermute(nxt, 'tm', far_route)  3.84 us
  transfers between devices with their start and end apart: 18, of which 7 were waited for; matrix products, arithmetic and copies ran while one was open for 0% of the time, Pallas kernels for 25%

profile of v1, /device:TPU:7, one launch (start us, length us, event | category | flops | bytes accessed | tf_op | source)
XLA Modules:
  0.0 89.0 jit_solution(3079238316198009477)
XLA Ops:
  0.0 0.0 copy-start
  0.0 1.5 %slice_bitcast_fusion = (bf16[1,384,256]{2,1,0:T(8,128)(2,1)S(1)}, bf16[1,384,256]{2,1,0:T(8,128)(2,1)S(1)}, bf16[1,384,256]{2,1,0:T(8,128)(2,1)S(1)}, bf16[1,38...) fusion(bf16[384,768]{1,0:T(8,128)(2,1)} %bitcast.20, ...), kind=kLoop, calls=%fused_computation.3 | loop fusion | bytes 2359296 | tf_op jit(solution)/shard_map/stack | solution.py:202
  1.5 0.3 collective-permute-start.6
  1.9 1.3 %collective-permute-start.12 = (bf16[2,384,256]{2,1,0:T(8,128)(2,1)S(1)}, bf16[2,384,256]{2,1,0:T(8,128)(2,1)S(1)}, u32[]{:S(2)}, u32[]{:S(2)}) collective-permute-start(bf16[2,384,256]{2,1,0:T(8,128)(2,1)S(1)} %pad_maximum_fusion.2.own_ref), channel_id=1, source_target_pairs={{0,2},{1,3},{2,0},{3,1},{4,6},{5,7},{6,4},{7,5},{8,10},{9,11},{10,... | collective-permute-start | bytes 1179656 | tf_op jit(solution)/shard_map/ppermute | solution.py:203
  3.2 0.3 collective-permute-start
  3.5 8.1 %collective-permute-done.6.next_ref = bf16[2,384,256]{2,1,0:T(8,128)(2,1)S(1)} collective-permute-done((bf16[2,384,256]{2,1,0:T(8,128)(2,1)S(1)}, bf16[2,384,256]{2,1,0:T(8,128)(2,1)S(1)}, u32[]{:S(2)}, u32[]{:S(2)}) %collective-permute-start.6) | collective-permute-done | bytes 393248 | tf_op jit(solution)/shard_map/ppermute | solution.py:203
  11.6 1.3 %collective-permute-start.7 = (bf16[2,384,256]{2,1,0:T(8,128)(2,1)S(1)}, bf16[2,384,256]{2,1,0:T(8,128)(2,1)S(1)}, u32[]{:S(2)}, u32[]{:S(2)}) collective-permute-start(bf16[2,384,256]{2,1,0:T(8,128)(2,1)S(1)} %collective-permute-done.6.next_ref), channel_id=1, source_target_pairs={{0,4},{1,5},{6,2},{7,3},{8,12},{9,13},{14,10},{15,11},{16,20},{17,... | collective-permute-start | bytes 1179656 | tf_op jit(solution)/shard_map/ppermute | solution.py:204
  12.9 7.1 %collective-permute-done.12.next_ref = bf16[2,384,256]{2,1,0:T(8,128)(2,1)S(1)} collective-permute-done((bf16[2,384,256]{2,1,0:T(8,128)(2,1)S(1)}, bf16[2,384,256]{2,1,0:T(8,128)(2,1)S(1)}, u32[]{:S(2)}, u32[]{:S(2)}) %collective-permute-start.12) | collective-permute-done | bytes 393248 | tf_op jit(solution)/shard_map/ppermute | solution.py:203
  20.0 1.3 %collective-permute-start.13 = (bf16[2,384,256]{2,1,0:T(8,128)(2,1)S(1)}, bf16[2,384,256]{2,1,0:T(8,128)(2,1)S(1)}, u32[]{:S(2)}, u32[]{:S(2)}) collective-permute-start(bf16[2,384,256]{2,1,0:T(8,128)(2,1)S(1)} %collective-permute-done.12.next_ref), channel_id=1, source_target_pairs={{0,4},{1,5},{6,2},{7,3},{8,12},{9,13},{14,10},{15,11},{16,20},{17,... | collective-permute-start | bytes 1179656 | tf_op jit(solution)/shard_map/ppermute | solution.py:204
  21.3 0.0 copy-done
  21.4 2.4 %collective-permute-start.8 = (bf16[384,256]{1,0:T(8,128)(2,1)S(1)}, bf16[384,256]{1,0:T(8,128)(2,1)S(1)}, u32[]{:S(2)}, u32[]{:S(2)}) collective-permute-start(bf16[384,256]{1,0:T(8,128)(2,1)S(1)} %get-tuple-element.36.q_ref), channel_id=1, source_target_pairs={{0,8},{1,9},{2,10},{3,11},{4,12},{5,13},{6,14},{7,15},{8,0},{9,1},... | collective-permute-start | bytes 589832 | tf_op jit(solution)/shard_map/ppermute | solution.py:201
  23.7 4.7 %collective-permute-done.next_ref = bf16[2,384,256]{2,1,0:T(8,128)(2,1)S(1)} collective-permute-done((bf16[2,384,256]{2,1,0:T(8,128)(2,1)S(1)}, bf16[2,384,256]{2,1,0:T(8,128)(2,1)S(1)}, u32[]{:S(2)}, u32[]{:S(2)}) %collective-permute-start) | collective-permute-done | bytes 393248 | tf_op jit(solution)/shard_map/ppermute | solution.py:203
  28.4 1.3 %collective-permute-start.1 = (bf16[2,384,256]{2,1,0:T(8,128)(2,1)S(1)}, bf16[2,384,256]{2,1,0:T(8,128)(2,1)S(1)}, u32[]{:S(2)}, u32[]{:S(2)}) collective-permute-start(bf16[2,384,256]{2,1,0:T(8,128)(2,1)S(1)} %collective-permute-done.next_ref), channel_id=1, source_target_pairs={{0,4},{1,5},{6,2},{7,3},{8,12},{9,13},{14,10},{15,11},{16,20},{17,... | collective-permute-start | bytes 1179656 | tf_op jit(solution)/shard_map/ppermute | solution.py:204
  29.7 2.4 %collective-permute-start.14 = (bf16[384,256]{1,0:T(8,128)(2,1)S(1)}, bf16[384,256]{1,0:T(8,128)(2,1)S(1)}, u32[]{:S(2)}, u32[]{:S(2)}) collective-permute-start(bf16[384,256]{1,0:T(8,128)(2,1)S(1)} %get-tuple-element.35.q_ref), channel_id=1, source_target_pairs={{0,8},{1,9},{2,10},{3,11},{4,12},{5,13},{6,14},{7,15},{8,0},{9,1},... | collective-permute-start | bytes 589832 | tf_op jit(solution)/shard_map/ppermute | solution.py:201
  32.1 0.0 collective-permute-done.8.q_ref
  32.1 0.1 collective-permute-start.2
  32.2 0.0 collective-permute-done.7.far_ref
  32.2 1.9 %attend.9 = (bf16[208,256]{1,0:T(8,128)(2,1)S(1)}, bf16[208,256]{1,0:T(8,128)(2,1)S(1)}) custom-call(bf16[384,256]{1,0:T(8,128)(2,1)S(1)} %collective-permute-done.8.q_ref, bf16[2,384,256]{2,1,0:T(8,128)(2,1)S(1)} %pad_maximum_fusion.1.own_ref, bf16[2,384,256]{2,1,0:T(8,128)(2,1)S(1)} %collective-permute-done.6.next_ref, ...), custom_call_target="tpu_custom_call" | custom-call | flops 452984832 | bytes 1572864 | tf_op jit(solution)/shard_map/attend/pallas_call | solution.py:81
  34.1 2.3 %collective-permute-start.9 = (bf16[208,256]{1,0:T(8,128)(2,1)S(1)}, bf16[208,256]{1,0:T(8,128)(2,1)S(1)}, u32[]{:S(2)}, u32[]{:S(2)}) collective-permute-start(bf16[208,256]{1,0:T(8,128)(2,1)S(1)} %get-tuple-element.22), channel_id=1, source_target_pairs={{8,0},{9,1},{10,2},{11,3},{12,4},{13,5},{14,6},{15,7},{0,8},{1,9},... | collective-permute-start | bytes 319496 | tf_op jit(solution)/shard_map/ppermute | solution.py:208
  36.4 1.5 %collective-permute-done.14.q_ref = bf16[384,256]{1,0:T(8,128)(2,1)S(1)} collective-permute-done((bf16[384,256]{1,0:T(8,128)(2,1)S(1)}, bf16[384,256]{1,0:T(8,128)(2,1)S(1)}, u32[]{:S(2)}, u32[]{:S(2)}) %collective-permute-start.14) | collective-permute-done | bytes 196640 | tf_op jit(solution)/shard_map/ppermute | solution.py:201
  37.9 3.1 %collective-permute-done.13.far_ref = bf16[2,384,256]{2,1,0:T(8,128)(2,1)S(1)} collective-permute-done((bf16[2,384,256]{2,1,0:T(8,128)(2,1)S(1)}, bf16[2,384,256]{2,1,0:T(8,128)(2,1)S(1)}, u32[]{:S(2)}, u32[]{:S(2)}) %collective-permute-start.13) | collective-permute-done | bytes 393248 | tf_op jit(solution)/shard_map/ppermute | solution.py:204
  41.0 1.9 %attend.11 = (bf16[208,256]{1,0:T(8,128)(2,1)S(1)}, bf16[208,256]{1,0:T(8,128)(2,1)S(1)}) custom-call(bf16[384,256]{1,0:T(8,128)(2,1)S(1)} %collective-permute-done.14.q_ref, bf16[2,384,256]{2,1,0:T(8,128)(2,1)S(1)} %pad_maximum_fusion.2.own_ref, bf16[2,384,256]{2,1,0:T(8,128)(2,1)S(1)} %collective-permute-done.12.next_ref, ...), custom_call_target="tpu_custom_call" | custom-call | flops 452984832 | bytes 1572864 | tf_op jit(solution)/shard_map/attend/pallas_call | solution.py:81
  42.9 0.1 collective-permute-start.15
  43.0 9.3 %collective-permute-start.17 = (bf16[208,256]{1,0:T(8,128)(2,1)S(1)}, bf16[208,256]{1,0:T(8,128)(2,1)S(1)}, u32[]{:S(2)}, u32[]{:S(2)}) collective-permute-start(bf16[208,256]{1,0:T(8,128)(2,1)S(1)} %get-tuple-element.28), channel_id=1, source_target_pairs={{8,1},{9,0},{10,3},{11,2},{12,5},{13,4},{14,7},{15,6},{0,9},{1,8},... | collective-permute-start | bytes 319496 | tf_op jit(solution)/shard_map/ppermute | solution.py:209
  52.3 1.9 %attend.10 = (bf16[208,256]{1,0:T(8,128)(2,1)S(1)}, bf16[208,256]{1,0:T(8,128)(2,1)S(1)}) custom-call(bf16[384,256]{1,0:T(8,128)(2,1)S(1)} %get-tuple-element.35.q_ref, bf16[2,384,256]{2,1,0:T(8,128)(2,1)S(1)} %pad_maximum_fusion.2.own_ref, bf16[2,384,256]{2,1,0:T(8,128)(2,1)S(1)} %collective-permute-done.12.next_ref, ...), custom_call_target="tpu_custom_call" | custom-call | flops 452984832 | bytes 1572864 | tf_op jit(solution)/shard_map/attend/pallas_call | solution.py:81
  54.2 0.0 collective-permute-done.2.q_ref
  54.2 0.1 collective-permute-start.16
  54.3 1.9 %attend.8 = (bf16[208,256]{1,0:T(8,128)(2,1)S(1)}, bf16[208,256]{1,0:T(8,128)(2,1)S(1)}) custom-call(bf16[384,256]{1,0:T(8,128)(2,1)S(1)} %get-tuple-element.36.q_ref, bf16[2,384,256]{2,1,0:T(8,128)(2,1)S(1)} %pad_maximum_fusion.1.own_ref, bf16[2,384,256]{2,1,0:T(8,128)(2,1)S(1)} %collective-permute-done.6.next_ref, ...), custom_call_target="tpu_custom_call" | custom-call | flops 452984832 | bytes 1572864 | tf_op jit(solution)/shard_map/attend/pallas_call | solution.py:81
  56.2 0.0 collective-permute-done.1.far_ref
  56.2 0.2 collective-permute-start.11
  56.5 0.0 collective-permute-done.9.refs_1_
  56.5 4.4 %collective-permute-start.10 = (bf16[208,256]{1,0:T(8,128)(2,1)S(1)}, bf16[208,256]{1,0:T(8,128)(2,1)S(1)}, u32[]{:S(2)}, u32[]{:S(2)}) collective-permute-start(bf16[208,256]{1,0:T(8,128)(2,1)S(1)} %get-tuple-element.23), channel_id=1, source_target_pairs={{0,1},{1,0},{2,3},{3,2},{4,5},{5,4},{6,7},{7,6},{8,9},{9,8},{10,11... | collective-permute-start | bytes 319496 | tf_op jit(solution)/shard_map/ppermute | solution.py:212
  60.9 1.9 %attend.6 = (bf16[208,256]{1,0:T(8,128)(2,1)S(1)}, bf16[208,256]{1,0:T(8,128)(2,1)S(1)}) custom-call(bf16[384,256]{1,0:T(8,128)(2,1)S(1)} %get-tuple-element.37.q_ref, bf16[2,384,256]{2,1,0:T(8,128)(2,1)S(1)} %pad_maximum_fusion.own_ref, bf16[2,384,256]{2,1,0:T(8,128)(2,1)S(1)} %collective-permute-done.next_ref, ...), custom_call_target="tpu_custom_call" | custom-call | flops 452984832 | bytes 1572864 | tf_op jit(solution)/shard_map/attend/pallas_call | solution.py:81
  62.8 2.1 %attend.7 = (bf16[208,256]{1,0:T(8,128)(2,1)S(1)}, bf16[208,256]{1,0:T(8,128)(2,1)S(1)}) custom-call(bf16[384,256]{1,0:T(8,128)(2,1)S(1)} %collective-permute-done.2.q_ref, bf16[2,384,256]{2,1,0:T(8,128)(2,1)S(1)} %pad_maximum_fusion.own_ref, bf16[2,384,256]{2,1,0:T(8,128)(2,1)S(1)} %collective-permute-done.next_ref, ...), custom_call_target="tpu_custom_call" | custom-call | flops 452984832 | bytes 1572864 | tf_op jit(solution)/shard_map/attend/pallas_call | solution.py:81
  64.9 0.0 collective-permute-done.15.refs_1_
  64.9 0.1 collective-permute-start.3
  65.0 5.8 %collective-permute-done.17.refs_3_ = bf16[208,256]{1,0:T(8,128)(2,1)S(1)} collective-permute-done((bf16[208,256]{1,0:T(8,128)(2,1)S(1)}, bf16[208,256]{1,0:T(8,128)(2,1)S(1)}, u32[]{:S(2)}, u32[]{:S(2)}) %collective-permute-start.17) | collective-permute-done | bytes 106528 | tf_op jit(solution)/shard_map/ppermute | solution.py:209
  70.8 0.0 collective-permute-start.5
  70.8 0.0 collective-permute-done.16.refs_2_
  70.8 0.0 collective-permute-start.4
  70.8 5.3 %project.3.refs_5_ = f32[192,3072]{1,0:T(8,128)S(1)} custom-call(bf16[208,256]{1,0:T(8,128)(2,1)S(1)} %get-tuple-element.25.refs_0_, bf16[208,256]{1,0:T(8,128)(2,1)S(1)} %collective-permute-done.15.refs_1_, bf16[208,256]{1,0:T(8,128)(2,1)S(1)} %collective-permute-done.16.refs_2_, bf16[208,256]{1,0:T(8,128)(2,1)S(1)} %collective-permute-done.17.refs_3_, ...), custom_call_target="tpu_custom_call" | custom-call | flops 603979776 | bytes 5505024 | tf_op jit(solution)/shard_map/project/pallas_call | solution.py:157
  76.1 1.2 %collective-permute-done.11.refs_3_ = bf16[208,256]{1,0:T(8,128)(2,1)S(1)} collective-permute-done((bf16[208,256]{1,0:T(8,128)(2,1)S(1)}, bf16[208,256]{1,0:T(8,128)(2,1)S(1)}, u32[]{:S(2)}, u32[]{:S(2)}) %collective-permute-start.11) | collective-permute-done | bytes 106528 | tf_op jit(solution)/shard_map/ppermute | solution.py:209
  77.3 0.0 collective-permute-done.10.refs_2_
  77.3 5.3 %project.4.refs_5_ = f32[192,3072]{1,0:T(8,128)S(1)} custom-call(bf16[208,256]{1,0:T(8,128)(2,1)S(1)} %get-tuple-element.21.refs_0_, bf16[208,256]{1,0:T(8,128)(2,1)S(1)} %collective-permute-done.9.refs_1_, bf16[208,256]{1,0:T(8,128)(2,1)S(1)} %collective-permute-done.10.refs_2_, bf16[208,256]{1,0:T(8,128)(2,1)S(1)} %collective-permute-done.11.refs_3_, ...), custom_call_target="tpu_custom_call" | custom-call | flops 603979776 | bytes 5505024 | tf_op jit(solution)/shard_map/project/pallas_call | solution.py:157
  82.7 0.0 collective-permute-done.3.refs_1_
  82.7 0.0 collective-permute-done.5.refs_3_
  82.7 0.0 collective-permute-done.4.refs_2_
  82.7 6.3 %project.5 = bf16[192,3072]{1,0:T(8,128)(2,1)} custom-call(bf16[208,256]{1,0:T(8,128)(2,1)S(1)} %get-tuple-element.17.refs_0_, bf16[208,256]{1,0:T(8,128)(2,1)S(1)} %collective-permute-done.3.refs_1_, bf16[208,256]{1,0:T(8,128)(2,1)S(1)} %collective-permute-done.4.refs_2_, bf16[208,256]{1,0:T(8,128)(2,1)S(1)} %collective-permute-done.5.refs_3_, ...), custom_call_target="tpu_custom_call" | custom-call | flops 603979776 | bytes 5505024 | tf_op jit(solution)/shard_map/project/pallas_call | solution.py:157
  (4 shorter events, 0.2 us)
Async XLA Ops:
  0.0 21.3 %copy-start = (bf16[1,384,768]{2,1,0:T(8,128)(2,1)S(1)}, bf16[1,384,768]{2,1,0:T(8,128)(2,1)}, u32[]{:S(2)}) copy-start(bf16[1,384,768]{2,1,0:T(8,128)(2,1)} %param.4) | copy-start | bytes 1769476
  1.5 10.0 %collective-permute-start.6 = (bf16[2,384,256]{2,1,0:T(8,128)(2,1)S(1)}, bf16[2,384,256]{2,1,0:T(8,128)(2,1)S(1)}, u32[]{:S(2)}, u32[]{:S(2)}) collective-permute-start(bf16[2,384,256]{2,1,0:T(8,128)(2,1)S(1)} %pad_maximum_fusion.1.own_ref), channel_id=1, source_target_pairs={{0,2},{1,3},{2,0},{3,1},{4,6},{5,7},{6,4},{7,5},{8,10},{9,11},{10,... | collective-permute-start | bytes 1179656 | tf_op jit(solution)/shard_map/ppermute | solution.py:203
  1.9 18.1 %collective-permute-start.12 = (bf16[2,384,256]{2,1,0:T(8,128)(2,1)S(1)}, bf16[2,384,256]{2,1,0:T(8,128)(2,1)S(1)}, u32[]{:S(2)}, u32[]{:S(2)}) collective-permute-start(bf16[2,384,256]{2,1,0:T(8,128)(2,1)S(1)} %pad_maximum_fusion.2.own_ref), channel_id=1, source_target_pairs={{0,2},{1,3},{2,0},{3,1},{4,6},{5,7},{6,4},{7,5},{8,10},{9,11},{10,... | collective-permute-start | bytes 1179656 | tf_op jit(solution)/shard_map/ppermute | solution.py:203
  3.2 25.2 %collective-permute-start = (bf16[2,384,256]{2,1,0:T(8,128)(2,1)S(1)}, bf16[2,384,256]{2,1,0:T(8,128)(2,1)S(1)}, u32[]{:S(2)}, u32[]{:S(2)}) collective-permute-start(bf16[2,384,256]{2,1,0:T(8,128)(2,1)S(1)} %pad_maximum_fusion.own_ref), channel_id=1, source_target_pairs={{0,2},{1,3},{2,0},{3,1},{4,6},{5,7},{6,4},{7,5},{8,10},{9,11},{10,... | collective-permute-start | bytes 1179656 | tf_op jit(solution)/shard_map/ppermute | solution.py:203
  11.6 20.6 %collective-permute-start.7 = (bf16[2,384,256]{2,1,0:T(8,128)(2,1)S(1)}, bf16[2,384,256]{2,1,0:T(8,128)(2,1)S(1)}, u32[]{:S(2)}, u32[]{:S(2)}) collective-permute-start(bf16[2,384,256]{2,1,0:T(8,128)(2,1)S(1)} %collective-permute-done.6.next_ref), channel_id=1, source_target_pairs={{0,4},{1,5},{6,2},{7,3},{8,12},{9,13},{14,10},{15,11},{16,20},{17,... | collective-permute-start | bytes 1179656 | tf_op jit(solution)/shard_map/ppermute | solution.py:204
  20.0 21.0 %collective-permute-start.13 = (bf16[2,384,256]{2,1,0:T(8,128)(2,1)S(1)}, bf16[2,384,256]{2,1,0:T(8,128)(2,1)S(1)}, u32[]{:S(2)}, u32[]{:S(2)}) collective-permute-start(bf16[2,384,256]{2,1,0:T(8,128)(2,1)S(1)} %collective-permute-done.12.next_ref), channel_id=1, source_target_pairs={{0,4},{1,5},{6,2},{7,3},{8,12},{9,13},{14,10},{15,11},{16,20},{17,... | collective-permute-start | bytes 1179656 | tf_op jit(solution)/shard_map/ppermute | solution.py:204
  21.4 10.7 %collective-permute-start.8 = (bf16[384,256]{1,0:T(8,128)(2,1)S(1)}, bf16[384,256]{1,0:T(8,128)(2,1)S(1)}, u32[]{:S(2)}, u32[]{:S(2)}) collective-permute-start(bf16[384,256]{1,0:T(8,128)(2,1)S(1)} %get-tuple-element.36.q_ref), channel_id=1, source_target_pairs={{0,8},{1,9},{2,10},{3,11},{4,12},{5,13},{6,14},{7,15},{8,0},{9,1},... | collective-permute-start | bytes 589832 | tf_op jit(solution)/shard_map/ppermute | solution.py:201
  28.4 27.8 %collective-permute-start.1 = (bf16[2,384,256]{2,1,0:T(8,128)(2,1)S(1)}, bf16[2,384,256]{2,1,0:T(8,128)(2,1)S(1)}, u32[]{:S(2)}, u32[]{:S(2)}) collective-permute-start(bf16[2,384,256]{2,1,0:T(8,128)(2,1)S(1)} %collective-permute-done.next_ref), channel_id=1, source_target_pairs={{0,4},{1,5},{6,2},{7,3},{8,12},{9,13},{14,10},{15,11},{16,20},{17,... | collective-permute-start | bytes 1179656 | tf_op jit(solution)/shard_map/ppermute | solution.py:204
  29.7 8.2 %collective-permute-start.14 = (bf16[384,256]{1,0:T(8,128)(2,1)S(1)}, bf16[384,256]{1,0:T(8,128)(2,1)S(1)}, u32[]{:S(2)}, u32[]{:S(2)}) collective-permute-start(bf16[384,256]{1,0:T(8,128)(2,1)S(1)} %get-tuple-element.35.q_ref), channel_id=1, source_target_pairs={{0,8},{1,9},{2,10},{3,11},{4,12},{5,13},{6,14},{7,15},{8,0},{9,1},... | collective-permute-start | bytes 589832 | tf_op jit(solution)/shard_map/ppermute | solution.py:201
  32.1 22.1 %collective-permute-start.2 = (bf16[384,256]{1,0:T(8,128)(2,1)S(1)}, bf16[384,256]{1,0:T(8,128)(2,1)S(1)}, u32[]{:S(2)}, u32[]{:S(2)}) collective-permute-start(bf16[384,256]{1,0:T(8,128)(2,1)S(1)} %get-tuple-element.37.q_ref), channel_id=1, source_target_pairs={{0,8},{1,9},{2,10},{3,11},{4,12},{5,13},{6,14},{7,15},{8,0},{9,1},... | collective-permute-start | bytes 589832 | tf_op jit(solution)/shard_map/ppermute | solution.py:201
  34.1 22.4 %collective-permute-start.9 = (bf16[208,256]{1,0:T(8,128)(2,1)S(1)}, bf16[208,256]{1,0:T(8,128)(2,1)S(1)}, u32[]{:S(2)}, u32[]{:S(2)}) collective-permute-start(bf16[208,256]{1,0:T(8,128)(2,1)S(1)} %get-tuple-element.22), channel_id=1, source_target_pairs={{8,0},{9,1},{10,2},{11,3},{12,4},{13,5},{14,6},{15,7},{0,8},{1,9},... | collective-permute-start | bytes 319496 | tf_op jit(solution)/shard_map/ppermute | solution.py:208
  42.9 22.0 %collective-permute-start.15 = (bf16[208,256]{1,0:T(8,128)(2,1)S(1)}, bf16[208,256]{1,0:T(8,128)(2,1)S(1)}, u32[]{:S(2)}, u32[]{:S(2)}) collective-permute-start(bf16[208,256]{1,0:T(8,128)(2,1)S(1)} %get-tuple-element.26), channel_id=1, source_target_pairs={{8,0},{9,1},{10,2},{11,3},{12,4},{13,5},{14,6},{15,7},{0,8},{1,9},... | collective-permute-start | bytes 319496 | tf_op jit(solution)/shard_map/ppermute | solution.py:208
  43.0 27.8 %collective-permute-start.17 = (bf16[208,256]{1,0:T(8,128)(2,1)S(1)}, bf16[208,256]{1,0:T(8,128)(2,1)S(1)}, u32[]{:S(2)}, u32[]{:S(2)}) collective-permute-start(bf16[208,256]{1,0:T(8,128)(2,1)S(1)} %get-tuple-element.28), channel_id=1, source_target_pairs={{8,1},{9,0},{10,3},{11,2},{12,5},{13,4},{14,7},{15,6},{0,9},{1,8},... | collective-permute-start | bytes 319496 | tf_op jit(solution)/shard_map/ppermute | solution.py:209
  54.2 16.6 %collective-permute-start.16 = (bf16[208,256]{1,0:T(8,128)(2,1)S(1)}, bf16[208,256]{1,0:T(8,128)(2,1)S(1)}, u32[]{:S(2)}, u32[]{:S(2)}) collective-permute-start(bf16[208,256]{1,0:T(8,128)(2,1)S(1)} %get-tuple-element.27), channel_id=1, source_target_pairs={{0,1},{1,0},{2,3},{3,2},{4,5},{5,4},{6,7},{7,6},{8,9},{9,8},{10,11... | collective-permute-start | bytes 319496 | tf_op jit(solution)/shard_map/ppermute | solution.py:212
  56.2 21.1 %collective-permute-start.11 = (bf16[208,256]{1,0:T(8,128)(2,1)S(1)}, bf16[208,256]{1,0:T(8,128)(2,1)S(1)}, u32[]{:S(2)}, u32[]{:S(2)}) collective-permute-start(bf16[208,256]{1,0:T(8,128)(2,1)S(1)} %get-tuple-element.24), channel_id=1, source_target_pairs={{8,1},{9,0},{10,3},{11,2},{12,5},{13,4},{14,7},{15,6},{0,9},{1,8},... | collective-permute-start | bytes 319496 | tf_op jit(solution)/shard_map/ppermute | solution.py:209
  56.5 20.9 %collective-permute-start.10 = (bf16[208,256]{1,0:T(8,128)(2,1)S(1)}, bf16[208,256]{1,0:T(8,128)(2,1)S(1)}, u32[]{:S(2)}, u32[]{:S(2)}) collective-permute-start(bf16[208,256]{1,0:T(8,128)(2,1)S(1)} %get-tuple-element.23), channel_id=1, source_target_pairs={{0,1},{1,0},{2,3},{3,2},{4,5},{5,4},{6,7},{7,6},{8,9},{9,8},{10,11... | collective-permute-start | bytes 319496 | tf_op jit(solution)/shard_map/ppermute | solution.py:212
  64.9 17.8 %collective-permute-start.3 = (bf16[208,256]{1,0:T(8,128)(2,1)S(1)}, bf16[208,256]{1,0:T(8,128)(2,1)S(1)}, u32[]{:S(2)}, u32[]{:S(2)}) collective-permute-start(bf16[208,256]{1,0:T(8,128)(2,1)S(1)} %get-tuple-element.18), channel_id=1, source_target_pairs={{8,0},{9,1},{10,2},{11,3},{12,4},{13,5},{14,6},{15,7},{0,8},{1,9},... | collective-permute-start | bytes 319496 | tf_op jit(solution)/shard_map/ppermute | solution.py:208
  70.8 11.9 %collective-permute-start.5 = (bf16[208,256]{1,0:T(8,128)(2,1)S(1)}, bf16[208,256]{1,0:T(8,128)(2,1)S(1)}, u32[]{:S(2)}, u32[]{:S(2)}) collective-permute-start(bf16[208,256]{1,0:T(8,128)(2,1)S(1)} %get-tuple-element.20), channel_id=1, source_target_pairs={{8,1},{9,0},{10,3},{11,2},{12,5},{13,4},{14,7},{15,6},{0,9},{1,8},... | collective-permute-start | bytes 319496 | tf_op jit(solution)/shard_map/ppermute | solution.py:209
  70.8 11.9 %collective-permute-start.4 = (bf16[208,256]{1,0:T(8,128)(2,1)S(1)}, bf16[208,256]{1,0:T(8,128)(2,1)S(1)}, u32[]{:S(2)}, u32[]{:S(2)}) collective-permute-start(bf16[208,256]{1,0:T(8,128)(2,1)S(1)} %get-tuple-element.19), channel_id=1, source_target_pairs={{0,1},{1,0},{2,3},{3,2},{4,5},{5,4},{6,7},{7,6},{8,9},{9,8},{10,11... | collective-permute-start | bytes 319496 | tf_op jit(solution)/shard_map/ppermute | solution.py:212

commit v2 on v1

v2 whole, which is shorter than its diff:
```python
import functools
import math

import jax
import jax.numpy as jnp
from jax import lax
from jax.experimental import pallas as pl
from jax.experimental.pallas import tpu as pltpu
from jax.sharding import PartitionSpec as P

TCOLS = 4
HD = 128
CHUNK_HEADS = 2
STAT_ROWS = 16
EXP2_SCALE = HD ** (-0.5) * math.log2(math.e)
MASKED = -1e30
VMEM_BYTES = 32 * 1024 * 1024


def after(array, *earlier):
    return lax.optimization_barrier((array, *earlier))[0]


def dot_rows(a, b):
    return lax.dot_general(a, b, (((1,), (1,)), ((), ())), preferred_element_type=jnp.float32)


def stat_blocks(rows, width):
    return -(-rows // width)


def attend_kernel(q_ref, own_ref, next_ref, far_ref, out_ref):
    col = (lax.axis_index("tm") // 2) % TCOLS
    far_ok = (col == 1) | (col == 2)
    rows, width = q_ref.shape
    stats = []
    for head in range(width // HD):
        cols = slice(head * HD, (head + 1) * HD)
        query = q_ref[:, cols]
        s_own = dot_rows(own_ref[0, :, cols], query)
        s_next = dot_rows(next_ref[0, :, cols], query)
        s_far = dot_rows(far_ref[0, :, cols], query)
        s_far = jnp.where(far_ok, s_far, MASKED)
        top = jnp.maximum(jnp.maximum(s_own, s_next), s_far)
        top = jnp.max(top, axis=0, keepdims=True).astype(jnp.bfloat16).astype(jnp.float32)
        total = jnp.zeros((1, rows), jnp.float32)
        out = jnp.zeros((HD, rows), jnp.float32)
        for scores, ref in ((s_own, own_ref), (s_next, next_ref), (s_far, far_ref)):
            probs = jnp.exp2((scores - top) * EXP2_SCALE).astype(jnp.bfloat16)
            total += jnp.sum(probs.astype(jnp.float32), axis=0, keepdims=True)
            out += lax.dot_general(
                ref[1, :, cols],
                probs,
                (((0,), (0,)), ((), ())),
                preferred_element_type=jnp.float32,
            )
        high = total.astype(jnp.bfloat16).astype(jnp.float32)
        stats += [top, high, total - high]
        out_ref[:rows, cols] = out.T.astype(out_ref.dtype)
    stats.append(jnp.zeros((STAT_ROWS - len(stats), rows), jnp.float32))
    stats = jnp.concatenate(stats, axis=0)
    for block in range(stat_blocks(rows, width)):
        piece = stats[:, block * width : (block + 1) * width]
        if piece.shape[1] < width:
            piece = jnp.concatenate(
                (piece, jnp.zeros((STAT_ROWS, width - piece.shape[1]), jnp.float32)), axis=1
            )
        first = rows + block * STAT_ROWS
        out_ref[first : first + STAT_ROWS, :] = piece.astype(out_ref.dtype)


def attend(query, own, nxt, far, dtype):
    rows, width = query.shape
    keys = 3 * own.shape[1]
    return pl.pallas_call(
        attend_kernel,
        out_shape=jax.ShapeDtypeStruct((rows + STAT_ROWS * stat_blocks(rows, width), width), dtype),
        compiler_params=pltpu.CompilerParams(vmem_limit_bytes=VMEM_BYTES),
        cost_estimate=pl.CostEstimate(
            flops=4 * rows * keys * width,
            bytes_accessed=2 * width * (2 * rows + 2 * keys),
            transcendentals=rows * keys * width // HD,
        ),
        name="attend",
    )(query, own, nxt, far)


def join_kernel(steps, time_count, *refs):
    mine_ref, other_ref = refs[-2:]
    half, width = mine_ref.shape
    rows = 2 * half
    position = lax.axis_index("tm")
    group = position % 2
    time_tile = position // (2 * TCOLS)
    parts = []
    for ref, step in zip(refs, (0, *steps)):
        source = time_tile + step
        ok = None if step == 0 or time_count == 2 else (source >= 0) & (source < time_count)
        stats = [
            ref[rows + block * STAT_ROWS : rows + (block + 1) * STAT_ROWS, :].astype(jnp.float32)
            for block in range(stat_blocks(rows, width))
        ]
        stats = jnp.concatenate(stats, axis=1)[:, :rows].T
        parts.append((ref, stats, ok))
    for head in range(width // HD):
        cols = slice(head * HD, (head + 1) * HD)
        tops, sums = [], []
        for _, stats, ok in parts:
            top = stats[:, 3 * head : 3 * head + 1]
            tops.append(top if ok is None else jnp.where(ok, top, MASKED))
            sums.append(stats[:, 3 * head + 1 : 3 * head + 2] + stats[:, 3 * head + 2 : 3 * head + 3])
        top = functools.reduce(jnp.maximum, tops)
        weights = [jnp.exp2((t - top) * EXP2_SCALE) for t in tops]
        inverse = 1.0 / sum(w * s for w, s in zip(weights, sums))
        value = sum((w * inverse) * p[0][:rows, cols].astype(jnp.float32) for w, p in zip(weights, parts))
        value = value.astype(jnp.bfloat16)
        mine_ref[:, cols] = jnp.where(group == 0, value[:half], value[half:])
        other_ref[:, cols] = jnp.where(group == 0, value[half:], value[:half])


def join(parts, rows, steps, time_count):
    width = parts[0].shape[1]
    out = jax.ShapeDtypeStruct((rows // 2, width), jnp.bfloat16)
    return pl.pallas_call(
        functools.partial(join_kernel, steps, time_count),
        out_shape=(out, out),
        compiler_params=pltpu.CompilerParams(vmem_limit_bytes=VMEM_BYTES),
        cost_estimate=pl.CostEstimate(
            flops=8 * rows * width, bytes_accessed=10 * rows * width, transcendentals=0
        ),
        name="join",
    )(*parts)


def project_kernel(first, swaps, has_total, *refs):
    inputs, w_ref, out_ref = refs[: len(swaps)], refs[len(swaps)], refs[-1]
    group = lax.axis_index("tm") % 2
    width = inputs[0].shape[1]
    model = w_ref.shape[2]
    block = 512 if model % 512 == 0 else model
    for start in range(0, model, block):
        cols = slice(start, start + block)
        result = refs[len(swaps) + 1][:, cols] if has_total else 0.0
        for ref, swap in zip(inputs, swaps):
            which = 1 - group if swap else group
            result += jnp.dot(
                ref[...], w_ref[which, first : first + width, cols], preferred_element_type=jnp.float32
            )
        out_ref[:, cols] = result.astype(out_ref.dtype)


def project(inputs, swaps, weight, first, total, dtype):
    half, width = inputs[0].shape
    model = weight.shape[2]
    args = [*inputs, weight] if total is None else [*inputs, weight, total]
    return pl.pallas_call(
        functools.partial(project_kernel, first, swaps, total is not None),
        in_specs=[pl.BlockSpec(memory_space=pltpu.VMEM)] * len(args),
        out_specs=pl.BlockSpec(memory_space=pltpu.VMEM),
        out_shape=jax.ShapeDtypeStruct((half, model), dtype),
        compiler_params=pltpu.CompilerParams(vmem_limit_bytes=VMEM_BYTES),
        cost_estimate=pl.CostEstimate(
            flops=2 * len(inputs) * half * width * model,
            bytes_accessed=2 * len(inputs) * width * model + 4 * half * model,
            transcendentals=0,
        ),
        name="project",
    )(*args)


def per_device(query_states, key_states, value_states, out_weight):
    query, key, value = query_states[0], key_states[0], value_states[0]
    half_width = query.shape[1]
    devices = lax.axis_size("tm")
    time_count = devices // (2 * TCOLS)
    places = range(devices)
    row = 2 * TCOLS
    width = CHUNK_HEADS * HD
    chunks = half_width // width

    next_route = [(p, p ^ 2) for p in places]
    far_route = [(p, p ^ 4) for p in places if (p // 2) % TCOLS in (0, 3)]
    across_route = [(p, p ^ 6) for p in places if (p // 2) % TCOLS in (1, 2)]
    if time_count == 2:
        steps = (1,)
        ask_routes = [[(p, p ^ row) for p in places]]
    else:
        steps = (1, -1)
        ask_routes = [[(p, p + s * row) for p in places if 0 <= p + s * row < devices] for s in steps]
    back_routes = [[(b, a) for a, b in route] for route in ask_routes]
    core_route = [(p, p ^ 1) for p in places]

    weight = out_weight.reshape(2, half_width, out_weight.shape[1])
    cuts = [slice(c * width, (c + 1) * width) for c in range(chunks)]
    q_parts = [query[:, cut] for cut in cuts]
    kv_parts = [jnp.stack((key[:, cuts[0]], value[:, cuts[0]]))]
    key, value = after((key, value), kv_parts[0])
    kv_parts += [jnp.stack((key[:, cut], value[:, cut])) for cut in cuts[1:]]
    asked_all = [lax.ppermute(query, "tm", route) for route in ask_routes]
    asked = [[q[:, cut] for q in asked_all] for cut in cuts]
    nexts, fars = [], []
    for c in range(chunks):
        kv_part = after(kv_parts[c], nexts[0]) if c == chunks - 1 else kv_parts[c]
        nexts.append(lax.ppermute(kv_part, "tm", next_route))
        if c < chunks - 1:
            fars.append(lax.ppermute(after(nexts[c], *asked_all) if c else nexts[c], "tm", far_route))
        else:
            fars.append(lax.ppermute(kv_part, "tm", across_route))
    total = None
    owns, backs = [], []
    for c in range(chunks):
        keys = kv_parts[c], nexts[c], fars[c]
        remote = [attend(q, *keys, jnp.bfloat16) for q in asked[c]]
        backs.append([lax.ppermute(part, "tm", route) for part, route in zip(remote, back_routes)])
        owns.append(keys)
    owns = [attend(after(q_parts[c], *remote), *owns[c], jnp.float32) for c in range(chunks)]
    backs = [[after(back, *owns) for back in parts] for parts in backs]
    for c in range(chunks):
        mine, other = join((owns[c], *backs[c]), query.shape[0], steps, time_count)
        other = lax.ppermute(other, "tm", core_route)
        if c < chunks - 1:
            total = project((mine, other), (False, True), weight, cuts[c].start, total, jnp.float32)
        else:
            total = project((mine,), (False,), weight, cuts[c].start, total, jnp.float32)
            total = project((other,), (True,), weight, cuts[c].start, total, jnp.bfloat16)
    return total


def solution(mesh):
    in_specs = (
        P(("parts", "tm"), None, None),
        P(("parts", "tm"), None, None),
        P(("parts", "tm"), None, None),
        P(),
    )
    out_specs = P(("parts", "tm"), None)
    return jax.shard_map(
        per_device, mesh=mesh, in_specs=in_specs, out_specs=out_specs, check_vma=False
    )
```

time: 90.5 us -> 75.2 us (0.83); the launches traced: 89 us -> 74.7 us
  Pallas kernels: 28.5 us -> 17.6 us
  starting transfers between devices: 27.1 us -> 18.2 us
  waiting for transfers between devices: 31.5 us -> 36.3 us
    pallas_call x9 -> x13, Pallas kernels: 28.5 us -> 17.6 us  [the longest x6 12 us: attend(): pl.pallas_call(attend_kernel, out_shape=jax.ShapeDtypeStruct((rows + STAT...]
    ppermute x18 -> x13, starting transfers between devices: 27.1 us -> 18.2 us  [the longest x3 4.78 us: per_device(): other = lax.ppermute(other, 'tm', core_route)]
    ppermute x18 -> x13, waiting for transfers between devices: 31.5 us -> 36.3 us  [the longest x2 15 us: per_device(): lax.ppermute(after(nexts[c], *asked_all) if c else nexts[c], 'tm', far_ro...]
    another operation x1 -> x3, local copies, waits for them, and re-layouts: 1.48 us -> 2.19 us  [the longest x1 1.11 us: per_device(): kv_parts = [jnp.stack((key[:, cuts[0]], value[:, cuts[0]]))]]
  transfers between devices with their start and end apart: 18 -> 13, of which waited for: 7 -> 7; matrix products, arithmetic and copies ran while one was open for 0% -> 3% of each run, Pallas kernels for 25% -> 22%
where the time goes in v2:
time: 75.2 us; the launch traced here: 74.7 us
  waiting for transfers between devices  36.3 us (48%)
  starting transfers between devices  18.2 us (24%)
  Pallas kernels  17.6 us (23%)
  local copies, waits for them, and re-layouts  2.28 us (3%)
    ppermute x2, waiting for transfers between devices, per_device(): lax.ppermute(after(nexts[c], *asked_all) if c else nexts[c], 'tm', far_ro...  15 us
    pallas_call x6, Pallas kernels, attend(): pl.pallas_call(attend_kernel, out_shape=jax.ShapeDtypeStruct((rows + STAT...  12 us
    ppermute x3, waiting for transfers between devices, per_device(): nexts.append(lax.ppermute(kv_part, 'tm', next_route))  9.79 us
    ppermute x1, waiting for transfers between devices, per_device(): asked_all = [lax.ppermute(query, 'tm', route) for route in ask_routes]  6.28 us
    ppermute x3, waiting for transfers between devices, per_device(): lax.ppermute(part, 'tm', route)  5.2 us
    ppermute x3, starting transfers between devices, per_device(): other = lax.ppermute(other, 'tm', core_route)  4.78 us
    ppermute x1, starting transfers between devices, per_device(): fars.append(lax.ppermute(kv_part, 'tm', across_route))  4.15 us
    pallas_call x4, Pallas kernels, project(): pl.pallas_call(functools.partial(project_kernel, first, swaps, total is n...  3.63 us
  transfers between devices with their start and end apart: 13, of which 7 were waited for; matrix products, arithmetic and copies ran while one was open for 3% of the time, Pallas kernels for 22%

profile of v2, /device:TPU:7, one launch (start us, length us, event | category | flops | bytes accessed | tf_op | source)
XLA Modules:
  0.0 74.7 jit_solution(1280195075963320669)
XLA Ops:
  0.0 0.0 copy-start.1
  0.0 2.3 %collective-permute-start = (bf16[384,768]{1,0:T(8,128)(2,1)}, bf16[384,768]{1,0:T(8,128)(2,1)S(1)}, u32[]{:S(2)}, u32[]{:S(2)}) collective-permute-start(bf16[384,768]{1,0:T(8,128)(2,1)} %bitcast.24), channel_id=1, source_target_pairs={{0,8},{1,9},{2,10},{3,11},{4,12},{5,13},{6,14},{7,15},{8,0},{9,1},... | collective-permute-start | bytes 1769480 | tf_op jit(solution)/shard_map/ppermute | solution.py:199
  2.3 0.0 copy-start.2
  2.3 1.1 %slice_bitcast_fusion = (bf16[1,384,256]{2,1,0:T(8,128)(2,1)S(1)}, bf16[1,384,256]{2,1,0:T(8,128)(2,1)S(1)}) fusion(bf16[384,768]{1,0:T(8,128)(2,1)} %bitcast.20, bf16[384,768]{1,0:T(8,128)(2,1)} %bitcast.22), kind=kLoop, calls=%fused_computation.3 | loop fusion | bytes 786432 | tf_op jit(solution)/shard_map/stack | solution.py:196
  3.5 0.3 collective-permute-start.1
  3.8 1.1 %slice_bitcast_fusion.2 = (bf16[1,384,256]{2,1,0:T(8,128)(2,1)S(1)}, bf16[1,384,256]{2,1,0:T(8,128)(2,1)S(1)}) fusion(bf16[384,768]{1,0:T(8,128)(2,1)} %bitcast.21), kind=kLoop, calls=%fused_computation.5 | loop fusion | bytes 786432 | tf_op jit(solution)/shard_map/stack | solution.py:198
  4.8 0.0 copy-done.1
  4.9 1.3 %collective-permute-start.6 = (bf16[2,384,256]{2,1,0:T(8,128)(2,1)S(1)}, bf16[2,384,256]{2,1,0:T(8,128)(2,1)S(1)}, u32[]{:S(2)}, u32[]{:S(2)}) collective-permute-start(bf16[2,384,256]{2,1,0:T(8,128)(2,1)S(1)} %pad_maximum_fusion.2.own_ref), channel_id=1, source_target_pairs={{0,2},{1,3},{2,0},{3,1},{4,6},{5,7},{6,4},{7,5},{8,10},{9,11},{10,... | collective-permute-start | bytes 1179656 | tf_op jit(solution)/shard_map/ppermute | solution.py:204
  6.3 6.9 %collective-permute-done.1.next_ref = bf16[2,384,256]{2,1,0:T(8,128)(2,1)S(1)} collective-permute-done((bf16[2,384,256]{2,1,0:T(8,128)(2,1)S(1)}, bf16[2,384,256]{2,1,0:T(8,128)(2,1)S(1)}, u32[]{:S(2)}, u32[]{:S(2)}) %collective-permute-start.1) | collective-permute-done | bytes 393248 | tf_op jit(solution)/shard_map/ppermute | solution.py:204
  13.2 0.2 collective-permute-start.2
  13.4 4.1 %collective-permute-start.3 = (bf16[2,384,256]{2,1,0:T(8,128)(2,1)S(1)}, bf16[2,384,256]{2,1,0:T(8,128)(2,1)S(1)}, u32[]{:S(2)}, u32[]{:S(2)}) collective-permute-start(bf16[2,384,256]{2,1,0:T(8,128)(2,1)S(1)} %pad_maximum_fusion.1.own_ref), channel_id=1, source_target_pairs={{2,4},{3,5},{4,2},{5,3},{10,12},{11,13},{12,10},{13,11},{18,20},{1... | collective-permute-start | bytes 1179656 | tf_op jit(solution)/shard_map/ppermute | solution.py:208
  17.6 1.3 %collective-permute-start.5 = (bf16[2,384,256]{2,1,0:T(8,128)(2,1)S(1)}, bf16[2,384,256]{2,1,0:T(8,128)(2,1)S(1)}, u32[]{:S(2)}, u32[]{:S(2)}) collective-permute-start(bf16[2,384,256]{2,1,0:T(8,128)(2,1)S(1)} %collective-permute-done.1.next_ref), channel_id=1, source_target_pairs={{0,4},{1,5},{6,2},{7,3},{8,12},{9,13},{14,10},{15,11},{16,20},{17,... | collective-permute-start | bytes 1179656 | tf_op jit(solution)/shard_map/ppermute | solution.py:206
  18.9 2.8 %collective-permute-done.6.next_ref = bf16[2,384,256]{2,1,0:T(8,128)(2,1)S(1)} collective-permute-done((bf16[2,384,256]{2,1,0:T(8,128)(2,1)S(1)}, bf16[2,384,256]{2,1,0:T(8,128)(2,1)S(1)}, u32[]{:S(2)}, u32[]{:S(2)}) %collective-permute-start.6) | collective-permute-done | bytes 393248 | tf_op jit(solution)/shard_map/ppermute | solution.py:204
  21.7 6.3 %collective-permute-done = bf16[384,768]{1,0:T(8,128)(2,1)S(1)} collective-permute-done((bf16[384,768]{1,0:T(8,128)(2,1)}, bf16[384,768]{1,0:T(8,128)(2,1)S(1)}, u32[]{:S(2)}, u32[]{:S(2)}) %collective-permute-start) | collective-permute-done | bytes 589856 | tf_op jit(solution)/shard_map/ppermute | solution.py:199
  28.0 1.3 %collective-permute-start.7 = (bf16[2,384,256]{2,1,0:T(8,128)(2,1)S(1)}, bf16[2,384,256]{2,1,0:T(8,128)(2,1)S(1)}, u32[]{:S(2)}, u32[]{:S(2)}) collective-permute-start(bf16[2,384,256]{2,1,0:T(8,128)(2,1)S(1)} %collective-permute-done.6.next_ref), channel_id=1, source_target_pairs={{0,4},{1,5},{6,2},{7,3},{8,12},{9,13},{14,10},{15,11},{16,20},{17,... | collective-permute-start | bytes 1179656 | tf_op jit(solution)/shard_map/ppermute | solution.py:206
  29.3 0.0 copy-done.2
  29.4 8.0 %collective-permute-done.5.far_ref = bf16[2,384,256]{2,1,0:T(8,128)(2,1)S(1)} collective-permute-done((bf16[2,384,256]{2,1,0:T(8,128)(2,1)S(1)}, bf16[2,384,256]{2,1,0:T(8,128)(2,1)S(1)}, u32[]{:S(2)}, u32[]{:S(2)}) %collective-permute-start.5) | collective-permute-done | bytes 393248 | tf_op jit(solution)/shard_map/ppermute | solution.py:206
  37.4 2.0 %attend.11 = bf16[416,256]{1,0:T(8,128)(2,1)S(1)} custom-call(bf16[384,256]{1,0:T(8,128)(2,1)S(1)} %get-tuple-element.37.q_ref, bf16[2,384,256]{2,1,0:T(8,128)(2,1)S(1)} %pad_maximum_fusion.own_ref, bf16[2,384,256]{2,1,0:T(8,128)(2,1)S(1)} %collective-permute-done.1.next_ref, bf16[2,384,256]{2,1,0:T(8,128)(2,1)S(1)} %collective-permute-done.5.far_ref), custom_call_target="tpu_custom_call" | custom-call | flops 452984832 | bytes 1572864 | tf_op jit(solution)/shard_map/attend/pallas_call | solution.py:75
  39.4 0.1 collective-permute-start.11
  39.5 7.0 %collective-permute-done.7.far_ref = bf16[2,384,256]{2,1,0:T(8,128)(2,1)S(1)} collective-permute-done((bf16[2,384,256]{2,1,0:T(8,128)(2,1)S(1)}, bf16[2,384,256]{2,1,0:T(8,128)(2,1)S(1)}, u32[]{:S(2)}, u32[]{:S(2)}) %collective-permute-start.7) | collective-permute-done | bytes 393248 | tf_op jit(solution)/shard_map/ppermute | solution.py:206
  46.5 0.0 copy-start
  46.5 2.0 %attend.10 = bf16[416,256]{1,0:T(8,128)(2,1)S(1)} custom-call(bf16[384,256]{1,0:T(8,128)(2,1)S(1)} %get-tuple-element.38.q_ref, bf16[2,384,256]{2,1,0:T(8,128)(2,1)S(1)} %pad_maximum_fusion.2.own_ref, bf16[2,384,256]{2,1,0:T(8,128)(2,1)S(1)} %collective-permute-done.6.next_ref, bf16[2,384,256]{2,1,0:T(8,128)(2,1)S(1)} %collective-permute-done.7.far_ref), custom_call_target="tpu_custom_call" | custom-call | flops 452984832 | bytes 1572864 | tf_op jit(solution)/shard_map/attend/pallas_call | solution.py:75
  48.5 0.1 collective-permute-start.9
  48.6 0.0 collective-permute-done.2.next_ref
  48.6 0.0 collective-permute-done.3.far_ref
  48.6 2.0 %attend.6 = bf16[416,256]{1,0:T(8,128)(2,1)S(1)} custom-call(bf16[384,256]{1,0:T(8,128)(2,1)S(1)} %get-tuple-element.39.q_ref, bf16[2,384,256]{2,1,0:T(8,128)(2,1)S(1)} %pad_maximum_fusion.1.own_ref, bf16[2,384,256]{2,1,0:T(8,128)(2,1)S(1)} %collective-permute-done.2.next_ref, bf16[2,384,256]{2,1,0:T(8,128)(2,1)S(1)} %collective-permute-done.3.far_ref), custom_call_target="tpu_custom_call" | custom-call | flops 452984832 | bytes 1572864 | tf_op jit(solution)/shard_map/attend/pallas_call | solution.py:75
  50.6 2.4 %collective-permute-start.4 = (bf16[416,256]{1,0:T(8,128)(2,1)S(1)}, bf16[416,256]{1,0:T(8,128)(2,1)S(1)}, u32[]{:S(2)}, u32[]{:S(2)}) collective-permute-start(bf16[416,256]{1,0:T(8,128)(2,1)S(1)} %attend.6), channel_id=1, source_target_pairs={{8,0},{9,1},{10,2},{11,3},{12,4},{13,5},{14,6},{15,7},{0,8},{1,9},... | collective-permute-start | bytes 638984 | tf_op jit(solution)/shard_map/ppermute | solution.py:214
  53.0 2.0 %attend.7.refs_0_ = f32[416,256]{1,0:T(8,128)S(1)} custom-call(bf16[384,256]{1,0:T(8,128)(2,1)S(1)} %get-tuple-element.24.q_ref, bf16[2,384,256]{2,1,0:T(8,128)(2,1)S(1)} %pad_maximum_fusion.1.own_ref, bf16[2,384,256]{2,1,0:T(8,128)(2,1)S(1)} %collective-permute-done.2.next_ref, bf16[2,384,256]{2,1,0:T(8,128)(2,1)S(1)} %collective-permute-done.3.far_ref), custom_call_target="tpu_custom_call" | custom-call | flops 452984832 | bytes 1572864 | tf_op jit(solution)/shard_map/attend/pallas_call | solution.py:75
  55.0 2.0 %attend.8.refs_0_ = f32[416,256]{1,0:T(8,128)S(1)} custom-call(bf16[384,256]{1,0:T(8,128)(2,1)S(1)} %get-tuple-element.25.q_ref, bf16[2,384,256]{2,1,0:T(8,128)(2,1)S(1)} %pad_maximum_fusion.own_ref, bf16[2,384,256]{2,1,0:T(8,128)(2,1)S(1)} %collective-permute-done.1.next_ref, bf16[2,384,256]{2,1,0:T(8,128)(2,1)S(1)} %collective-permute-done.5.far_ref), custom_call_target="tpu_custom_call" | custom-call | flops 452984832 | bytes 1572864 | tf_op jit(solution)/shard_map/attend/pallas_call | solution.py:75
  57.1 2.0 %attend.9.refs_0_ = f32[416,256]{1,0:T(8,128)S(1)} custom-call(bf16[384,256]{1,0:T(8,128)(2,1)S(1)} %get-tuple-element.26.q_ref, bf16[2,384,256]{2,1,0:T(8,128)(2,1)S(1)} %pad_maximum_fusion.2.own_ref, bf16[2,384,256]{2,1,0:T(8,128)(2,1)S(1)} %collective-permute-done.6.next_ref, bf16[2,384,256]{2,1,0:T(8,128)(2,1)S(1)} %collective-permute-done.7.far_ref), custom_call_target="tpu_custom_call" | custom-call | flops 452984832 | bytes 1572864 | tf_op jit(solution)/shard_map/attend/pallas_call | solution.py:75
  59.1 0.0 collective-permute-done.11.refs_1_
  59.1 0.6 join.5
  59.7 2.6 %collective-permute-start.12 = (bf16[192,256]{1,0:T(8,128)(2,1)S(1)}, bf16[192,256]{1,0:T(8,128)(2,1)S(1)}, u32[]{:S(2)}, u32[]{:S(2)}) collective-permute-start(bf16[192,256]{1,0:T(8,128)(2,1)S(1)} %get-tuple-element.36), channel_id=1, source_target_pairs={{0,1},{1,0},{2,3},{3,2},{4,5},{5,4},{6,7},{7,6},{8,9},{9,8},{10,11... | collective-permute-start | bytes 294920 | tf_op jit(solution)/shard_map/ppermute | solution.py:220
  62.3 2.7 %collective-permute-done.9.refs_1_ = bf16[416,256]{1,0:T(8,128)(2,1)S(1)} collective-permute-done((bf16[416,256]{1,0:T(8,128)(2,1)S(1)}, bf16[416,256]{1,0:T(8,128)(2,1)S(1)}, u32[]{:S(2)}, u32[]{:S(2)}) %collective-permute-start.9) | collective-permute-done | bytes 213024 | tf_op jit(solution)/shard_map/ppermute | solution.py:214
  65.0 0.8 %join.4 = (bf16[192,256]{1,0:T(8,128)(2,1)S(1)}, bf16[192,256]{1,0:T(8,128)(2,1)S(1)}) custom-call(f32[416,256]{1,0:T(8,128)S(1)} %attend.9.refs_0_, bf16[416,256]{1,0:T(8,128)(2,1)S(1)} %collective-permute-done.9.refs_1_), custom_call_target="tpu_custom_call" | custom-call | flops 786432 | bytes 983040 | tf_op jit(solution)/shard_map/join/pallas_call | solution.py:124
  65.8 1.3 %collective-permute-start.10 = (bf16[192,256]{1,0:T(8,128)(2,1)S(1)}, bf16[192,256]{1,0:T(8,128)(2,1)S(1)}, u32[]{:S(2)}, u32[]{:S(2)}) collective-permute-start(bf16[192,256]{1,0:T(8,128)(2,1)S(1)} %get-tuple-element.33), channel_id=1, source_target_pairs={{0,1},{1,0},{2,3},{3,2},{4,5},{5,4},{6,7},{7,6},{8,9},{9,8},{10,11... | collective-permute-start | bytes 294920 | tf_op jit(solution)/shard_map/ppermute | solution.py:220
  67.1 2.5 %collective-permute-done.4.refs_1_ = bf16[416,256]{1,0:T(8,128)(2,1)S(1)} collective-permute-done((bf16[416,256]{1,0:T(8,128)(2,1)S(1)}, bf16[416,256]{1,0:T(8,128)(2,1)S(1)}, u32[]{:S(2)}, u32[]{:S(2)}) %collective-permute-start.4) | collective-permute-done | bytes 213024 | tf_op jit(solution)/shard_map/ppermute | solution.py:214
  69.6 0.6 join.3
  70.2 0.9 %collective-permute-start.8 = (bf16[192,256]{1,0:T(8,128)(2,1)S(1)}, bf16[192,256]{1,0:T(8,128)(2,1)S(1)}, u32[]{:S(2)}, u32[]{:S(2)}) collective-permute-start(bf16[192,256]{1,0:T(8,128)(2,1)S(1)} %get-tuple-element.29), channel_id=1, source_target_pairs={{0,1},{1,0},{2,3},{3,2},{4,5},{5,4},{6,7},{7,6},{8,9},{9,8},{10,11... | collective-permute-start | bytes 294920 | tf_op jit(solution)/shard_map/ppermute | solution.py:220
  71.1 0.0 collective-permute-done.12.refs_1_
  71.1 0.0 copy-done
  71.1 0.8 %project.4.refs_3_ = f32[192,3072]{1,0:T(8,128)S(1)} custom-call(bf16[192,256]{1,0:T(8,128)(2,1)S(1)} %get-tuple-element.35.refs_0_, bf16[192,256]{1,0:T(8,128)(2,1)S(1)} %collective-permute-done.12.refs_1_, bf16[2,768,3072]{2,1,0:T(8,128)(2,1)S(1)} %bitcast.16), custom_call_target="tpu_custom_call" | custom-call | flops 603979776 | bytes 5505024 | tf_op jit(solution)/shard_map/project/pallas_call | solution.py:156
  71.9 0.0 collective-permute-done.10.refs_1_
  71.9 0.8 %project.5.refs_2_ = f32[192,3072]{1,0:T(8,128)S(1)} custom-call(bf16[192,256]{1,0:T(8,128)(2,1)S(1)} %get-tuple-element.32.refs_0_, bf16[192,256]{1,0:T(8,128)(2,1)S(1)} %collective-permute-done.10.refs_1_, bf16[2,768,3072]{2,1,0:T(8,128)(2,1)S(1)} %bitcast.17, f32[192,3072]{1,0:T(8,128)S(1)} %project.4.refs_3_), custom_call_target="tpu_custom_call" | custom-call | flops 603979776 | bytes 5505024 | tf_op jit(solution)/shard_map/project/pallas_call | solution.py:156
  72.7 0.5 project.6.refs_2_
  73.2 0.0 collective-permute-done.8.refs_0_
  73.2 1.5 %project.7 = bf16[192,3072]{1,0:T(8,128)(2,1)} custom-call(bf16[192,256]{1,0:T(8,128)(2,1)S(1)} %collective-permute-done.8.refs_0_, bf16[2,768,3072]{2,1,0:T(8,128)(2,1)S(1)} %bitcast.19, f32[192,3072]{1,0:T(8,128)S(1)} %project.6.refs_2_), custom_call_target="tpu_custom_call" | custom-call | flops 301989888 | bytes 3932160 | tf_op jit(solution)/shard_map/project/pallas_call | solution.py:156
  (6 shorter events, 0.2 us)
Async XLA Ops:
  0.0 4.8 %copy-start.1 = (bf16[1,384,768]{2,1,0:T(8,128)(2,1)S(1)}, bf16[1,384,768]{2,1,0:T(8,128)(2,1)}, u32[]{:S(2)}) copy-start(bf16[1,384,768]{2,1,0:T(8,128)(2,1)} %param.5) | copy-start | bytes 1769476
  0.0 28.0 %collective-permute-start = (bf16[384,768]{1,0:T(8,128)(2,1)}, bf16[384,768]{1,0:T(8,128)(2,1)S(1)}, u32[]{:S(2)}, u32[]{:S(2)}) collective-permute-start(bf16[384,768]{1,0:T(8,128)(2,1)} %bitcast.24), channel_id=1, source_target_pairs={{0,8},{1,9},{2,10},{3,11},{4,12},{5,13},{6,14},{7,15},{8,0},{9,1},... | collective-permute-start | bytes 1769480 | tf_op jit(solution)/shard_map/ppermute | solution.py:199
  2.3 27.0 %copy-start.2 = (bf16[1,384,768]{2,1,0:T(8,128)(2,1)S(1)}, bf16[1,384,768]{2,1,0:T(8,128)(2,1)}, u32[]{:S(2)}) copy-start(bf16[1,384,768]{2,1,0:T(8,128)(2,1)} %param.4) | copy-start | bytes 1769476
  3.5 9.7 %collective-permute-start.1 = (bf16[2,384,256]{2,1,0:T(8,128)(2,1)S(1)}, bf16[2,384,256]{2,1,0:T(8,128)(2,1)S(1)}, u32[]{:S(2)}, u32[]{:S(2)}) collective-permute-start(bf16[2,384,256]{2,1,0:T(8,128)(2,1)S(1)} %pad_maximum_fusion.own_ref), channel_id=1, source_target_pairs={{0,2},{1,3},{2,0},{3,1},{4,6},{5,7},{6,4},{7,5},{8,10},{9,11},{10,... | collective-permute-start | bytes 1179656 | tf_op jit(solution)/shard_map/ppermute | solution.py:204
  4.9 16.8 %collective-permute-start.6 = (bf16[2,384,256]{2,1,0:T(8,128)(2,1)S(1)}, bf16[2,384,256]{2,1,0:T(8,128)(2,1)S(1)}, u32[]{:S(2)}, u32[]{:S(2)}) collective-permute-start(bf16[2,384,256]{2,1,0:T(8,128)(2,1)S(1)} %pad_maximum_fusion.2.own_ref), channel_id=1, source_target_pairs={{0,2},{1,3},{2,0},{3,1},{4,6},{5,7},{6,4},{7,5},{8,10},{9,11},{10,... | collective-permute-start | bytes 1179656 | tf_op jit(solution)/shard_map/ppermute | solution.py:204
  13.2 35.4 %collective-permute-start.2 = (bf16[2,384,256]{2,1,0:T(8,128)(2,1)S(1)}, bf16[2,384,256]{2,1,0:T(8,128)(2,1)S(1)}, u32[]{:S(2)}, u32[]{:S(2)}) collective-permute-start(bf16[2,384,256]{2,1,0:T(8,128)(2,1)S(1)} %pad_maximum_fusion.1.own_ref), channel_id=1, source_target_pairs={{0,2},{1,3},{2,0},{3,1},{4,6},{5,7},{6,4},{7,5},{8,10},{9,11},{10,... | collective-permute-start | bytes 1179656 | tf_op jit(solution)/shard_map/ppermute | solution.py:204
  13.4 35.2 %collective-permute-start.3 = (bf16[2,384,256]{2,1,0:T(8,128)(2,1)S(1)}, bf16[2,384,256]{2,1,0:T(8,128)(2,1)S(1)}, u32[]{:S(2)}, u32[]{:S(2)}) collective-permute-start(bf16[2,384,256]{2,1,0:T(8,128)(2,1)S(1)} %pad_maximum_fusion.1.own_ref), channel_id=1, source_target_pairs={{2,4},{3,5},{4,2},{5,3},{10,12},{11,13},{12,10},{13,11},{18,20},{1... | collective-permute-start | bytes 1179656 | tf_op jit(solution)/shard_map/ppermute | solution.py:208
  17.6 19.8 %collective-permute-start.5 = (bf16[2,384,256]{2,1,0:T(8,128)(2,1)S(1)}, bf16[2,384,256]{2,1,0:T(8,128)(2,1)S(1)}, u32[]{:S(2)}, u32[]{:S(2)}) collective-permute-start(bf16[2,384,256]{2,1,0:T(8,128)(2,1)S(1)} %collective-permute-done.1.next_ref), channel_id=1, source_target_pairs={{0,4},{1,5},{6,2},{7,3},{8,12},{9,13},{14,10},{15,11},{16,20},{17,... | collective-permute-start | bytes 1179656 | tf_op jit(solution)/shard_map/ppermute | solution.py:206
  28.0 18.5 %collective-permute-start.7 = (bf16[2,384,256]{2,1,0:T(8,128)(2,1)S(1)}, bf16[2,384,256]{2,1,0:T(8,128)(2,1)S(1)}, u32[]{:S(2)}, u32[]{:S(2)}) collective-permute-start(bf16[2,384,256]{2,1,0:T(8,128)(2,1)S(1)} %collective-permute-done.6.next_ref), channel_id=1, source_target_pairs={{0,4},{1,5},{6,2},{7,3},{8,12},{9,13},{14,10},{15,11},{16,20},{17,... | collective-permute-start | bytes 1179656 | tf_op jit(solution)/shard_map/ppermute | solution.py:206
  39.4 19.7 %collective-permute-start.11 = (bf16[416,256]{1,0:T(8,128)(2,1)S(1)}, bf16[416,256]{1,0:T(8,128)(2,1)S(1)}, u32[]{:S(2)}, u32[]{:S(2)}) collective-permute-start(bf16[416,256]{1,0:T(8,128)(2,1)S(1)} %attend.11), channel_id=1, source_target_pairs={{8,0},{9,1},{10,2},{11,3},{12,4},{13,5},{14,6},{15,7},{0,8},{1,9},... | collective-permute-start | bytes 638984 | tf_op jit(solution)/shard_map/ppermute | solution.py:214
  46.5 24.6 %copy-start = (bf16[1536,3072]{1,0:T(8,128)(2,1)S(1)}, bf16[1536,3072]{1,0:T(8,128)(2,1)}, u32[]{:S(2)}) copy-start(bf16[1536,3072]{1,0:T(8,128)(2,1)} %param.7) | copy-start | bytes 28311556
  48.5 16.5 %collective-permute-start.9 = (bf16[416,256]{1,0:T(8,128)(2,1)S(1)}, bf16[416,256]{1,0:T(8,128)(2,1)S(1)}, u32[]{:S(2)}, u32[]{:S(2)}) collective-permute-start(bf16[416,256]{1,0:T(8,128)(2,1)S(1)} %attend.10), channel_id=1, source_target_pairs={{8,0},{9,1},{10,2},{11,3},{12,4},{13,5},{14,6},{15,7},{0,8},{1,9},... | collective-permute-start | bytes 638984 | tf_op jit(solution)/shard_map/ppermute | solution.py:214
  50.6 19.0 %collective-permute-start.4 = (bf16[416,256]{1,0:T(8,128)(2,1)S(1)}, bf16[416,256]{1,0:T(8,128)(2,1)S(1)}, u32[]{:S(2)}, u32[]{:S(2)}) collective-permute-start(bf16[416,256]{1,0:T(8,128)(2,1)S(1)} %attend.6), channel_id=1, source_target_pairs={{8,0},{9,1},{10,2},{11,3},{12,4},{13,5},{14,6},{15,7},{0,8},{1,9},... | collective-permute-start | bytes 638984 | tf_op jit(solution)/shard_map/ppermute | solution.py:214
  59.7 11.4 %collective-permute-start.12 = (bf16[192,256]{1,0:T(8,128)(2,1)S(1)}, bf16[192,256]{1,0:T(8,128)(2,1)S(1)}, u32[]{:S(2)}, u32[]{:S(2)}) collective-permute-start(bf16[192,256]{1,0:T(8,128)(2,1)S(1)} %get-tuple-element.36), channel_id=1, source_target_pairs={{0,1},{1,0},{2,3},{3,2},{4,5},{5,4},{6,7},{7,6},{8,9},{9,8},{10,11... | collective-permute-start | bytes 294920 | tf_op jit(solution)/shard_map/ppermute | solution.py:220
  65.8 6.1 %collective-permute-start.10 = (bf16[192,256]{1,0:T(8,128)(2,1)S(1)}, bf16[192,256]{1,0:T(8,128)(2,1)S(1)}, u32[]{:S(2)}, u32[]{:S(2)}) collective-permute-start(bf16[192,256]{1,0:T(8,128)(2,1)S(1)} %get-tuple-element.33), channel_id=1, source_target_pairs={{0,1},{1,0},{2,3},{3,2},{4,5},{5,4},{6,7},{7,6},{8,9},{9,8},{10,11... | collective-permute-start | bytes 294920 | tf_op jit(solution)/shard_map/ppermute | solution.py:220
  70.2 3.0 %collective-permute-start.8 = (bf16[192,256]{1,0:T(8,128)(2,1)S(1)}, bf16[192,256]{1,0:T(8,128)(2,1)S(1)}, u32[]{:S(2)}, u32[]{:S(2)}) collective-permute-start(bf16[192,256]{1,0:T(8,128)(2,1)S(1)} %get-tuple-element.29), channel_id=1, source_target_pairs={{0,1},{1,0},{2,3},{3,2},{4,5},{5,4},{6,7},{7,6},{8,9},{9,8},{10,11... | collective-permute-start | bytes 294920 | tf_op jit(solution)/shard_map/ppermute | solution.py:220

commit v3 on v2

--- a/solution.py
+++ b/solution.py
@@ -29,30 +29,27 @@
     return -(-rows // width)
 
 
-def attend_kernel(q_ref, own_ref, next_ref, far_ref, out_ref):
+def is_edge():
     col = (lax.axis_index("tm") // 2) % TCOLS
-    far_ok = (col == 1) | (col == 2)
+    return (col == 0) | (col == TCOLS - 1)
+
+
+def attend_tiles(q_ref, tiles, out_ref):
     rows, width = q_ref.shape
     stats = []
     for head in range(width // HD):
         cols = slice(head * HD, (head + 1) * HD)
         query = q_ref[:, cols]
-        s_own = dot_rows(own_ref[0, :, cols], query)
-        s_next = dot_rows(next_ref[0, :, cols], query)
-        s_far = dot_rows(far_ref[0, :, cols], query)
-        s_far = jnp.where(far_ok, s_far, MASKED)
-        top = jnp.maximum(jnp.maximum(s_own, s_next), s_far)
-        top = jnp.max(top, axis=0, keepdims=True).astype(jnp.bfloat16).astype(jnp.float32)
+        scores = [dot_rows(tile[0, :, cols], query) for tile in tiles]
+        top = jnp.max(functools.reduce(jnp.maximum, scores), axis=0, keepdims=True)
+        top = top.astype(jnp.bfloat16).astype(jnp.float32)
         total = jnp.zeros((1, rows), jnp.float32)
         out = jnp.zeros((HD, rows), jnp.float32)
-        for scores, ref in ((s_own, own_ref), (s_next, next_ref), (s_far, far_ref)):
-            probs = jnp.exp2((scores - top) * EXP2_SCALE).astype(jnp.bfloat16)
+        for score, tile in zip(scores, tiles):
+            probs = jnp.exp2((score - top) * EXP2_SCALE).astype(jnp.bfloat16)
             total += jnp.sum(probs.astype(jnp.float32), axis=0, keepdims=True)
             out += lax.dot_general(
-                ref[1, :, cols],
-                probs,
-                (((0,), (0,)), ((), ())),
-                preferred_element_type=jnp.float32,
+                tile[1, :, cols], probs, (((0,), (0,)), ((), ())), preferred_element_type=jnp.float32
             )
         high = total.astype(jnp.bfloat16).astype(jnp.float32)
         stats += [top, high, total - high]
@@ -69,20 +66,31 @@
         out_ref[first : first + STAT_ROWS, :] = piece.astype(out_ref.dtype)
 
 
-def attend(query, own, nxt, far, dtype):
+def attend_kernel(edges, inners, q_ref, *refs):
+    tiles, out_ref = refs[:-1], refs[-1]
+    edge = is_edge()
+    if edges and inners:
+        attend_tiles(q_ref, tiles, out_ref)
+    elif edges:
+        pl.when(edge)(lambda: attend_tiles(q_ref, tiles, out_ref))
+    else:
+        pl.when(jnp.logical_not(edge))(lambda: attend_tiles(q_ref, tiles, out_ref))
+
+
+def attend(query, tiles, edges, inners, dtype, weight=1.0):
     rows, width = query.shape
-    keys = 3 * own.shape[1]
+    keys = len(tiles) * rows
     return pl.pallas_call(
-        attend_kernel,
+        functools.partial(attend_kernel, edges, inners),
         out_shape=jax.ShapeDtypeStruct((rows + STAT_ROWS * stat_blocks(rows, width), width), dtype),
         compiler_params=pltpu.CompilerParams(vmem_limit_bytes=VMEM_BYTES),
         cost_estimate=pl.CostEstimate(
-            flops=4 * rows * keys * width,
-            bytes_accessed=2 * width * (2 * rows + 2 * keys),
-            transcendentals=rows * keys * width // HD,
+            flops=int(weight * 4 * rows * keys * width),
+            bytes_accessed=int(weight * 2 * width * (2 * rows + 2 * keys)),
+            transcendentals=int(weight * rows * keys * width // HD),
         ),
         name="attend",
-    )(query, own, nxt, far)
+    )(query, *tiles)
 
 
 def join_kernel(steps, time_count, *refs):
@@ -92,12 +100,23 @@
     position = lax.axis_index("tm")
     group = position % 2
     time_tile = position // (2 * TCOLS)
+    edge = is_edge()
+
+    def load(ref, *index):
+        at_edge, inner = ref
+        inner = inner[index].astype(jnp.float32)
+        return jnp.where(edge, 0.0 if at_edge is None else at_edge[index].astype(jnp.float32), inner)
+
+    near, far = refs[:2]
+    sources = [(near, near), (None, far)] + [refs[2 + 2 * n : 4 + 2 * n] for n in range(len(steps))]
     parts = []
-    for ref, step in zip(refs, (0, *steps)):
+    for ref, step in zip(sources, (0, 0, *steps)):
         source = time_tile + step
         ok = None if step == 0 or time_count == 2 else (source >= 0) & (source < time_count)
+        if ref[0] is None:
+            ok = jnp.logical_not(edge)
         stats = [
-            ref[rows + block * STAT_ROWS : rows + (block + 1) * STAT_ROWS, :].astype(jnp.float32)
+            load(ref, slice(rows + block * STAT_ROWS, rows + (block + 1) * STAT_ROWS), slice(None))
             for block in range(stat_blocks(rows, width))
         ]
         stats = jnp.concatenate(stats, axis=1)[:, :rows].T
@@ -112,7 +131,7 @@
         top = functools.reduce(jnp.maximum, tops)
         weights = [jnp.exp2((t - top) * EXP2_SCALE) for t in tops]
         inverse = 1.0 / sum(w * s for w, s in zip(weights, sums))
-        value = sum((w * inverse) * p[0][:rows, cols].astype(jnp.float32) for w, p in zip(weights, parts))
+        value = sum((w * inverse) * load(p[0], slice(rows), cols) for w, p in zip(weights, parts))
         value = value.astype(jnp.bfloat16)
         mine_ref[:, cols] = jnp.where(group == 0, value[:half], value[half:])
         other_ref[:, cols] = jnp.where(group == 0, value[half:], value[:half])
@@ -168,62 +187,83 @@
     )(*args)
 
 
+def reverse(route):
+    return [(b, a) for a, b in route]
+
+
 def per_device(query_states, key_states, value_states, out_weight):
     query, key, value = query_states[0], key_states[0], value_states[0]
-    half_width = query.shape[1]
+    rows, half_width = query.shape
     devices = lax.axis_size("tm")
     time_count = devices // (2 * TCOLS)
     places = range(devices)
     row = 2 * TCOLS
-    width = CHUNK_HEADS * HD
-    chunks = half_width // width
+
+    def at_edge(place):
+        return (place // 2) % TCOLS in (0, TCOLS - 1)
 
     next_route = [(p, p ^ 2) for p in places]
-    far_route = [(p, p ^ 4) for p in places if (p // 2) % TCOLS in (0, 3)]
-    across_route = [(p, p ^ 6) for p in places if (p // 2) % TCOLS in (1, 2)]
+    far_route = [(p, p ^ 4) for p in places if at_edge(p)]
+    across_route = [(p, p ^ 6) for p in places if not at_edge(p)]
     if time_count == 2:
         steps = (1,)
         ask_routes = [[(p, p ^ row) for p in places]]
     else:
         steps = (1, -1)
         ask_routes = [[(p, p + s * row) for p in places if 0 <= p + s * row < devices] for s in steps]
-    back_routes = [[(b, a) for a, b in route] for route in ask_routes]
+    edge_routes = [[pair for pair in route if at_edge(pair[0])] for route in ask_routes]
+    inner_routes = [[pair for pair in route if not at_edge(pair[0])] for route in ask_routes]
     core_route = [(p, p ^ 1) for p in places]
 
     weight = out_weight.reshape(2, half_width, out_weight.shape[1])
-    cuts = [slice(c * width, (c + 1) * width) for c in range(chunks)]
+    middle = half_width // HD // 2 * HD
+    cuts = slice(0, middle), slice(middle, half_width)
     q_parts = [query[:, cut] for cut in cuts]
-    kv_parts = [jnp.stack((key[:, cuts[0]], value[:, cuts[0]]))]
-    key, value = after((key, value), kv_parts[0])
-    kv_parts += [jnp.stack((key[:, cut], value[:, cut])) for cut in cuts[1:]]
-    asked_all = [lax.ppermute(query, "tm", route) for route in ask_routes]
-    asked = [[q[:, cut] for q in asked_all] for cut in cuts]
-    nexts, fars = [], []
-    for c in range(chunks):
-        kv_part = after(kv_parts[c], nexts[0]) if c == chunks - 1 else kv_parts[c]
-        nexts.append(lax.ppermute(kv_part, "tm", next_route))
-        if c < chunks - 1:
-            fars.append(lax.ppermute(after(nexts[c], *asked_all) if c else nexts[c], "tm", far_route))
-        else:
-            fars.append(lax.ppermute(kv_part, "tm", across_route))
-    total = None
-    owns, backs = [], []
-    for c in range(chunks):
-        keys = kv_parts[c], nexts[c], fars[c]
-        remote = [attend(q, *keys, jnp.bfloat16) for q in asked[c]]
-        backs.append([lax.ppermute(part, "tm", route) for part, route in zip(remote, back_routes)])
-        owns.append(keys)
-    owns = [attend(after(q_parts[c], *remote), *owns[c], jnp.float32) for c in range(chunks)]
-    backs = [[after(back, *owns) for back in parts] for parts in backs]
-    for c in range(chunks):
-        mine, other = join((owns[c], *backs[c]), query.shape[0], steps, time_count)
-        other = lax.ppermute(other, "tm", core_route)
-        if c < chunks - 1:
-            total = project((mine, other), (False, True), weight, cuts[c].start, total, jnp.float32)
-        else:
-            total = project((mine,), (False,), weight, cuts[c].start, total, jnp.float32)
-            total = project((other,), (True,), weight, cuts[c].start, total, jnp.bfloat16)
-    return total
+    own_0 = jnp.stack((key[:, cuts[0]], value[:, cuts[0]]))
+    key, value = after((key, value), own_0)
+    own_1 = jnp.stack((key[:, cuts[1]], value[:, cuts[1]]))
+
+    edge_query = after(query, own_0)
+    edge_asks = [lax.ppermute(edge_query, "tm", route) for route in edge_routes]
+    next_0 = lax.ppermute(own_0, "tm", next_route)
+    next_1 = lax.ppermute(own_1, "tm", next_route)
+    inner_query = after(query, next_0)
+    inner_asks = [lax.ppermute(inner_query, "tm", route) for route in inner_routes]
+    far_0 = lax.ppermute(next_0, "tm", far_route)
+    far_1 = lax.ppermute(after(own_1, next_0), "tm", across_route)
+    tiles = (own_0, next_0, far_0), (own_1, next_1, far_1)
+
+    def answer(asks, chunk, edges, earlier):
+        near = tiles[chunk][:2] if edges else tiles[chunk]
+        return [attend(after(q[:, cuts[chunk]], *earlier), near, edges, not edges, jnp.bfloat16) for q in asks]
+
+    def back(parts, routes):
+        return [lax.ppermute(part, "tm", reverse(route)) for part, route in zip(parts, routes)]
+
+    edge_0 = answer(edge_asks, 0, True, ())
+    edge_back_0 = back(edge_0, edge_routes)
+    edge_1 = answer(edge_asks, 1, True, edge_0)
+    edge_back_1 = back(edge_1, edge_routes)
+    nears = [
+        attend(after(q_parts[c], *edge_1), tiles[c][:2], True, True, jnp.float32, weight=0.01)
+        for c in range(2)
+    ]
+    inner_0 = answer(inner_asks, 0, False, nears)
+    inner_back_0 = back(inner_0, inner_routes)
+    inner_1 = answer(inner_asks, 1, False, (*inner_0, *edge_back_1))
+    inner_back_1 = back(inner_1, inner_routes)
+    fars = [attend(after(q_parts[c], *inner_1), tiles[c][2:], False, True, jnp.float32) for c in range(2)]
+
+    def joined(chunk, edge_back, inner_back, earlier):
+        backs = [after(part, earlier) for pair in zip(edge_back, inner_back) for part in pair]
+        mine, other = join((nears[chunk], fars[chunk], *backs), rows, steps, time_count)
+        return mine, lax.ppermute(other, "tm", core_route)
+
+    mine, other = joined(0, edge_back_0, inner_back_0, fars[1])
+    total = project((mine, other), (False, True), weight, 0, None, jnp.float32)
+    mine, other = joined(1, edge_back_1, inner_back_1, total)
+    total = project((mine,), (False,), weight, middle, total, jnp.float32)
+    return project((other,), (True,), weight, middle, total, jnp.bfloat16)
 
 
 def solution(mesh):

time: 75.2 us -> 72.7 us (0.967)
  waiting for transfers between devices: 36.3 us -> 26.4 us
  starting transfers between devices: 18.2 us -> 25.1 us
  Pallas kernels: 17.6 us -> 18.5 us
  local copies, waits for them, and re-layouts: 2.28 us -> 1.52 us
    ppermute x13 -> x12, waiting for transfers between devices: 36.3 us -> 26.4 us  [the longest x1 9.35 us: per_device(): next_1 = lax.ppermute(own_1, 'tm', next_route)]
    ppermute x13 -> x12, starting transfers between devices: 18.2 us -> 25.1 us  [the longest x4 7.53 us: back(): lax.ppermute(part, 'tm', reverse(route))]
    another operation x3, local copies, waits for them, and re-layouts: 2.19 us -> 1.3 us  [the longest x1 1.24 us: per_device(): own_0 = jnp.stack((key[:, cuts[0]], value[:, cuts[0]]))]
    pallas_call x4 -> x3, Pallas kernels: 3.63 us -> 3.99 us  [project(): pl.pallas_call(functools.partial(project_kernel, first, swaps, total is n...]
    pallas_call x6 -> x8, Pallas kernels: 12 us -> 12.4 us  [attend(): pl.pallas_call(functools.partial(attend_kernel, edges, inners), out_shape...]
    pallas_call x3 -> x2, Pallas kernels: 1.98 us -> 2.13 us  [join(): pl.pallas_call(functools.partial(join_kernel, steps, time_count), out_sha...]
  transfers between devices with their start and end apart: 13 -> 12, of which waited for: 7 -> 6; matrix products, arithmetic and copies ran while one was open for 3% -> 0% of each run, Pallas kernels for 22% -> 22%
where the time goes in v3:
time: 72.7 us; the launch traced here: 71.9 us
  waiting for transfers between devices  26.4 us (36%)
  starting transfers between devices  25.1 us (35%)
  Pallas kernels  18.5 us (25%)
  local copies, waits for them, and re-layouts  1.52 us (2%)
    pallas_call x8, Pallas kernels, attend(): pl.pallas_call(functools.partial(attend_kernel, edges, inners), out_shape...  12.4 us
    ppermute x1, waiting for transfers between devices, per_device(): next_1 = lax.ppermute(own_1, 'tm', next_route)  9.35 us
    ppermute x1, waiting for transfers between devices, per_device(): next_0 = lax.ppermute(own_0, 'tm', next_route)  8.26 us
    ppermute x4, starting transfers between devices, back(): lax.ppermute(part, 'tm', reverse(route))  7.53 us
    ppermute x1, waiting for transfers between devices, per_device(): far_0 = lax.ppermute(next_0, 'tm', far_route)  6.79 us
    ppermute x1, starting transfers between devices, per_device(): next_1 = lax.ppermute(own_1, 'tm', next_route)  4.82 us
    ppermute x1, starting transfers between devices, per_device(): lax.ppermute(inner_query, 'tm', route)  4.21 us
    pallas_call x3, Pallas kernels, project(): pl.pallas_call(functools.partial(project_kernel, first, swaps, total is n...  3.99 us
  transfers between devices with their start and end apart: 12, of which 6 were waited for; matrix products, arithmetic and copies ran while one was open for 0% of the time, Pallas kernels for 22%

profile of v3, /device:TPU:7, one launch (start us, length us, event | category | flops | bytes accessed | tf_op | source)
XLA Modules:
  0.0 71.9 jit_solution(5441167871056689860)
XLA Ops:
  0.0 1.2 %slice_bitcast_fusion = (bf16[1,384,384]{2,1,0:T(8,128)(2,1)S(1)}, bf16[1,384,384]{2,1,0:T(8,128)(2,1)S(1)}) fusion(bf16[384,768]{1,0:T(8,128)(2,1)} %bitcast.20, bf16[384,768]{1,0:T(8,128)(2,1)} %bitcast.22), kind=kLoop, calls=%fused_computation.2 | loop fusion | bytes 1179648 | tf_op jit(solution)/shard_map/stack | solution.py:222
  1.3 0.1 pad_maximum_fusion.refs_0_
  1.3 0.3 collective-permute-start.1
  1.6 0.0 copy-done
  1.6 0.7 collective-permute-start
  2.3 0.0 copy-done.1
  2.4 0.0 copy-done.2
  2.4 0.0 slice-start
  2.4 0.1 pad_maximum_fusion.1.refs_0_
  2.5 4.8 %collective-permute-start.2 = (bf16[2,384,384]{2,1,0:T(8,128)(2,1)S(1)}, bf16[2,384,384]{2,1,0:T(8,128)(2,1)S(1)}, u32[]{:S(2)}, u32[]{:S(2)}) collective-permute-start(bf16[2,384,384]{2,1,0:T(8,128)(2,1)S(1)} %pad_maximum_fusion.1.refs_0_), channel_id=1, source_target_pairs={{0,2},{1,3},{2,0},{3,1},{4,6},{5,7},{6,4},{7,5},{8,10},{9,11},{10,... | collective-permute-start | bytes 1769480 | tf_op jit(solution)/shard_map/ppermute | solution.py:229
  7.3 8.3 %collective-permute-done.1.refs_1_ = bf16[2,384,384]{2,1,0:T(8,128)(2,1)S(1)} collective-permute-done((bf16[2,384,384]{2,1,0:T(8,128)(2,1)S(1)}, bf16[2,384,384]{2,1,0:T(8,128)(2,1)S(1)}, u32[]{:S(2)}, u32[]{:S(2)}) %collective-permute-start.1) | collective-permute-done | bytes 589856 | tf_op jit(solution)/shard_map/ppermute | solution.py:228
  15.6 4.2 %collective-permute-start.3 = (bf16[384,768]{1,0:T(8,128)(2,1)S(1)}, bf16[384,768]{1,0:T(8,128)(2,1)S(1)}, u32[]{:S(2)}, u32[]{:S(2)}) collective-permute-start(bf16[384,768]{1,0:T(8,128)(2,1)S(1)} %bitcast.18), channel_id=1, source_target_pairs={{2,10},{3,11},{4,12},{5,13},{10,2},{11,3},{12,4},{13,5},{18,26},{1... | collective-permute-start | bytes 1769480 | tf_op jit(solution)/shard_map/ppermute | solution.py:231
  19.8 1.3 %collective-permute-start.4 = (bf16[2,384,384]{2,1,0:T(8,128)(2,1)S(1)}, bf16[2,384,384]{2,1,0:T(8,128)(2,1)S(1)}, u32[]{:S(2)}, u32[]{:S(2)}) collective-permute-start(bf16[2,384,384]{2,1,0:T(8,128)(2,1)S(1)} %collective-permute-done.1.refs_1_), channel_id=1, source_target_pairs={{0,4},{1,5},{6,2},{7,3},{8,12},{9,13},{14,10},{15,11},{16,20},{17,... | collective-permute-start | bytes 1769480 | tf_op jit(solution)/shard_map/ppermute | solution.py:232
  21.1 0.1 fusion
  21.2 3.1 %collective-permute-start.6 = (bf16[2,384,384]{2,1,0:T(8,128)(2,1)S(1)}, bf16[2,384,384]{2,1,0:T(8,128)(2,1)S(1)}, u32[]{:S(2)}, u32[]{:S(2)}) collective-permute-start(bf16[2,384,384]{2,1,0:T(8,128)(2,1)S(1)} %pad_maximum_fusion.1.refs_0_), channel_id=1, source_target_pairs={{2,4},{3,5},{4,2},{5,3},{10,12},{11,13},{12,10},{13,11},{18,20},{1... | collective-permute-start | bytes 1769480 | tf_op jit(solution)/shard_map/ppermute | solution.py:233
  24.3 0.0 collective-permute-done
  24.3 0.1 fusion.2
  24.4 0.7 collective-permute-start.7
  25.1 9.3 %collective-permute-done.2.refs_1_ = bf16[2,384,384]{2,1,0:T(8,128)(2,1)S(1)} collective-permute-done((bf16[2,384,384]{2,1,0:T(8,128)(2,1)S(1)}, bf16[2,384,384]{2,1,0:T(8,128)(2,1)S(1)}, u32[]{:S(2)}, u32[]{:S(2)}) %collective-permute-start.2) | collective-permute-done | bytes 589856 | tf_op jit(solution)/shard_map/ppermute | solution.py:229
  34.5 0.7 collective-permute-start.5
  35.2 0.0 slice-start.1
  35.2 2.1 %attend.10.refs_0_ = f32[400,384]{1,0:T(8,128)S(1)} custom-call(bf16[384,384]{1,0:T(8,128)(2,1)S(1)} %get-tuple-element.35.q_ref, bf16[2,384,384]{2,1,0:T(8,128)(2,1)S(1)} %pad_maximum_fusion.1.refs_0_, bf16[2,384,384]{2,1,0:T(8,128)(2,1)S(1)} %collective-permute-done.2.refs_1_), custom_call_target="tpu_custom_call" | custom-call | flops 4529848 | bytes 17694 | tf_op jit(solution)/shard_map/attend/pallas_call | solution.py:83
  37.3 2.1 %attend.11.refs_0_ = f32[400,384]{1,0:T(8,128)S(1)} custom-call(bf16[384,384]{1,0:T(8,128)(2,1)S(1)} %get-tuple-element.36.q_ref, bf16[2,384,384]{2,1,0:T(8,128)(2,1)S(1)} %pad_maximum_fusion.refs_0_, bf16[2,384,384]{2,1,0:T(8,128)(2,1)S(1)} %collective-permute-done.1.refs_1_), custom_call_target="tpu_custom_call" | custom-call | flops 4529848 | bytes 17694 | tf_op jit(solution)/shard_map/attend/pallas_call | solution.py:83
  39.4 0.0 collective-permute-done.3
  39.4 0.1 fusion.1
  39.5 0.0 slice-start.2
  39.5 6.8 %collective-permute-done.4.refs_2_.refs_0_ = bf16[2,384,384]{2,1,0:T(8,128)(2,1)S(1)} collective-permute-done((bf16[2,384,384]{2,1,0:T(8,128)(2,1)S(1)}, bf16[2,384,384]{2,1,0:T(8,128)(2,1)S(1)}, u32[]{:S(2)}, u32[]{:S(2)}) %collective-permute-start.4) | collective-permute-done | bytes 589856 | tf_op jit(solution)/shard_map/ppermute | solution.py:232
  46.3 2.6 %attend.12 = bf16[400,384]{1,0:T(8,128)(2,1)S(1)} custom-call(bf16[384,384]{1,0:T(8,128)(2,1)S(1)} %get-tuple-element.32.q_ref, bf16[2,384,384]{2,1,0:T(8,128)(2,1)S(1)} %pad_maximum_fusion.refs_0_, bf16[2,384,384]{2,1,0:T(8,128)(2,1)S(1)} %collective-permute-done.1.refs_1_, bf16[2,384,384]{2,1,0:T(8,128)(2,1)S(1)} %collective-permute-done.4.refs_2_.refs_0_), custom_call_target="tpu_custom_call" | custom-call | flops 679477248 | bytes 2359296 | tf_op jit(solution)/shard_map/attend/pallas_call | solution.py:83
  48.9 1.9 %collective-permute-start.8 = (bf16[400,384]{1,0:T(8,128)(2,1)S(1)}, bf16[400,384]{1,0:T(8,128)(2,1)S(1)}, u32[]{:S(2)}, u32[]{:S(2)}) collective-permute-start(bf16[400,384]{1,0:T(8,128)(2,1)S(1)} %attend.12), channel_id=1, source_target_pairs={{10,2},{11,3},{12,4},{13,5},{2,10},{3,11},{4,12},{5,13},{26,18},{2... | collective-permute-start | bytes 921608 | tf_op jit(solution)/shard_map/ppermute | solution.py:241
  50.9 0.0 collective-permute-done.5.refs_2_
  50.9 0.0 collective-permute-done.6.refs_2_.refs_0_
  50.9 2.8 %attend.13 = bf16[400,384]{1,0:T(8,128)(2,1)S(1)} custom-call(bf16[384,384]{1,0:T(8,128)(2,1)S(1)} %get-tuple-element.33.q_ref, bf16[2,384,384]{2,1,0:T(8,128)(2,1)S(1)} %pad_maximum_fusion.1.refs_0_, bf16[2,384,384]{2,1,0:T(8,128)(2,1)S(1)} %collective-permute-done.2.refs_1_, bf16[2,384,384]{2,1,0:T(8,128)(2,1)S(1)} %collective-permute-done.6.refs_2_.refs_0_), custom_call_target="tpu_custom_call" | custom-call | flops 679477248 | bytes 2359296 | tf_op jit(solution)/shard_map/attend/pallas_call | solution.py:83
  53.7 4.3 %collective-permute-start.10 = (bf16[400,384]{1,0:T(8,128)(2,1)S(1)}, bf16[400,384]{1,0:T(8,128)(2,1)S(1)}, u32[]{:S(2)}, u32[]{:S(2)}) collective-permute-start(bf16[400,384]{1,0:T(8,128)(2,1)S(1)} %attend.13), channel_id=1, source_target_pairs={{10,2},{11,3},{12,4},{13,5},{2,10},{3,11},{4,12},{5,13},{26,18},{2... | collective-permute-start | bytes 921608 | tf_op jit(solution)/shard_map/ppermute | solution.py:241
  58.0 1.3 %attend.14.refs_1_ = f32[400,384]{1,0:T(8,128)S(1)} custom-call(bf16[384,384]{1,0:T(8,128)(2,1)S(1)} %get-tuple-element.35.q_ref, bf16[2,384,384]{2,1,0:T(8,128)(2,1)S(1)} %collective-permute-done.6.refs_2_.refs_0_), custom_call_target="tpu_custom_call" | custom-call | flops 226492416 | bytes 1179648 | tf_op jit(solution)/shard_map/attend/pallas_call | solution.py:83
  59.3 0.0 collective-permute-done.7.refs_2_
  59.3 1.3 %attend.15.refs_1_ = f32[400,384]{1,0:T(8,128)S(1)} custom-call(bf16[384,384]{1,0:T(8,128)(2,1)S(1)} %get-tuple-element.36.q_ref, bf16[2,384,384]{2,1,0:T(8,128)(2,1)S(1)} %collective-permute-done.4.refs_2_.refs_0_), custom_call_target="tpu_custom_call" | custom-call | flops 226492416 | bytes 1179648 | tf_op jit(solution)/shard_map/attend/pallas_call | solution.py:83
  60.6 0.0 collective-permute-done.8.refs_3_
  60.7 1.1 %join.2 = (bf16[192,384]{1,0:T(8,128)(2,1)S(1)}, bf16[192,384]{1,0:T(8,128)(2,1)S(1)}) custom-call(f32[400,384]{1,0:T(8,128)S(1)} %attend.11.refs_0_, f32[400,384]{1,0:T(8,128)S(1)} %attend.15.refs_1_, bf16[400,384]{1,0:T(8,128)(2,1)S(1)} %collective-permute-done.7.refs_2_, bf16[400,384]{1,0:T(8,128)(2,1)S(1)} %collective-permute-done.8.refs_3_), custom_call_target="tpu_custom_call" | custom-call | flops 1179648 | bytes 1474560 | tf_op jit(solution)/shard_map/join/pallas_call | solution.py:143
  61.7 1.7 %collective-permute-start.9 = (bf16[192,384]{1,0:T(8,128)(2,1)S(1)}, bf16[192,384]{1,0:T(8,128)(2,1)S(1)}, u32[]{:S(2)}, u32[]{:S(2)}) collective-permute-start(bf16[192,384]{1,0:T(8,128)(2,1)S(1)} %get-tuple-element.40), channel_id=1, source_target_pairs={{0,1},{1,0},{2,3},{3,2},{4,5},{5,4},{6,7},{7,6},{8,9},{9,8},{10,11... | collective-permute-start | bytes 442376 | tf_op jit(solution)/shard_map/ppermute | solution.py:260
  63.5 1.0 %collective-permute-done.9.refs_1_ = bf16[192,384]{1,0:T(8,128)(2,1)S(1)} collective-permute-done((bf16[192,384]{1,0:T(8,128)(2,1)S(1)}, bf16[192,384]{1,0:T(8,128)(2,1)S(1)}, u32[]{:S(2)}, u32[]{:S(2)}) %collective-permute-start.9) | collective-permute-done | bytes 147488 | tf_op jit(solution)/shard_map/ppermute | solution.py:260
  64.5 0.0 slice-done.1
  64.5 1.4 %project.3.refs_2_ = f32[192,3072]{1,0:T(8,128)S(1)} custom-call(bf16[192,384]{1,0:T(8,128)(2,1)S(1)} %get-tuple-element.39.refs_0_, bf16[192,384]{1,0:T(8,128)(2,1)S(1)} %collective-permute-done.9.refs_1_, bf16[2,768,3072]{2,1,0:T(8,128)(2,1)S(1)} %bitcast.14), custom_call_target="tpu_custom_call" | custom-call | flops 905969664 | bytes 7077888 | tf_op jit(solution)/shard_map/project/pallas_call | solution.py:175
  65.9 0.8 %collective-permute-done.10.refs_3_ = bf16[400,384]{1,0:T(8,128)(2,1)S(1)} collective-permute-done((bf16[400,384]{1,0:T(8,128)(2,1)S(1)}, bf16[400,384]{1,0:T(8,128)(2,1)S(1)}, u32[]{:S(2)}, u32[]{:S(2)}) %collective-permute-start.10) | collective-permute-done | bytes 307232 | tf_op jit(solution)/shard_map/ppermute | solution.py:241
  66.7 1.1 %join.3 = (bf16[192,384]{1,0:T(8,128)(2,1)S(1)}, bf16[192,384]{1,0:T(8,128)(2,1)S(1)}) custom-call(f32[400,384]{1,0:T(8,128)S(1)} %attend.10.refs_0_, f32[400,384]{1,0:T(8,128)S(1)} %attend.14.refs_1_, bf16[400,384]{1,0:T(8,128)(2,1)S(1)} %collective-permute-done.5.refs_2_, bf16[400,384]{1,0:T(8,128)(2,1)S(1)} %collective-permute-done.10.refs_3_), custom_call_target="tpu_custom_call" | custom-call | flops 1179648 | bytes 1474560 | tf_op jit(solution)/shard_map/join/pallas_call | solution.py:143
  67.7 1.4 %collective-permute-start.11 = (bf16[192,384]{1,0:T(8,128)(2,1)S(1)}, bf16[192,384]{1,0:T(8,128)(2,1)S(1)}, u32[]{:S(2)}, u32[]{:S(2)}) collective-permute-start(bf16[192,384]{1,0:T(8,128)(2,1)S(1)} %get-tuple-element.43), channel_id=1, source_target_pairs={{0,1},{1,0},{2,3},{3,2},{4,5},{5,4},{6,7},{7,6},{8,9},{9,8},{10,11... | collective-permute-start | bytes 442376 | tf_op jit(solution)/shard_map/ppermute | solution.py:260
  69.1 0.8 %project.4.refs_2_ = f32[192,3072]{1,0:T(8,128)S(1)} custom-call(bf16[192,384]{1,0:T(8,128)(2,1)S(1)} %get-tuple-element.44.refs_0_, bf16[2,768,3072]{2,1,0:T(8,128)(2,1)S(1)} %bitcast.15, f32[192,3072]{1,0:T(8,128)S(1)} %project.3.refs_2_), custom_call_target="tpu_custom_call" | custom-call | flops 452984832 | bytes 4718592 | tf_op jit(solution)/shard_map/project/pallas_call | solution.py:175
  69.9 0.2 collective-permute-done.11.refs_0_
  70.1 1.8 %project.5 = bf16[192,3072]{1,0:T(8,128)(2,1)} custom-call(bf16[192,384]{1,0:T(8,128)(2,1)S(1)} %collective-permute-done.11.refs_0_, bf16[2,768,3072]{2,1,0:T(8,128)(2,1)S(1)} %bitcast.16, f32[192,3072]{1,0:T(8,128)S(1)} %project.4.refs_2_), custom_call_target="tpu_custom_call" | custom-call | flops 452984832 | bytes 4718592 | tf_op jit(solution)/shard_map/project/pallas_call | solution.py:175
  (10 shorter events, 0.1 us)
Async XLA Ops:
  0.0 2.3 %copy-start.1 = (bf16[1,384,768]{2,1,0:T(8,128)(2,1)S(1)}, bf16[1,384,768]{2,1,0:T(8,128)(2,1)}, u32[]{:S(2)}) copy-start(bf16[1,384,768]{2,1,0:T(8,128)(2,1)} %param.6) | copy-start | bytes 1769476
  0.0 2.4 %copy-start.2 = (bf16[1,384,768]{2,1,0:T(8,128)(2,1)S(1)}, bf16[1,384,768]{2,1,0:T(8,128)(2,1)}, u32[]{:S(2)}) copy-start(bf16[1,384,768]{2,1,0:T(8,128)(2,1)} %param.5) | copy-start | bytes 1769476
  0.0 1.6 %copy-start = (bf16[1,384,768]{2,1,0:T(8,128)(2,1)S(1)}, bf16[1,384,768]{2,1,0:T(8,128)(2,1)}, u32[]{:S(2)}) copy-start(bf16[1,384,768]{2,1,0:T(8,128)(2,1)} %param.4) | copy-start | bytes 1769476
  1.3 14.3 %collective-permute-start.1 = (bf16[2,384,384]{2,1,0:T(8,128)(2,1)S(1)}, bf16[2,384,384]{2,1,0:T(8,128)(2,1)S(1)}, u32[]{:S(2)}, u32[]{:S(2)}) collective-permute-start(bf16[2,384,384]{2,1,0:T(8,128)(2,1)S(1)} %pad_maximum_fusion.refs_0_), channel_id=1, source_target_pairs={{0,2},{1,3},{2,0},{3,1},{4,6},{5,7},{6,4},{7,5},{8,10},{9,11},{10,... | collective-permute-start | bytes 1769480 | tf_op jit(solution)/shard_map/ppermute | solution.py:228
  1.6 22.7 %collective-permute-start = (bf16[384,768]{1,0:T(8,128)(2,1)S(1)}, bf16[384,768]{1,0:T(8,128)(2,1)S(1)}, u32[]{:S(2)}, u32[]{:S(2)}) collective-permute-start(bf16[384,768]{1,0:T(8,128)(2,1)S(1)} %bitcast.17), channel_id=1, source_target_pairs={{0,8},{1,9},{6,14},{7,15},{8,0},{9,1},{14,6},{15,7},{16,24},{17,25... | collective-permute-start | bytes 1769480 | tf_op jit(solution)/shard_map/ppermute | solution.py:227
  2.4 62.1 %slice-start = ((s8[9437184]{0:T(1024)(128)(4,1)}), s8[4194304]{0:T(1024)(128)(4,1)S(1)}, s32[]{:S(2)}) async-start(s8[9437184]{0:T(1024)(128)(4,1)} %bitcast.12), calls=%async_computation | async-start | bytes 8388608
  2.5 32.0 %collective-permute-start.2 = (bf16[2,384,384]{2,1,0:T(8,128)(2,1)S(1)}, bf16[2,384,384]{2,1,0:T(8,128)(2,1)S(1)}, u32[]{:S(2)}, u32[]{:S(2)}) collective-permute-start(bf16[2,384,384]{2,1,0:T(8,128)(2,1)S(1)} %pad_maximum_fusion.1.refs_0_), channel_id=1, source_target_pairs={{0,2},{1,3},{2,0},{3,1},{4,6},{5,7},{6,4},{7,5},{8,10},{9,11},{10,... | collective-permute-start | bytes 1769480 | tf_op jit(solution)/shard_map/ppermute | solution.py:229
  15.6 23.8 %collective-permute-start.3 = (bf16[384,768]{1,0:T(8,128)(2,1)S(1)}, bf16[384,768]{1,0:T(8,128)(2,1)S(1)}, u32[]{:S(2)}, u32[]{:S(2)}) collective-permute-start(bf16[384,768]{1,0:T(8,128)(2,1)S(1)} %bitcast.18), channel_id=1, source_target_pairs={{2,10},{3,11},{4,12},{5,13},{10,2},{11,3},{12,4},{13,5},{18,26},{1... | collective-permute-start | bytes 1769480 | tf_op jit(solution)/shard_map/ppermute | solution.py:231
  19.8 26.5 %collective-permute-start.4 = (bf16[2,384,384]{2,1,0:T(8,128)(2,1)S(1)}, bf16[2,384,384]{2,1,0:T(8,128)(2,1)S(1)}, u32[]{:S(2)}, u32[]{:S(2)}) collective-permute-start(bf16[2,384,384]{2,1,0:T(8,128)(2,1)S(1)} %collective-permute-done.1.refs_1_), channel_id=1, source_target_pairs={{0,4},{1,5},{6,2},{7,3},{8,12},{9,13},{14,10},{15,11},{16,20},{17,... | collective-permute-start | bytes 1769480 | tf_op jit(solution)/shard_map/ppermute | solution.py:232
  21.2 29.7 %collective-permute-start.6 = (bf16[2,384,384]{2,1,0:T(8,128)(2,1)S(1)}, bf16[2,384,384]{2,1,0:T(8,128)(2,1)S(1)}, u32[]{:S(2)}, u32[]{:S(2)}) collective-permute-start(bf16[2,384,384]{2,1,0:T(8,128)(2,1)S(1)} %pad_maximum_fusion.1.refs_0_), channel_id=1, source_target_pairs={{2,4},{3,5},{4,2},{5,3},{10,12},{11,13},{12,10},{13,11},{18,20},{1... | collective-permute-start | bytes 1769480 | tf_op jit(solution)/shard_map/ppermute | solution.py:233
  24.4 34.9 %collective-permute-start.7 = (bf16[400,384]{1,0:T(8,128)(2,1)S(1)}, bf16[400,384]{1,0:T(8,128)(2,1)S(1)}, u32[]{:S(2)}, u32[]{:S(2)}) collective-permute-start(bf16[400,384]{1,0:T(8,128)(2,1)S(1)} %attend.8), channel_id=1, source_target_pairs={{8,0},{9,1},{14,6},{15,7},{0,8},{1,9},{6,14},{7,15},{24,16},{25,17... | collective-permute-start | bytes 921608 | tf_op jit(solution)/shard_map/ppermute | solution.py:241
  34.5 16.4 %collective-permute-start.5 = (bf16[400,384]{1,0:T(8,128)(2,1)S(1)}, bf16[400,384]{1,0:T(8,128)(2,1)S(1)}, u32[]{:S(2)}, u32[]{:S(2)}) collective-permute-start(bf16[400,384]{1,0:T(8,128)(2,1)S(1)} %attend.9), channel_id=1, source_target_pairs={{8,0},{9,1},{14,6},{15,7},{0,8},{1,9},{6,14},{7,15},{24,16},{25,17... | collective-permute-start | bytes 921608 | tf_op jit(solution)/shard_map/ppermute | solution.py:241
  35.2 29.3 %slice-start.1 = ((s8[9437184]{0:T(1024)(128)(4,1)}), s8[4194304]{0:T(1024)(128)(4,1)S(1)}, s32[]{:S(2)}) async-start(s8[9437184]{0:T(1024)(128)(4,1)} %bitcast.12), calls=%async_computation.1 | async-start | bytes 8388608
  39.5 25.0 %slice-start.2 = ((s8[9437184]{0:T(1024)(128)(4,1)}), s8[1048576]{0:T(1024)(128)(4,1)S(1)}, s32[]{:S(2)}) async-start(s8[9437184]{0:T(1024)(128)(4,1)} %bitcast.12), calls=%async_computation.2 | async-start | bytes 2097152
  48.9 11.7 %collective-permute-start.8 = (bf16[400,384]{1,0:T(8,128)(2,1)S(1)}, bf16[400,384]{1,0:T(8,128)(2,1)S(1)}, u32[]{:S(2)}, u32[]{:S(2)}) collective-permute-start(bf16[400,384]{1,0:T(8,128)(2,1)S(1)} %attend.12), channel_id=1, source_target_pairs={{10,2},{11,3},{12,4},{13,5},{2,10},{3,11},{4,12},{5,13},{26,18},{2... | collective-permute-start | bytes 921608 | tf_op jit(solution)/shard_map/ppermute | solution.py:241
  53.7 12.9 %collective-permute-start.10 = (bf16[400,384]{1,0:T(8,128)(2,1)S(1)}, bf16[400,384]{1,0:T(8,128)(2,1)S(1)}, u32[]{:S(2)}, u32[]{:S(2)}) collective-permute-start(bf16[400,384]{1,0:T(8,128)(2,1)S(1)} %attend.13), channel_id=1, source_target_pairs={{10,2},{11,3},{12,4},{13,5},{2,10},{3,11},{4,12},{5,13},{26,18},{2... | collective-permute-start | bytes 921608 | tf_op jit(solution)/shard_map/ppermute | solution.py:241
  61.7 2.7 %collective-permute-start.9 = (bf16[192,384]{1,0:T(8,128)(2,1)S(1)}, bf16[192,384]{1,0:T(8,128)(2,1)S(1)}, u32[]{:S(2)}, u32[]{:S(2)}) collective-permute-start(bf16[192,384]{1,0:T(8,128)(2,1)S(1)} %get-tuple-element.40), channel_id=1, source_target_pairs={{0,1},{1,0},{2,3},{3,2},{4,5},{5,4},{6,7},{7,6},{8,9},{9,8},{10,11... | collective-permute-start | bytes 442376 | tf_op jit(solution)/shard_map/ppermute | solution.py:260
  67.7 2.4 %collective-permute-start.11 = (bf16[192,384]{1,0:T(8,128)(2,1)S(1)}, bf16[192,384]{1,0:T(8,128)(2,1)S(1)}, u32[]{:S(2)}, u32[]{:S(2)}) collective-permute-start(bf16[192,384]{1,0:T(8,128)(2,1)S(1)} %get-tuple-element.43), channel_id=1, source_target_pairs={{0,1},{1,0},{2,3},{3,2},{4,5},{5,4},{6,7},{7,6},{8,9},{9,8},{10,11... | collective-permute-start | bytes 442376 | tf_op jit(solution)/shard_map/ppermute | solution.py:260

commit v4 on v3

--- a/solution.py
+++ b/solution.py
@@ -12,6 +12,7 @@
 HD = 128
 CHUNK_HEADS = 2
 STAT_ROWS = 16
+PROJECT_COLS = 512
 EXP2_SCALE = HD ** (-0.5) * math.log2(math.e)
 MASKED = -1e30
 VMEM_BYTES = 32 * 1024 * 1024
@@ -34,23 +35,31 @@
     return (col == 0) | (col == TCOLS - 1)
 
 
-def attend_tiles(q_ref, tiles, out_ref):
-    rows, width = q_ref.shape
+def attend_head(q_ref, tiles, cols):
+    query = q_ref[:, cols]
+    scores = [dot_rows(tile[0, :, cols], query) for tile in tiles]
+    top = jnp.max(functools.reduce(jnp.maximum, scores), axis=0, keepdims=True)
+    top = top.astype(jnp.bfloat16).astype(jnp.float32)
+    total = jnp.zeros_like(top)
+    out = jnp.zeros((HD, query.shape[0]), jnp.float32)
+    for score, tile in zip(scores, tiles):
+        probs = jnp.exp2((score - top) * EXP2_SCALE).astype(jnp.bfloat16)
+        total += jnp.sum(probs.astype(jnp.float32), axis=0, keepdims=True)
+        out += lax.dot_general(
+            tile[1, :, cols], probs, (((0,), (0,)), ((), ())), preferred_element_type=jnp.float32
+        )
+    return top, total, out
+
+
+def head_columns(width):
+    return [slice(first, first + HD) for first in range(0, width, HD)]
+
+
+def put_partial(heads, out_ref):
+    width = out_ref.shape[1]
+    rows = heads[0][0].shape[1]
     stats = []
-    for head in range(width // HD):
-        cols = slice(head * HD, (head + 1) * HD)
-        query = q_ref[:, cols]
-        scores = [dot_rows(tile[0, :, cols], query) for tile in tiles]
-        top = jnp.max(functools.reduce(jnp.maximum, scores), axis=0, keepdims=True)
-        top = top.astype(jnp.bfloat16).astype(jnp.float32)
-        total = jnp.zeros((1, rows), jnp.float32)
-        out = jnp.zeros((HD, rows), jnp.float32)
-        for score, tile in zip(scores, tiles):
-            probs = jnp.exp2((score - top) * EXP2_SCALE).astype(jnp.bfloat16)
-            total += jnp.sum(probs.astype(jnp.float32), axis=0, keepdims=True)
-            out += lax.dot_general(
-                tile[1, :, cols], probs, (((0,), (0,)), ((), ())), preferred_element_type=jnp.float32
-            )
+    for cols, (top, total, out) in zip(head_columns(width), heads):
         high = total.astype(jnp.bfloat16).astype(jnp.float32)
         stats += [top, high, total - high]
         out_ref[:rows, cols] = out.T.astype(out_ref.dtype)
@@ -66,31 +75,90 @@
         out_ref[first : first + STAT_ROWS, :] = piece.astype(out_ref.dtype)
 
 
-def attend_kernel(edges, inners, q_ref, *refs):
-    tiles, out_ref = refs[:-1], refs[-1]
-    edge = is_edge()
-    if edges and inners:
-        attend_tiles(q_ref, tiles, out_ref)
-    elif edges:
-        pl.when(edge)(lambda: attend_tiles(q_ref, tiles, out_ref))
+def edge_kernel(q_ref, own_ref, next_ref, out_ref):
+    @pl.when(is_edge())
+    def _():
+        columns = head_columns(q_ref.shape[1])
+        put_partial([attend_head(q_ref, (own_ref, next_ref), cols) for cols in columns], out_ref)
+
+
+def near_kernel(everywhere, q_ref, own_ref, next_ref, state_ref):
+    def attend():
+        rows, width = q_ref.shape
+        stats = []
+        for cols in head_columns(width):
+            top, total, out = attend_head(q_ref, (own_ref, next_ref), cols)
+            state_ref[cols, :] = out
+            stats += [top, total]
+        stats.append(jnp.zeros((STAT_ROWS - len(stats), rows), jnp.float32))
+        state_ref[width:, :] = jnp.concatenate(stats, axis=0)
+
+    if everywhere:
+        attend()
     else:
-        pl.when(jnp.logical_not(edge))(lambda: attend_tiles(q_ref, tiles, out_ref))
-
-
-def attend(query, tiles, edges, inners, dtype, weight=1.0):
-    rows, width = query.shape
-    keys = len(tiles) * rows
+        pl.when(jnp.logical_not(is_edge()))(attend)
+
+
+def finish_kernel(everywhere, q_ref, far_ref, state_ref, out_ref):
+    width = q_ref.shape[1]
+
+    def held():
+        stats = state_ref[width:, :]
+        return [
+            (stats[2 * n : 2 * n + 1], stats[2 * n + 1 : 2 * n + 2], state_ref[cols, :])
+            for n, cols in enumerate(head_columns(width))
+        ]
+
+    @pl.when(jnp.logical_not(is_edge()))
+    def _():
+        heads = []
+        for cols, (top_0, total_0, out_0) in zip(head_columns(width), held()):
+            top_1, total_1, out_1 = attend_head(q_ref, (far_ref,), cols)
+            top = jnp.maximum(top_0, top_1)
+            weight_0 = jnp.exp2((top_0 - top) * EXP2_SCALE)
+            weight_1 = jnp.exp2((top_1 - top) * EXP2_SCALE)
+            total = weight_0 * total_0 + weight_1 * total_1
+            heads.append((top, total, weight_0 * out_0 + weight_1 * out_1))
+        put_partial(heads, out_ref)
+
+    if everywhere:
+        pl.when(is_edge())(lambda: put_partial(held(), out_ref))
+
+
+def partial_call(kernel, name, out_shape, dtype, tiles, weight, *args):
+    rows, width = args[0].shape
+    keys = tiles * rows
     return pl.pallas_call(
-        functools.partial(attend_kernel, edges, inners),
-        out_shape=jax.ShapeDtypeStruct((rows + STAT_ROWS * stat_blocks(rows, width), width), dtype),
+        kernel,
+        out_shape=jax.ShapeDtypeStruct(out_shape, dtype),
         compiler_params=pltpu.CompilerParams(vmem_limit_bytes=VMEM_BYTES),
         cost_estimate=pl.CostEstimate(
             flops=int(weight * 4 * rows * keys * width),
             bytes_accessed=int(weight * 2 * width * (2 * rows + 2 * keys)),
             transcendentals=int(weight * rows * keys * width // HD),
         ),
-        name="attend",
-    )(query, *tiles)
+        name=name,
+    )(*args)
+
+
+def partial_shape(query):
+    rows, width = query.shape
+    return rows + STAT_ROWS * stat_blocks(rows, width), width
+
+
+def attend_edge(query, own, nxt):
+    return partial_call(edge_kernel, "edge", partial_shape(query), jnp.bfloat16, 2, 1.0, query, own, nxt)
+
+
+def attend_near(query, own, nxt, everywhere):
+    rows, width = query.shape
+    kernel = functools.partial(near_kernel, everywhere)
+    return partial_call(kernel, "near", (width + STAT_ROWS, rows), jnp.float32, 2, 0.01, query, own, nxt)
+
+
+def attend_far(query, far, state, everywhere, dtype):
+    kernel = functools.partial(finish_kernel, everywhere)
+    return partial_call(kernel, "far", partial_shape(query), dtype, 1, 1.0, query, far, state)
 
 
 def join_kernel(steps, time_count, *refs):
@@ -104,17 +172,14 @@
 
     def load(ref, *index):
         at_edge, inner = ref
-        inner = inner[index].astype(jnp.float32)
-        return jnp.where(edge, 0.0 if at_edge is None else at_edge[index].astype(jnp.float32), inner)
-
-    near, far = refs[:2]
-    sources = [(near, near), (None, far)] + [refs[2 + 2 * n : 4 + 2 * n] for n in range(len(steps))]
+        value = at_edge[index].astype(jnp.float32)
+        return value if inner is None else jnp.where(edge, value, inner[index].astype(jnp.float32))
+
+    sources = [(refs[0], None)] + [refs[1 + 2 * n : 3 + 2 * n] for n in range(len(steps))]
     parts = []
-    for ref, step in zip(sources, (0, 0, *steps)):
+    for ref, step in zip(sources, (0, *steps)):
         source = time_tile + step
         ok = None if step == 0 or time_count == 2 else (source >= 0) & (source < time_count)
-        if ref[0] is None:
-            ok = jnp.logical_not(edge)
         stats = [
             load(ref, slice(rows + block * STAT_ROWS, rows + (block + 1) * STAT_ROWS), slice(None))
             for block in range(stat_blocks(rows, width))
@@ -151,12 +216,14 @@
     )(*parts)
 
 
-def project_kernel(first, swaps, has_total, *refs):
-    inputs, w_ref, out_ref = refs[: len(swaps)], refs[len(swaps)], refs[-1]
+def project_kernel(first, swaps, has_total, last, *refs):
+    inputs, w_ref = refs[: len(swaps)], refs[len(swaps)]
+    out_ref = refs[-2] if last else refs[-1]
+    copies = []
     group = lax.axis_index("tm") % 2
     width = inputs[0].shape[1]
     model = w_ref.shape[2]
-    block = 512 if model % 512 == 0 else model
+    block = PROJECT_COLS if model % PROJECT_COLS == 0 else model
     for start in range(0, model, block):
         cols = slice(start, start + block)
         result = refs[len(swaps) + 1][:, cols] if has_total else 0.0
@@ -166,17 +233,26 @@
                 ref[...], w_ref[which, first : first + width, cols], preferred_element_type=jnp.float32
             )
         out_ref[:, cols] = result.astype(out_ref.dtype)
-
-
-def project(inputs, swaps, weight, first, total, dtype):
+        if last:
+            home = refs[-3].at[:, cols]
+            copies.append(pltpu.make_async_copy(out_ref.at[:, cols], home, refs[-1].at[len(copies)]))
+            copies[-1].start()
+    for copy in copies:
+        copy.wait()
+
+
+def project(inputs, swaps, weight, first, total, last):
     half, width = inputs[0].shape
     model = weight.shape[2]
     args = [*inputs, weight] if total is None else [*inputs, weight, total]
+    dtype = jnp.bfloat16 if last else jnp.float32
+    scratch = [pltpu.VMEM((half, model), dtype), pltpu.SemaphoreType.DMA((-(-model // PROJECT_COLS),))]
     return pl.pallas_call(
-        functools.partial(project_kernel, first, swaps, total is not None),
+        functools.partial(project_kernel, first, swaps, total is not None, last),
         in_specs=[pl.BlockSpec(memory_space=pltpu.VMEM)] * len(args),
-        out_specs=pl.BlockSpec(memory_space=pltpu.VMEM),
+        out_specs=pl.BlockSpec(memory_space=pl.ANY if last else pltpu.VMEM),
         out_shape=jax.ShapeDtypeStruct((half, model), dtype),
+        scratch_shapes=scratch if last else [],
         compiler_params=pltpu.CompilerParams(vmem_limit_bytes=VMEM_BYTES),
         cost_estimate=pl.CostEstimate(
             flops=2 * len(inputs) * half * width * model,
@@ -231,39 +307,43 @@
     inner_asks = [lax.ppermute(inner_query, "tm", route) for route in inner_routes]
     far_0 = lax.ppermute(next_0, "tm", far_route)
     far_1 = lax.ppermute(after(own_1, next_0), "tm", across_route)
-    tiles = (own_0, next_0, far_0), (own_1, next_1, far_1)
-
-    def answer(asks, chunk, edges, earlier):
-        near = tiles[chunk][:2] if edges else tiles[chunk]
-        return [attend(after(q[:, cuts[chunk]], *earlier), near, edges, not edges, jnp.bfloat16) for q in asks]
+    nears = (own_0, next_0), (own_1, next_1)
 
     def back(parts, routes):
         return [lax.ppermute(part, "tm", reverse(route)) for part, route in zip(parts, routes)]
 
-    edge_0 = answer(edge_asks, 0, True, ())
+    edge_0 = [attend_edge(q[:, cuts[0]], *nears[0]) for q in edge_asks]
     edge_back_0 = back(edge_0, edge_routes)
-    edge_1 = answer(edge_asks, 1, True, edge_0)
+    own_states = [attend_near(after(q_parts[0], *edge_0), *nears[0], True)]
+    edge_1 = [attend_edge(after(q[:, cuts[1]], *edge_0, *own_states), *nears[1]) for q in edge_asks]
     edge_back_1 = back(edge_1, edge_routes)
-    nears = [
-        attend(after(q_parts[c], *edge_1), tiles[c][:2], True, True, jnp.float32, weight=0.01)
-        for c in range(2)
+
+    asked_0 = [after(q[:, cuts[0]], *own_states) for q in inner_asks]
+    states_0 = [attend_near(q, *nears[0], False) for q in asked_0]
+    asked_1 = [after(q[:, cuts[1]], *states_0) for q in inner_asks]
+    states_1 = [attend_near(q, *nears[1], False) for q in asked_1]
+    states_0 = [after(state, *states_1) for state in states_0]
+    inner_0 = [attend_far(q, far_0, state, False, jnp.bfloat16) for q, state in zip(asked_0, states_0)]
+    inner_back_0 = back(inner_0, inner_routes)
+    states_1 = [after(state, *inner_0, *edge_back_1) for state in states_1]
+    inner_1 = [attend_far(q, far_1, state, False, jnp.bfloat16) for q, state in zip(asked_1, states_1)]
+    inner_back_1 = back(inner_1, inner_routes)
+    own_states.append(attend_near(after(q_parts[1], *inner_1), *nears[1], True))
+    owns = [
+        attend_far(after(q_parts[c], *inner_1), far, own_states[c], True, jnp.float32)
+        for c, far in enumerate((far_0, far_1))
     ]
-    inner_0 = answer(inner_asks, 0, False, nears)
-    inner_back_0 = back(inner_0, inner_routes)
-    inner_1 = answer(inner_asks, 1, False, (*inner_0, *edge_back_1))
-    inner_back_1 = back(inner_1, inner_routes)
-    fars = [attend(after(q_parts[c], *inner_1), tiles[c][2:], False, True, jnp.float32) for c in range(2)]
 
     def joined(chunk, edge_back, inner_back, earlier):
         backs = [after(part, earlier) for pair in zip(edge_back, inner_back) for part in pair]
-        mine, other = join((nears[chunk], fars[chunk], *backs), rows, steps, time_count)
+        mine, other = join((owns[chunk], *backs), rows, steps, time_count)
         return mine, lax.ppermute(other, "tm", core_route)
 
-    mine, other = joined(0, edge_back_0, inner_back_0, fars[1])
-    total = project((mine, other), (False, True), weight, 0, None, jnp.float32)
+    mine, other = joined(0, edge_back_0, inner_back_0, owns[1])
+    total = project((mine, other), (False, True), weight, 0, None, False)
     mine, other = joined(1, edge_back_1, inner_back_1, total)
-    total = project((mine,), (False,), weight, middle, total, jnp.float32)
-    return project((other,), (True,), weight, middle, total, jnp.bfloat16)
+    total = project((mine,), (False,), weight, middle, total, False)
+    return project((other,), (True,), weight, middle, total, True)
 
 
 def solution(mesh):

time: 72.7 us -> 70.4 us (0.968)
  waiting for transfers between devices: 26.4 us -> 24.8 us
    ppermute x1, waiting for transfers between devices: 9.35 us -> 7.32 us  [per_device(): next_1 = lax.ppermute(own_1, 'tm', next_route)]
    pallas_call x8 -> x10, Pallas kernels: 12.4 us -> 13.6 us  [partial_call(): pl.pallas_call(kernel, out_shape=jax.ShapeDtypeStruct(out_shape, dtype),...]
  transfers between devices with their start and end apart: 12 -> 12, of which waited for: 6 -> 6; matrix products, arithmetic and copies ran while one was open for 0% -> 0% of each run, Pallas kernels for 22% -> 24%
where the time goes in v4:
time: 70.4 us; the launch traced here: 70.1 us
  waiting for transfers between devices  24.8 us (35%)
  starting transfers between devices  24.5 us (35%)
  Pallas kernels  18.7 us (27%)
  local copies, waits for them, and re-layouts  1.52 us (2%)
    pallas_call x10, Pallas kernels, partial_call(): pl.pallas_call(kernel, out_shape=jax.ShapeDtypeStruct(out_shape, dtype),...  13.6 us
    ppermute x1, waiting for transfers between devices, per_device(): next_0 = lax.ppermute(own_0, 'tm', next_route)  8.27 us
    ppermute x4, starting transfers between devices, back(): lax.ppermute(part, 'tm', reverse(route))  7.53 us
    ppermute x1, waiting for transfers between devices, per_device(): next_1 = lax.ppermute(own_1, 'tm', next_route)  7.32 us
    ppermute x1, waiting for transfers between devices, per_device(): far_0 = lax.ppermute(next_0, 'tm', far_route)  6.93 us
    ppermute x1, starting transfers between devices, per_device(): next_1 = lax.ppermute(own_1, 'tm', next_route)  4.82 us
    ppermute x1, starting transfers between devices, per_device(): lax.ppermute(inner_query, 'tm', route)  4.21 us
    pallas_call x3, Pallas kernels, project(): pl.pallas_call(functools.partial(project_kernel, first, swaps, total is n...  3.71 us
  transfers between devices with their start and end apart: 12, of which 6 were waited for; matrix products, arithmetic and copies ran while one was open for 0% of the time, Pallas kernels for 24%

profile of v4, /device:TPU:7, one launch (start us, length us, event | category | flops | bytes accessed | tf_op | source)
XLA Modules:
  0.0 70.1 jit_solution(2589290610518778056)
XLA Ops:
  0.0 1.2 %slice_bitcast_fusion = (bf16[1,384,384]{2,1,0:T(8,128)(2,1)S(1)}, bf16[1,384,384]{2,1,0:T(8,128)(2,1)S(1)}) fusion(bf16[384,768]{1,0:T(8,128)(2,1)} %bitcast.20, bf16[384,768]{1,0:T(8,128)(2,1)} %bitcast.22), kind=kLoop, calls=%fused_computation.2 | loop fusion | bytes 1179648 | tf_op jit(solution)/shard_map/stack | solution.py:298
  1.3 0.1 pad_maximum_fusion.own_ref
  1.3 0.3 collective-permute-start
  1.6 0.0 copy-done
  1.6 0.7 collective-permute-start.2
  2.4 0.1 pad_maximum_fusion.1.own_ref
  2.5 4.8 %collective-permute-start.4 = (bf16[2,384,384]{2,1,0:T(8,128)(2,1)S(1)}, bf16[2,384,384]{2,1,0:T(8,128)(2,1)S(1)}, u32[]{:S(2)}, u32[]{:S(2)}) collective-permute-start(bf16[2,384,384]{2,1,0:T(8,128)(2,1)S(1)} %pad_maximum_fusion.1.own_ref), channel_id=1, source_target_pairs={{0,2},{1,3},{2,0},{3,1},{4,6},{5,7},{6,4},{7,5},{8,10},{9,11},{10,... | collective-permute-start | bytes 1769480 | tf_op jit(solution)/shard_map/ppermute | solution.py:305
  7.3 8.3 %collective-permute-done.next_ref = bf16[2,384,384]{2,1,0:T(8,128)(2,1)S(1)} collective-permute-done((bf16[2,384,384]{2,1,0:T(8,128)(2,1)S(1)}, bf16[2,384,384]{2,1,0:T(8,128)(2,1)S(1)}, u32[]{:S(2)}, u32[]{:S(2)}) %collective-permute-start) | collective-permute-done | bytes 589856 | tf_op jit(solution)/shard_map/ppermute | solution.py:304
  15.6 4.2 %collective-permute-start.1 = (bf16[384,768]{1,0:T(8,128)(2,1)S(1)}, bf16[384,768]{1,0:T(8,128)(2,1)S(1)}, u32[]{:S(2)}, u32[]{:S(2)}) collective-permute-start(bf16[384,768]{1,0:T(8,128)(2,1)S(1)} %bitcast.18), channel_id=1, source_target_pairs={{2,10},{3,11},{4,12},{5,13},{10,2},{11,3},{12,4},{13,5},{18,26},{1... | collective-permute-start | bytes 1769480 | tf_op jit(solution)/shard_map/ppermute | solution.py:307
  19.8 1.3 %collective-permute-start.5 = (bf16[2,384,384]{2,1,0:T(8,128)(2,1)S(1)}, bf16[2,384,384]{2,1,0:T(8,128)(2,1)S(1)}, u32[]{:S(2)}, u32[]{:S(2)}) collective-permute-start(bf16[2,384,384]{2,1,0:T(8,128)(2,1)S(1)} %collective-permute-done.next_ref), channel_id=1, source_target_pairs={{0,4},{1,5},{6,2},{7,3},{8,12},{9,13},{14,10},{15,11},{16,20},{17,... | collective-permute-start | bytes 1769480 | tf_op jit(solution)/shard_map/ppermute | solution.py:308
  21.1 0.1 fusion.1
  21.2 3.1 %collective-permute-start.3 = (bf16[2,384,384]{2,1,0:T(8,128)(2,1)S(1)}, bf16[2,384,384]{2,1,0:T(8,128)(2,1)S(1)}, u32[]{:S(2)}, u32[]{:S(2)}) collective-permute-start(bf16[2,384,384]{2,1,0:T(8,128)(2,1)S(1)} %pad_maximum_fusion.1.own_ref), channel_id=1, source_target_pairs={{2,4},{3,5},{4,2},{5,3},{10,12},{11,13},{12,10},{13,11},{18,20},{1... | collective-permute-start | bytes 1769480 | tf_op jit(solution)/shard_map/ppermute | solution.py:309
  24.3 0.0 collective-permute-done.2
  24.3 0.1 fusion
  24.4 0.7 collective-permute-start.7
  25.1 0.0 slice-start
  25.1 2.0 %near.4.state_ref = f32[400,384]{1,0:T(8,128)S(1)} custom-call(bf16[384,384]{1,0:T(8,128)(2,1)S(1)} %get-tuple-element.38.q_ref, bf16[2,384,384]{2,1,0:T(8,128)(2,1)S(1)} %pad_maximum_fusion.own_ref, bf16[2,384,384]{2,1,0:T(8,128)(2,1)S(1)} %collective-permute-done.next_ref), custom_call_target="tpu_custom_call" | custom-call | flops 4529848 | bytes 17694 | tf_op jit(solution)/shard_map/near/pallas_call | solution.py:131
  27.2 7.3 %collective-permute-done.4.next_ref = bf16[2,384,384]{2,1,0:T(8,128)(2,1)S(1)} collective-permute-done((bf16[2,384,384]{2,1,0:T(8,128)(2,1)S(1)}, bf16[2,384,384]{2,1,0:T(8,128)(2,1)S(1)}, u32[]{:S(2)}, u32[]{:S(2)}) %collective-permute-start.4) | collective-permute-done | bytes 589856 | tf_op jit(solution)/shard_map/ppermute | solution.py:305
  34.5 0.7 collective-permute-start.6
  35.2 0.0 collective-permute-done.1
  35.2 0.1 fusion.2
  35.2 0.0 slice-start.1
  35.3 2.0 %near.5.state_ref = f32[400,384]{1,0:T(8,128)S(1)} custom-call(bf16[384,384]{1,0:T(8,128)(2,1)S(1)} %get-tuple-element.29.q_ref, bf16[2,384,384]{2,1,0:T(8,128)(2,1)S(1)} %pad_maximum_fusion.own_ref, bf16[2,384,384]{2,1,0:T(8,128)(2,1)S(1)} %collective-permute-done.next_ref), custom_call_target="tpu_custom_call" | custom-call | flops 4529848 | bytes 17694 | tf_op jit(solution)/shard_map/near/pallas_call | solution.py:131
  37.3 2.0 %near.6.state_ref = f32[400,384]{1,0:T(8,128)S(1)} custom-call(bf16[384,384]{1,0:T(8,128)(2,1)S(1)} %get-tuple-element.30.q_ref, bf16[2,384,384]{2,1,0:T(8,128)(2,1)S(1)} %pad_maximum_fusion.1.own_ref, bf16[2,384,384]{2,1,0:T(8,128)(2,1)S(1)} %collective-permute-done.4.next_ref), custom_call_target="tpu_custom_call" | custom-call | flops 4529848 | bytes 17694 | tf_op jit(solution)/shard_map/near/pallas_call | solution.py:131
  39.3 6.9 %collective-permute-done.5.far_ref = bf16[2,384,384]{2,1,0:T(8,128)(2,1)S(1)} collective-permute-done((bf16[2,384,384]{2,1,0:T(8,128)(2,1)S(1)}, bf16[2,384,384]{2,1,0:T(8,128)(2,1)S(1)}, u32[]{:S(2)}, u32[]{:S(2)}) %collective-permute-start.5) | collective-permute-done | bytes 589856 | tf_op jit(solution)/shard_map/ppermute | solution.py:308
  46.3 1.3 %far.4 = bf16[400,384]{1,0:T(8,128)(2,1)S(1)} custom-call(bf16[384,384]{1,0:T(8,128)(2,1)S(1)} %get-tuple-element.29.q_ref, bf16[2,384,384]{2,1,0:T(8,128)(2,1)S(1)} %collective-permute-done.5.far_ref, f32[400,384]{1,0:T(8,128)S(1)} %near.5.state_ref), custom_call_target="tpu_custom_call" | custom-call | flops 226492416 | bytes 1179648 | tf_op jit(solution)/shard_map/far/pallas_call | solution.py:131
  47.6 1.9 %collective-permute-start.8 = (bf16[400,384]{1,0:T(8,128)(2,1)S(1)}, bf16[400,384]{1,0:T(8,128)(2,1)S(1)}, u32[]{:S(2)}, u32[]{:S(2)}) collective-permute-start(bf16[400,384]{1,0:T(8,128)(2,1)S(1)} %far.4), channel_id=1, source_target_pairs={{10,2},{11,3},{12,4},{13,5},{2,10},{3,11},{4,12},{5,13},{26,18},{2... | collective-permute-start | bytes 921608 | tf_op jit(solution)/shard_map/ppermute | solution.py:313
  49.5 0.0 collective-permute-done.6.refs_1_
  49.5 0.0 collective-permute-done.3.far_ref
  49.5 1.5 %far.5 = bf16[400,384]{1,0:T(8,128)(2,1)S(1)} custom-call(bf16[384,384]{1,0:T(8,128)(2,1)S(1)} %get-tuple-element.30.q_ref, bf16[2,384,384]{2,1,0:T(8,128)(2,1)S(1)} %collective-permute-done.3.far_ref, f32[400,384]{1,0:T(8,128)S(1)} %near.6.state_ref), custom_call_target="tpu_custom_call" | custom-call | flops 226492416 | bytes 1179648 | tf_op jit(solution)/shard_map/far/pallas_call | solution.py:131
  51.0 4.3 %collective-permute-start.10 = (bf16[400,384]{1,0:T(8,128)(2,1)S(1)}, bf16[400,384]{1,0:T(8,128)(2,1)S(1)}, u32[]{:S(2)}, u32[]{:S(2)}) collective-permute-start(bf16[400,384]{1,0:T(8,128)(2,1)S(1)} %far.5), channel_id=1, source_target_pairs={{10,2},{11,3},{12,4},{13,5},{2,10},{3,11},{4,12},{5,13},{26,18},{2... | collective-permute-start | bytes 921608 | tf_op jit(solution)/shard_map/ppermute | solution.py:313
  55.3 0.0 slice-start.2
  55.3 2.0 %near.7.state_ref = f32[400,384]{1,0:T(8,128)S(1)} custom-call(bf16[384,384]{1,0:T(8,128)(2,1)S(1)} %get-tuple-element.37.q_ref, bf16[2,384,384]{2,1,0:T(8,128)(2,1)S(1)} %pad_maximum_fusion.1.own_ref, bf16[2,384,384]{2,1,0:T(8,128)(2,1)S(1)} %collective-permute-done.4.next_ref), custom_call_target="tpu_custom_call" | custom-call | flops 4529848 | bytes 17694 | tf_op jit(solution)/shard_map/near/pallas_call | solution.py:131
  57.3 1.4 %far.6.refs_0_ = f32[400,384]{1,0:T(8,128)S(1)} custom-call(bf16[384,384]{1,0:T(8,128)(2,1)S(1)} %get-tuple-element.37.q_ref, bf16[2,384,384]{2,1,0:T(8,128)(2,1)S(1)} %collective-permute-done.3.far_ref, f32[400,384]{1,0:T(8,128)S(1)} %near.7.state_ref), custom_call_target="tpu_custom_call" | custom-call | flops 226492416 | bytes 1179648 | tf_op jit(solution)/shard_map/far/pallas_call | solution.py:131
  58.7 0.0 collective-permute-done.7.refs_1_
  58.7 1.3 %far.7.refs_0_ = f32[400,384]{1,0:T(8,128)S(1)} custom-call(bf16[384,384]{1,0:T(8,128)(2,1)S(1)} %get-tuple-element.38.q_ref, bf16[2,384,384]{2,1,0:T(8,128)(2,1)S(1)} %collective-permute-done.5.far_ref, f32[400,384]{1,0:T(8,128)S(1)} %near.4.state_ref), custom_call_target="tpu_custom_call" | custom-call | flops 226492416 | bytes 1179648 | tf_op jit(solution)/shard_map/far/pallas_call | solution.py:131
  60.0 0.0 collective-permute-done.8.refs_2_
  60.0 0.7 %join.2 = (bf16[192,384]{1,0:T(8,128)(2,1)S(1)}, bf16[192,384]{1,0:T(8,128)(2,1)S(1)}) custom-call(f32[400,384]{1,0:T(8,128)S(1)} %far.7.refs_0_, bf16[400,384]{1,0:T(8,128)(2,1)S(1)} %collective-permute-done.7.refs_1_, bf16[400,384]{1,0:T(8,128)(2,1)S(1)} %collective-permute-done.8.refs_2_), custom_call_target="tpu_custom_call" | custom-call | flops 1179648 | bytes 1474560 | tf_op jit(solution)/shard_map/join/pallas_call | solution.py:208
  60.8 1.1 %collective-permute-start.9 = (bf16[192,384]{1,0:T(8,128)(2,1)S(1)}, bf16[192,384]{1,0:T(8,128)(2,1)S(1)}, u32[]{:S(2)}, u32[]{:S(2)}) collective-permute-start(bf16[192,384]{1,0:T(8,128)(2,1)S(1)} %get-tuple-element.42), channel_id=1, source_target_pairs={{0,1},{1,0},{2,3},{3,2},{4,5},{5,4},{6,7},{7,6},{8,9},{9,8},{10,11... | collective-permute-start | bytes 442376 | tf_op jit(solution)/shard_map/ppermute | solution.py:340
  61.9 1.0 %collective-permute-done.9.refs_1_ = bf16[192,384]{1,0:T(8,128)(2,1)S(1)} collective-permute-done((bf16[192,384]{1,0:T(8,128)(2,1)S(1)}, bf16[192,384]{1,0:T(8,128)(2,1)S(1)}, u32[]{:S(2)}, u32[]{:S(2)}) %collective-permute-start.9) | collective-permute-done | bytes 147488 | tf_op jit(solution)/shard_map/ppermute | solution.py:340
  62.9 0.0 slice-done.1
  62.9 1.4 %project.3.refs_2_ = f32[192,3072]{1,0:T(8,128)S(1)} custom-call(bf16[192,384]{1,0:T(8,128)(2,1)S(1)} %get-tuple-element.41.refs_0_, bf16[192,384]{1,0:T(8,128)(2,1)S(1)} %collective-permute-done.9.refs_1_, bf16[2,768,3072]{2,1,0:T(8,128)(2,1)S(1)} %bitcast.14), custom_call_target="tpu_custom_call" | custom-call | flops 905969664 | bytes 7077888 | tf_op jit(solution)/shard_map/project/pallas_call | solution.py:250
  64.3 1.0 %collective-permute-done.10.refs_2_ = bf16[400,384]{1,0:T(8,128)(2,1)S(1)} collective-permute-done((bf16[400,384]{1,0:T(8,128)(2,1)S(1)}, bf16[400,384]{1,0:T(8,128)(2,1)S(1)}, u32[]{:S(2)}, u32[]{:S(2)}) %collective-permute-start.10) | collective-permute-done | bytes 307232 | tf_op jit(solution)/shard_map/ppermute | solution.py:313
  65.3 0.7 %join.3 = (bf16[192,384]{1,0:T(8,128)(2,1)S(1)}, bf16[192,384]{1,0:T(8,128)(2,1)S(1)}) custom-call(f32[400,384]{1,0:T(8,128)S(1)} %far.6.refs_0_, bf16[400,384]{1,0:T(8,128)(2,1)S(1)} %collective-permute-done.6.refs_1_, bf16[400,384]{1,0:T(8,128)(2,1)S(1)} %collective-permute-done.10.refs_2_), custom_call_target="tpu_custom_call" | custom-call | flops 1179648 | bytes 1474560 | tf_op jit(solution)/shard_map/join/pallas_call | solution.py:208
  66.0 1.4 %collective-permute-start.11 = (bf16[192,384]{1,0:T(8,128)(2,1)S(1)}, bf16[192,384]{1,0:T(8,128)(2,1)S(1)}, u32[]{:S(2)}, u32[]{:S(2)}) collective-permute-start(bf16[192,384]{1,0:T(8,128)(2,1)S(1)} %get-tuple-element.45), channel_id=1, source_target_pairs={{0,1},{1,0},{2,3},{3,2},{4,5},{5,4},{6,7},{7,6},{8,9},{9,8},{10,11... | collective-permute-start | bytes 442376 | tf_op jit(solution)/shard_map/ppermute | solution.py:340
  67.4 0.8 %project.4.refs_2_ = f32[192,3072]{1,0:T(8,128)S(1)} custom-call(bf16[192,384]{1,0:T(8,128)(2,1)S(1)} %get-tuple-element.46.refs_0_, bf16[2,768,3072]{2,1,0:T(8,128)(2,1)S(1)} %bitcast.15, f32[192,3072]{1,0:T(8,128)S(1)} %project.3.refs_2_), custom_call_target="tpu_custom_call" | custom-call | flops 452984832 | bytes 4718592 | tf_op jit(solution)/shard_map/project/pallas_call | solution.py:250
  68.2 0.2 collective-permute-done.11.refs_0_
  68.4 1.5 %project.5 = bf16[192,3072]{1,0:T(8,128)(2,1)} custom-call(bf16[192,384]{1,0:T(8,128)(2,1)S(1)} %collective-permute-done.11.refs_0_, bf16[2,768,3072]{2,1,0:T(8,128)(2,1)S(1)} %bitcast.16, f32[192,3072]{1,0:T(8,128)S(1)} %project.4.refs_2_), custom_call_target="tpu_custom_call" | custom-call | flops 452984832 | bytes 4718592 | tf_op jit(solution)/shard_map/project/pallas_call | solution.py:250
  (12 shorter events, 0.1 us)
Async XLA Ops:
  0.0 2.4 %copy-start.2 = (bf16[1,384,768]{2,1,0:T(8,128)(2,1)S(1)}, bf16[1,384,768]{2,1,0:T(8,128)(2,1)}, u32[]{:S(2)}) copy-start(bf16[1,384,768]{2,1,0:T(8,128)(2,1)} %param.5) | copy-start | bytes 1769476
  0.0 2.3 %copy-start.1 = (bf16[1,384,768]{2,1,0:T(8,128)(2,1)S(1)}, bf16[1,384,768]{2,1,0:T(8,128)(2,1)}, u32[]{:S(2)}) copy-start(bf16[1,384,768]{2,1,0:T(8,128)(2,1)} %param.6) | copy-start | bytes 1769476
  0.0 1.6 %copy-start = (bf16[1,384,768]{2,1,0:T(8,128)(2,1)S(1)}, bf16[1,384,768]{2,1,0:T(8,128)(2,1)}, u32[]{:S(2)}) copy-start(bf16[1,384,768]{2,1,0:T(8,128)(2,1)} %param.4) | copy-start | bytes 1769476
  1.3 14.3 %collective-permute-start = (bf16[2,384,384]{2,1,0:T(8,128)(2,1)S(1)}, bf16[2,384,384]{2,1,0:T(8,128)(2,1)S(1)}, u32[]{:S(2)}, u32[]{:S(2)}) collective-permute-start(bf16[2,384,384]{2,1,0:T(8,128)(2,1)S(1)} %pad_maximum_fusion.own_ref), channel_id=1, source_target_pairs={{0,2},{1,3},{2,0},{3,1},{4,6},{5,7},{6,4},{7,5},{8,10},{9,11},{10,... | collective-permute-start | bytes 1769480 | tf_op jit(solution)/shard_map/ppermute | solution.py:304
  1.6 22.7 %collective-permute-start.2 = (bf16[384,768]{1,0:T(8,128)(2,1)S(1)}, bf16[384,768]{1,0:T(8,128)(2,1)S(1)}, u32[]{:S(2)}, u32[]{:S(2)}) collective-permute-start(bf16[384,768]{1,0:T(8,128)(2,1)S(1)} %bitcast.17), channel_id=1, source_target_pairs={{0,8},{1,9},{6,14},{7,15},{8,0},{9,1},{14,6},{15,7},{16,24},{17,25... | collective-permute-start | bytes 1769480 | tf_op jit(solution)/shard_map/ppermute | solution.py:303
  2.5 32.0 %collective-permute-start.4 = (bf16[2,384,384]{2,1,0:T(8,128)(2,1)S(1)}, bf16[2,384,384]{2,1,0:T(8,128)(2,1)S(1)}, u32[]{:S(2)}, u32[]{:S(2)}) collective-permute-start(bf16[2,384,384]{2,1,0:T(8,128)(2,1)S(1)} %pad_maximum_fusion.1.own_ref), channel_id=1, source_target_pairs={{0,2},{1,3},{2,0},{3,1},{4,6},{5,7},{6,4},{7,5},{8,10},{9,11},{10,... | collective-permute-start | bytes 1769480 | tf_op jit(solution)/shard_map/ppermute | solution.py:305
  15.6 19.6 %collective-permute-start.1 = (bf16[384,768]{1,0:T(8,128)(2,1)S(1)}, bf16[384,768]{1,0:T(8,128)(2,1)S(1)}, u32[]{:S(2)}, u32[]{:S(2)}) collective-permute-start(bf16[384,768]{1,0:T(8,128)(2,1)S(1)} %bitcast.18), channel_id=1, source_target_pairs={{2,10},{3,11},{4,12},{5,13},{10,2},{11,3},{12,4},{13,5},{18,26},{1... | collective-permute-start | bytes 1769480 | tf_op jit(solution)/shard_map/ppermute | solution.py:307
  19.8 26.5 %collective-permute-start.5 = (bf16[2,384,384]{2,1,0:T(8,128)(2,1)S(1)}, bf16[2,384,384]{2,1,0:T(8,128)(2,1)S(1)}, u32[]{:S(2)}, u32[]{:S(2)}) collective-permute-start(bf16[2,384,384]{2,1,0:T(8,128)(2,1)S(1)} %collective-permute-done.next_ref), channel_id=1, source_target_pairs={{0,4},{1,5},{6,2},{7,3},{8,12},{9,13},{14,10},{15,11},{16,20},{17,... | collective-permute-start | bytes 1769480 | tf_op jit(solution)/shard_map/ppermute | solution.py:308
  21.2 28.3 %collective-permute-start.3 = (bf16[2,384,384]{2,1,0:T(8,128)(2,1)S(1)}, bf16[2,384,384]{2,1,0:T(8,128)(2,1)S(1)}, u32[]{:S(2)}, u32[]{:S(2)}) collective-permute-start(bf16[2,384,384]{2,1,0:T(8,128)(2,1)S(1)} %pad_maximum_fusion.1.own_ref), channel_id=1, source_target_pairs={{2,4},{3,5},{4,2},{5,3},{10,12},{11,13},{12,10},{13,11},{18,20},{1... | collective-permute-start | bytes 1769480 | tf_op jit(solution)/shard_map/ppermute | solution.py:309
  24.4 34.2 %collective-permute-start.7 = (bf16[400,384]{1,0:T(8,128)(2,1)S(1)}, bf16[400,384]{1,0:T(8,128)(2,1)S(1)}, u32[]{:S(2)}, u32[]{:S(2)}) collective-permute-start(bf16[400,384]{1,0:T(8,128)(2,1)S(1)} %edge.2), channel_id=1, source_target_pairs={{8,0},{9,1},{14,6},{15,7},{0,8},{1,9},{6,14},{7,15},{24,16},{25,17... | collective-permute-start | bytes 921608 | tf_op jit(solution)/shard_map/ppermute | solution.py:313
  25.1 37.7 %slice-start = ((s8[9437184]{0:T(1024)(128)(4,1)}), s8[4194304]{0:T(1024)(128)(4,1)S(1)}, s32[]{:S(2)}) async-start(s8[9437184]{0:T(1024)(128)(4,1)} %bitcast.12), calls=%async_computation | async-start | bytes 8388608
  34.5 15.0 %collective-permute-start.6 = (bf16[400,384]{1,0:T(8,128)(2,1)S(1)}, bf16[400,384]{1,0:T(8,128)(2,1)S(1)}, u32[]{:S(2)}, u32[]{:S(2)}) collective-permute-start(bf16[400,384]{1,0:T(8,128)(2,1)S(1)} %edge.3), channel_id=1, source_target_pairs={{8,0},{9,1},{14,6},{15,7},{0,8},{1,9},{6,14},{7,15},{24,16},{25,17... | collective-permute-start | bytes 921608 | tf_op jit(solution)/shard_map/ppermute | solution.py:313
  35.2 27.6 %slice-start.1 = ((s8[9437184]{0:T(1024)(128)(4,1)}), s8[4194304]{0:T(1024)(128)(4,1)S(1)}, s32[]{:S(2)}) async-start(s8[9437184]{0:T(1024)(128)(4,1)} %bitcast.12), calls=%async_computation.1 | async-start | bytes 8388608
  47.6 12.5 %collective-permute-start.8 = (bf16[400,384]{1,0:T(8,128)(2,1)S(1)}, bf16[400,384]{1,0:T(8,128)(2,1)S(1)}, u32[]{:S(2)}, u32[]{:S(2)}) collective-permute-start(bf16[400,384]{1,0:T(8,128)(2,1)S(1)} %far.4), channel_id=1, source_target_pairs={{10,2},{11,3},{12,4},{13,5},{2,10},{3,11},{4,12},{5,13},{26,18},{2... | collective-permute-start | bytes 921608 | tf_op jit(solution)/shard_map/ppermute | solution.py:313
  51.0 14.3 %collective-permute-start.10 = (bf16[400,384]{1,0:T(8,128)(2,1)S(1)}, bf16[400,384]{1,0:T(8,128)(2,1)S(1)}, u32[]{:S(2)}, u32[]{:S(2)}) collective-permute-start(bf16[400,384]{1,0:T(8,128)(2,1)S(1)} %far.5), channel_id=1, source_target_pairs={{10,2},{11,3},{12,4},{13,5},{2,10},{3,11},{4,12},{5,13},{26,18},{2... | collective-permute-start | bytes 921608 | tf_op jit(solution)/shard_map/ppermute | solution.py:313
  55.3 7.6 %slice-start.2 = ((s8[9437184]{0:T(1024)(128)(4,1)}), s8[1048576]{0:T(1024)(128)(4,1)S(1)}, s32[]{:S(2)}) async-start(s8[9437184]{0:T(1024)(128)(4,1)} %bitcast.12), calls=%async_computation.2 | async-start | bytes 2097152
  60.8 2.1 %collective-permute-start.9 = (bf16[192,384]{1,0:T(8,128)(2,1)S(1)}, bf16[192,384]{1,0:T(8,128)(2,1)S(1)}, u32[]{:S(2)}, u32[]{:S(2)}) collective-permute-start(bf16[192,384]{1,0:T(8,128)(2,1)S(1)} %get-tuple-element.42), channel_id=1, source_target_pairs={{0,1},{1,0},{2,3},{3,2},{4,5},{5,4},{6,7},{7,6},{8,9},{9,8},{10,11... | collective-permute-start | bytes 442376 | tf_op jit(solution)/shard_map/ppermute | solution.py:340
  66.0 2.4 %collective-permute-start.11 = (bf16[192,384]{1,0:T(8,128)(2,1)S(1)}, bf16[192,384]{1,0:T(8,128)(2,1)S(1)}, u32[]{:S(2)}, u32[]{:S(2)}) collective-permute-start(bf16[192,384]{1,0:T(8,128)(2,1)S(1)} %get-tuple-element.45), channel_id=1, source_target_pairs={{0,1},{1,0},{2,3},{3,2},{4,5},{5,4},{6,7},{7,6},{8,9},{9,8},{10,11... | collective-permute-start | bytes 442376 | tf_op jit(solution)/shard_map/ppermute | solution.py:340

commit v5 on v4

--- a/solution.py
+++ b/solution.py
@@ -158,7 +158,7 @@
 
 def attend_far(query, far, state, everywhere, dtype):
     kernel = functools.partial(finish_kernel, everywhere)
-    return partial_call(kernel, "far", partial_shape(query), dtype, 1, 1.0, query, far, state)
+    return partial_call(kernel, "far", partial_shape(query), dtype, 1, 0.01, query, far, state)
 
 
 def join_kernel(steps, time_count, *refs):

time: 70.4 us -> 70.4 us (level)
  no operation moved by 1% of the time
where the time goes in v5:
time: 70.4 us; the launch traced here: 70.1 us
  waiting for transfers between devices  24.8 us (35%)
  starting transfers between devices  24.5 us (35%)
  Pallas kernels  18.7 us (27%)
  local copies, waits for them, and re-layouts  1.52 us (2%)
    pallas_call x10, Pallas kernels, partial_call(): pl.pallas_call(kernel, out_shape=jax.ShapeDtypeStruct(out_shape, dtype),...  13.6 us
    ppermute x1, waiting for transfers between devices, per_device(): next_0 = lax.ppermute(own_0, 'tm', next_route)  8.27 us
    ppermute x4, starting transfers between devices, back(): lax.ppermute(part, 'tm', reverse(route))  7.53 us
    ppermute x1, waiting for transfers between devices, per_device(): next_1 = lax.ppermute(own_1, 'tm', next_route)  7.32 us
    ppermute x1, waiting for transfers between devices, per_device(): far_0 = lax.ppermute(next_0, 'tm', far_route)  6.93 us
    ppermute x1, starting transfers between devices, per_device(): next_1 = lax.ppermute(own_1, 'tm', next_route)  4.82 us
    ppermute x1, starting transfers between devices, per_device(): lax.ppermute(inner_query, 'tm', route)  4.21 us
    pallas_call x3, Pallas kernels, project(): pl.pallas_call(functools.partial(project_kernel, first, swaps, total is n...  3.71 us
  transfers between devices with their start and end apart: 12, of which 6 were waited for; matrix products, arithmetic and copies ran while one was open for 0% of the time, Pallas kernels for 24%

profile of v5, /device:TPU:7, one launch (start us, length us, event | category | flops | bytes accessed | tf_op | source)
XLA Modules:
  0.0 70.1 jit_solution(2589290610518778056)
XLA Ops:
  0.0 1.2 %slice_bitcast_fusion = (bf16[1,384,384]{2,1,0:T(8,128)(2,1)S(1)}, bf16[1,384,384]{2,1,0:T(8,128)(2,1)S(1)}) fusion(bf16[384,768]{1,0:T(8,128)(2,1)} %bitcast.20, bf16[384,768]{1,0:T(8,128)(2,1)} %bitcast.22), kind=kLoop, calls=%fused_computation.2 | loop fusion | bytes 1179648 | tf_op jit(solution)/shard_map/stack | solution.py:298
  1.3 0.1 pad_maximum_fusion.own_ref
  1.3 0.3 collective-permute-start
  1.6 0.0 copy-done
  1.6 0.7 collective-permute-start.2
  2.4 0.1 pad_maximum_fusion.1.own_ref
  2.5 4.8 %collective-permute-start.4 = (bf16[2,384,384]{2,1,0:T(8,128)(2,1)S(1)}, bf16[2,384,384]{2,1,0:T(8,128)(2,1)S(1)}, u32[]{:S(2)}, u32[]{:S(2)}) collective-permute-start(bf16[2,384,384]{2,1,0:T(8,128)(2,1)S(1)} %pad_maximum_fusion.1.own_ref), channel_id=1, source_target_pairs={{0,2},{1,3},{2,0},{3,1},{4,6},{5,7},{6,4},{7,5},{8,10},{9,11},{10,... | collective-permute-start | bytes 1769480 | tf_op jit(solution)/shard_map/ppermute | solution.py:305
  7.3 8.3 %collective-permute-done.next_ref = bf16[2,384,384]{2,1,0:T(8,128)(2,1)S(1)} collective-permute-done((bf16[2,384,384]{2,1,0:T(8,128)(2,1)S(1)}, bf16[2,384,384]{2,1,0:T(8,128)(2,1)S(1)}, u32[]{:S(2)}, u32[]{:S(2)}) %collective-permute-start) | collective-permute-done | bytes 589856 | tf_op jit(solution)/shard_map/ppermute | solution.py:304
  15.6 4.2 %collective-permute-start.1 = (bf16[384,768]{1,0:T(8,128)(2,1)S(1)}, bf16[384,768]{1,0:T(8,128)(2,1)S(1)}, u32[]{:S(2)}, u32[]{:S(2)}) collective-permute-start(bf16[384,768]{1,0:T(8,128)(2,1)S(1)} %bitcast.18), channel_id=1, source_target_pairs={{2,10},{3,11},{4,12},{5,13},{10,2},{11,3},{12,4},{13,5},{18,26},{1... | collective-permute-start | bytes 1769480 | tf_op jit(solution)/shard_map/ppermute | solution.py:307
  19.8 1.3 %collective-permute-start.5 = (bf16[2,384,384]{2,1,0:T(8,128)(2,1)S(1)}, bf16[2,384,384]{2,1,0:T(8,128)(2,1)S(1)}, u32[]{:S(2)}, u32[]{:S(2)}) collective-permute-start(bf16[2,384,384]{2,1,0:T(8,128)(2,1)S(1)} %collective-permute-done.next_ref), channel_id=1, source_target_pairs={{0,4},{1,5},{6,2},{7,3},{8,12},{9,13},{14,10},{15,11},{16,20},{17,... | collective-permute-start | bytes 1769480 | tf_op jit(solution)/shard_map/ppermute | solution.py:308
  21.1 0.1 fusion.1
  21.2 3.1 %collective-permute-start.3 = (bf16[2,384,384]{2,1,0:T(8,128)(2,1)S(1)}, bf16[2,384,384]{2,1,0:T(8,128)(2,1)S(1)}, u32[]{:S(2)}, u32[]{:S(2)}) collective-permute-start(bf16[2,384,384]{2,1,0:T(8,128)(2,1)S(1)} %pad_maximum_fusion.1.own_ref), channel_id=1, source_target_pairs={{2,4},{3,5},{4,2},{5,3},{10,12},{11,13},{12,10},{13,11},{18,20},{1... | collective-permute-start | bytes 1769480 | tf_op jit(solution)/shard_map/ppermute | solution.py:309
  24.3 0.0 collective-permute-done.2
  24.3 0.1 fusion
  24.4 0.7 collective-permute-start.7
  25.1 0.0 slice-start
  25.1 2.0 %near.4.state_ref = f32[400,384]{1,0:T(8,128)S(1)} custom-call(bf16[384,384]{1,0:T(8,128)(2,1)S(1)} %get-tuple-element.38.q_ref, bf16[2,384,384]{2,1,0:T(8,128)(2,1)S(1)} %pad_maximum_fusion.own_ref, bf16[2,384,384]{2,1,0:T(8,128)(2,1)S(1)} %collective-permute-done.next_ref), custom_call_target="tpu_custom_call" | custom-call | flops 4529848 | bytes 17694 | tf_op jit(solution)/shard_map/near/pallas_call | solution.py:131
  27.2 7.3 %collective-permute-done.4.next_ref = bf16[2,384,384]{2,1,0:T(8,128)(2,1)S(1)} collective-permute-done((bf16[2,384,384]{2,1,0:T(8,128)(2,1)S(1)}, bf16[2,384,384]{2,1,0:T(8,128)(2,1)S(1)}, u32[]{:S(2)}, u32[]{:S(2)}) %collective-permute-start.4) | collective-permute-done | bytes 589856 | tf_op jit(solution)/shard_map/ppermute | solution.py:305
  34.5 0.7 collective-permute-start.6
  35.2 0.0 collective-permute-done.1
  35.2 0.1 fusion.2
  35.2 0.0 slice-start.1
  35.3 2.0 %near.5.state_ref = f32[400,384]{1,0:T(8,128)S(1)} custom-call(bf16[384,384]{1,0:T(8,128)(2,1)S(1)} %get-tuple-element.29.q_ref, bf16[2,384,384]{2,1,0:T(8,128)(2,1)S(1)} %pad_maximum_fusion.own_ref, bf16[2,384,384]{2,1,0:T(8,128)(2,1)S(1)} %collective-permute-done.next_ref), custom_call_target="tpu_custom_call" | custom-call | flops 4529848 | bytes 17694 | tf_op jit(solution)/shard_map/near/pallas_call | solution.py:131
  37.3 2.0 %near.6.state_ref = f32[400,384]{1,0:T(8,128)S(1)} custom-call(bf16[384,384]{1,0:T(8,128)(2,1)S(1)} %get-tuple-element.30.q_ref, bf16[2,384,384]{2,1,0:T(8,128)(2,1)S(1)} %pad_maximum_fusion.1.own_ref, bf16[2,384,384]{2,1,0:T(8,128)(2,1)S(1)} %collective-permute-done.4.next_ref), custom_call_target="tpu_custom_call" | custom-call | flops 4529848 | bytes 17694 | tf_op jit(solution)/shard_map/near/pallas_call | solution.py:131
  39.3 6.9 %collective-permute-done.5.far_ref = bf16[2,384,384]{2,1,0:T(8,128)(2,1)S(1)} collective-permute-done((bf16[2,384,384]{2,1,0:T(8,128)(2,1)S(1)}, bf16[2,384,384]{2,1,0:T(8,128)(2,1)S(1)}, u32[]{:S(2)}, u32[]{:S(2)}) %collective-permute-start.5) | collective-permute-done | bytes 589856 | tf_op jit(solution)/shard_map/ppermute | solution.py:308
  46.3 1.3 %far.4 = bf16[400,384]{1,0:T(8,128)(2,1)S(1)} custom-call(bf16[384,384]{1,0:T(8,128)(2,1)S(1)} %get-tuple-element.29.q_ref, bf16[2,384,384]{2,1,0:T(8,128)(2,1)S(1)} %collective-permute-done.5.far_ref, f32[400,384]{1,0:T(8,128)S(1)} %near.5.state_ref), custom_call_target="tpu_custom_call" | custom-call | flops 2264924 | bytes 11796 | tf_op jit(solution)/shard_map/far/pallas_call | solution.py:131
  47.6 1.9 %collective-permute-start.8 = (bf16[400,384]{1,0:T(8,128)(2,1)S(1)}, bf16[400,384]{1,0:T(8,128)(2,1)S(1)}, u32[]{:S(2)}, u32[]{:S(2)}) collective-permute-start(bf16[400,384]{1,0:T(8,128)(2,1)S(1)} %far.4), channel_id=1, source_target_pairs={{10,2},{11,3},{12,4},{13,5},{2,10},{3,11},{4,12},{5,13},{26,18},{2... | collective-permute-start | bytes 921608 | tf_op jit(solution)/shard_map/ppermute | solution.py:313
  49.5 0.0 collective-permute-done.6.refs_1_
  49.5 0.0 collective-permute-done.3.far_ref
  49.5 1.5 %far.5 = bf16[400,384]{1,0:T(8,128)(2,1)S(1)} custom-call(bf16[384,384]{1,0:T(8,128)(2,1)S(1)} %get-tuple-element.30.q_ref, bf16[2,384,384]{2,1,0:T(8,128)(2,1)S(1)} %collective-permute-done.3.far_ref, f32[400,384]{1,0:T(8,128)S(1)} %near.6.state_ref), custom_call_target="tpu_custom_call" | custom-call | flops 2264924 | bytes 11796 | tf_op jit(solution)/shard_map/far/pallas_call | solution.py:131
  51.0 4.3 %collective-permute-start.10 = (bf16[400,384]{1,0:T(8,128)(2,1)S(1)}, bf16[400,384]{1,0:T(8,128)(2,1)S(1)}, u32[]{:S(2)}, u32[]{:S(2)}) collective-permute-start(bf16[400,384]{1,0:T(8,128)(2,1)S(1)} %far.5), channel_id=1, source_target_pairs={{10,2},{11,3},{12,4},{13,5},{2,10},{3,11},{4,12},{5,13},{26,18},{2... | collective-permute-start | bytes 921608 | tf_op jit(solution)/shard_map/ppermute | solution.py:313
  55.3 0.0 slice-start.2
  55.3 2.0 %near.7.state_ref = f32[400,384]{1,0:T(8,128)S(1)} custom-call(bf16[384,384]{1,0:T(8,128)(2,1)S(1)} %get-tuple-element.37.q_ref, bf16[2,384,384]{2,1,0:T(8,128)(2,1)S(1)} %pad_maximum_fusion.1.own_ref, bf16[2,384,384]{2,1,0:T(8,128)(2,1)S(1)} %collective-permute-done.4.next_ref), custom_call_target="tpu_custom_call" | custom-call | flops 4529848 | bytes 17694 | tf_op jit(solution)/shard_map/near/pallas_call | solution.py:131
  57.3 1.4 %far.6.refs_0_ = f32[400,384]{1,0:T(8,128)S(1)} custom-call(bf16[384,384]{1,0:T(8,128)(2,1)S(1)} %get-tuple-element.37.q_ref, bf16[2,384,384]{2,1,0:T(8,128)(2,1)S(1)} %collective-permute-done.3.far_ref, f32[400,384]{1,0:T(8,128)S(1)} %near.7.state_ref), custom_call_target="tpu_custom_call" | custom-call | flops 2264924 | bytes 11796 | tf_op jit(solution)/shard_map/far/pallas_call | solution.py:131
  58.7 0.0 collective-permute-done.7.refs_1_
  58.7 1.3 %far.7.refs_0_ = f32[400,384]{1,0:T(8,128)S(1)} custom-call(bf16[384,384]{1,0:T(8,128)(2,1)S(1)} %get-tuple-element.38.q_ref, bf16[2,384,384]{2,1,0:T(8,128)(2,1)S(1)} %collective-permute-done.5.far_ref, f32[400,384]{1,0:T(8,128)S(1)} %near.4.state_ref), custom_call_target="tpu_custom_call" | custom-call | flops 2264924 | bytes 11796 | tf_op jit(solution)/shard_map/far/pallas_call | solution.py:131
  60.0 0.0 collective-permute-done.8.refs_2_
  60.0 0.7 %join.2 = (bf16[192,384]{1,0:T(8,128)(2,1)S(1)}, bf16[192,384]{1,0:T(8,128)(2,1)S(1)}) custom-call(f32[400,384]{1,0:T(8,128)S(1)} %far.7.refs_0_, bf16[400,384]{1,0:T(8,128)(2,1)S(1)} %collective-permute-done.7.refs_1_, bf16[400,384]{1,0:T(8,128)(2,1)S(1)} %collective-permute-done.8.refs_2_), custom_call_target="tpu_custom_call" | custom-call | flops 1179648 | bytes 1474560 | tf_op jit(solution)/shard_map/join/pallas_call | solution.py:208
  60.8 1.1 %collective-permute-start.9 = (bf16[192,384]{1,0:T(8,128)(2,1)S(1)}, bf16[192,384]{1,0:T(8,128)(2,1)S(1)}, u32[]{:S(2)}, u32[]{:S(2)}) collective-permute-start(bf16[192,384]{1,0:T(8,128)(2,1)S(1)} %get-tuple-element.42), channel_id=1, source_target_pairs={{0,1},{1,0},{2,3},{3,2},{4,5},{5,4},{6,7},{7,6},{8,9},{9,8},{10,11... | collective-permute-start | bytes 442376 | tf_op jit(solution)/shard_map/ppermute | solution.py:340
  61.9 1.0 %collective-permute-done.9.refs_1_ = bf16[192,384]{1,0:T(8,128)(2,1)S(1)} collective-permute-done((bf16[192,384]{1,0:T(8,128)(2,1)S(1)}, bf16[192,384]{1,0:T(8,128)(2,1)S(1)}, u32[]{:S(2)}, u32[]{:S(2)}) %collective-permute-start.9) | collective-permute-done | bytes 147488 | tf_op jit(solution)/shard_map/ppermute | solution.py:340
  62.9 0.0 slice-done.1
  62.9 1.4 %project.3.refs_2_ = f32[192,3072]{1,0:T(8,128)S(1)} custom-call(bf16[192,384]{1,0:T(8,128)(2,1)S(1)} %get-tuple-element.41.refs_0_, bf16[192,384]{1,0:T(8,128)(2,1)S(1)} %collective-permute-done.9.refs_1_, bf16[2,768,3072]{2,1,0:T(8,128)(2,1)S(1)} %bitcast.14), custom_call_target="tpu_custom_call" | custom-call | flops 905969664 | bytes 7077888 | tf_op jit(solution)/shard_map/project/pallas_call | solution.py:250
  64.3 1.0 %collective-permute-done.10.refs_2_ = bf16[400,384]{1,0:T(8,128)(2,1)S(1)} collective-permute-done((bf16[400,384]{1,0:T(8,128)(2,1)S(1)}, bf16[400,384]{1,0:T(8,128)(2,1)S(1)}, u32[]{:S(2)}, u32[]{:S(2)}) %collective-permute-start.10) | collective-permute-done | bytes 307232 | tf_op jit(solution)/shard_map/ppermute | solution.py:313
  65.3 0.7 %join.3 = (bf16[192,384]{1,0:T(8,128)(2,1)S(1)}, bf16[192,384]{1,0:T(8,128)(2,1)S(1)}) custom-call(f32[400,384]{1,0:T(8,128)S(1)} %far.6.refs_0_, bf16[400,384]{1,0:T(8,128)(2,1)S(1)} %collective-permute-done.6.refs_1_, bf16[400,384]{1,0:T(8,128)(2,1)S(1)} %collective-permute-done.10.refs_2_), custom_call_target="tpu_custom_call" | custom-call | flops 1179648 | bytes 1474560 | tf_op jit(solution)/shard_map/join/pallas_call | solution.py:208
  66.0 1.4 %collective-permute-start.11 = (bf16[192,384]{1,0:T(8,128)(2,1)S(1)}, bf16[192,384]{1,0:T(8,128)(2,1)S(1)}, u32[]{:S(2)}, u32[]{:S(2)}) collective-permute-start(bf16[192,384]{1,0:T(8,128)(2,1)S(1)} %get-tuple-element.45), channel_id=1, source_target_pairs={{0,1},{1,0},{2,3},{3,2},{4,5},{5,4},{6,7},{7,6},{8,9},{9,8},{10,11... | collective-permute-start | bytes 442376 | tf_op jit(solution)/shard_map/ppermute | solution.py:340
  67.4 0.8 %project.4.refs_2_ = f32[192,3072]{1,0:T(8,128)S(1)} custom-call(bf16[192,384]{1,0:T(8,128)(2,1)S(1)} %get-tuple-element.46.refs_0_, bf16[2,768,3072]{2,1,0:T(8,128)(2,1)S(1)} %bitcast.15, f32[192,3072]{1,0:T(8,128)S(1)} %project.3.refs_2_), custom_call_target="tpu_custom_call" | custom-call | flops 452984832 | bytes 4718592 | tf_op jit(solution)/shard_map/project/pallas_call | solution.py:250
  68.2 0.2 collective-permute-done.11.refs_0_
  68.4 1.5 %project.5 = bf16[192,3072]{1,0:T(8,128)(2,1)} custom-call(bf16[192,384]{1,0:T(8,128)(2,1)S(1)} %collective-permute-done.11.refs_0_, bf16[2,768,3072]{2,1,0:T(8,128)(2,1)S(1)} %bitcast.16, f32[192,3072]{1,0:T(8,128)S(1)} %project.4.refs_2_), custom_call_target="tpu_custom_call" | custom-call | flops 452984832 | bytes 4718592 | tf_op jit(solution)/shard_map/project/pallas_call | solution.py:250
  (12 shorter events, 0.1 us)
Async XLA Ops:
  0.0 2.4 %copy-start.2 = (bf16[1,384,768]{2,1,0:T(8,128)(2,1)S(1)}, bf16[1,384,768]{2,1,0:T(8,128)(2,1)}, u32[]{:S(2)}) copy-start(bf16[1,384,768]{2,1,0:T(8,128)(2,1)} %param.5) | copy-start | bytes 1769476
  0.0 2.3 %copy-start.1 = (bf16[1,384,768]{2,1,0:T(8,128)(2,1)S(1)}, bf16[1,384,768]{2,1,0:T(8,128)(2,1)}, u32[]{:S(2)}) copy-start(bf16[1,384,768]{2,1,0:T(8,128)(2,1)} %param.6) | copy-start | bytes 1769476
  0.0 1.6 %copy-start = (bf16[1,384,768]{2,1,0:T(8,128)(2,1)S(1)}, bf16[1,384,768]{2,1,0:T(8,128)(2,1)}, u32[]{:S(2)}) copy-start(bf16[1,384,768]{2,1,0:T(8,128)(2,1)} %param.4) | copy-start | bytes 1769476
  1.3 14.3 %collective-permute-start = (bf16[2,384,384]{2,1,0:T(8,128)(2,1)S(1)}, bf16[2,384,384]{2,1,0:T(8,128)(2,1)S(1)}, u32[]{:S(2)}, u32[]{:S(2)}) collective-permute-start(bf16[2,384,384]{2,1,0:T(8,128)(2,1)S(1)} %pad_maximum_fusion.own_ref), channel_id=1, source_target_pairs={{0,2},{1,3},{2,0},{3,1},{4,6},{5,7},{6,4},{7,5},{8,10},{9,11},{10,... | collective-permute-start | bytes 1769480 | tf_op jit(solution)/shard_map/ppermute | solution.py:304
  1.6 22.7 %collective-permute-start.2 = (bf16[384,768]{1,0:T(8,128)(2,1)S(1)}, bf16[384,768]{1,0:T(8,128)(2,1)S(1)}, u32[]{:S(2)}, u32[]{:S(2)}) collective-permute-start(bf16[384,768]{1,0:T(8,128)(2,1)S(1)} %bitcast.17), channel_id=1, source_target_pairs={{0,8},{1,9},{6,14},{7,15},{8,0},{9,1},{14,6},{15,7},{16,24},{17,25... | collective-permute-start | bytes 1769480 | tf_op jit(solution)/shard_map/ppermute | solution.py:303
  2.5 32.0 %collective-permute-start.4 = (bf16[2,384,384]{2,1,0:T(8,128)(2,1)S(1)}, bf16[2,384,384]{2,1,0:T(8,128)(2,1)S(1)}, u32[]{:S(2)}, u32[]{:S(2)}) collective-permute-start(bf16[2,384,384]{2,1,0:T(8,128)(2,1)S(1)} %pad_maximum_fusion.1.own_ref), channel_id=1, source_target_pairs={{0,2},{1,3},{2,0},{3,1},{4,6},{5,7},{6,4},{7,5},{8,10},{9,11},{10,... | collective-permute-start | bytes 1769480 | tf_op jit(solution)/shard_map/ppermute | solution.py:305
  15.6 19.6 %collective-permute-start.1 = (bf16[384,768]{1,0:T(8,128)(2,1)S(1)}, bf16[384,768]{1,0:T(8,128)(2,1)S(1)}, u32[]{:S(2)}, u32[]{:S(2)}) collective-permute-start(bf16[384,768]{1,0:T(8,128)(2,1)S(1)} %bitcast.18), channel_id=1, source_target_pairs={{2,10},{3,11},{4,12},{5,13},{10,2},{11,3},{12,4},{13,5},{18,26},{1... | collective-permute-start | bytes 1769480 | tf_op jit(solution)/shard_map/ppermute | solution.py:307
  19.8 26.5 %collective-permute-start.5 = (bf16[2,384,384]{2,1,0:T(8,128)(2,1)S(1)}, bf16[2,384,384]{2,1,0:T(8,128)(2,1)S(1)}, u32[]{:S(2)}, u32[]{:S(2)}) collective-permute-start(bf16[2,384,384]{2,1,0:T(8,128)(2,1)S(1)} %collective-permute-done.next_ref), channel_id=1, source_target_pairs={{0,4},{1,5},{6,2},{7,3},{8,12},{9,13},{14,10},{15,11},{16,20},{17,... | collective-permute-start | bytes 1769480 | tf_op jit(solution)/shard_map/ppermute | solution.py:308
  21.2 28.3 %collective-permute-start.3 = (bf16[2,384,384]{2,1,0:T(8,128)(2,1)S(1)}, bf16[2,384,384]{2,1,0:T(8,128)(2,1)S(1)}, u32[]{:S(2)}, u32[]{:S(2)}) collective-permute-start(bf16[2,384,384]{2,1,0:T(8,128)(2,1)S(1)} %pad_maximum_fusion.1.own_ref), channel_id=1, source_target_pairs={{2,4},{3,5},{4,2},{5,3},{10,12},{11,13},{12,10},{13,11},{18,20},{1... | collective-permute-start | bytes 1769480 | tf_op jit(solution)/shard_map/ppermute | solution.py:309
  24.4 34.2 %collective-permute-start.7 = (bf16[400,384]{1,0:T(8,128)(2,1)S(1)}, bf16[400,384]{1,0:T(8,128)(2,1)S(1)}, u32[]{:S(2)}, u32[]{:S(2)}) collective-permute-start(bf16[400,384]{1,0:T(8,128)(2,1)S(1)} %edge.2), channel_id=1, source_target_pairs={{8,0},{9,1},{14,6},{15,7},{0,8},{1,9},{6,14},{7,15},{24,16},{25,17... | collective-permute-start | bytes 921608 | tf_op jit(solution)/shard_map/ppermute | solution.py:313
  25.1 37.7 %slice-start = ((s8[9437184]{0:T(1024)(128)(4,1)}), s8[4194304]{0:T(1024)(128)(4,1)S(1)}, s32[]{:S(2)}) async-start(s8[9437184]{0:T(1024)(128)(4,1)} %bitcast.12), calls=%async_computation | async-start | bytes 8388608
  34.5 15.0 %collective-permute-start.6 = (bf16[400,384]{1,0:T(8,128)(2,1)S(1)}, bf16[400,384]{1,0:T(8,128)(2,1)S(1)}, u32[]{:S(2)}, u32[]{:S(2)}) collective-permute-start(bf16[400,384]{1,0:T(8,128)(2,1)S(1)} %edge.3), channel_id=1, source_target_pairs={{8,0},{9,1},{14,6},{15,7},{0,8},{1,9},{6,14},{7,15},{24,16},{25,17... | collective-permute-start | bytes 921608 | tf_op jit(solution)/shard_map/ppermute | solution.py:313
  35.2 27.6 %slice-start.1 = ((s8[9437184]{0:T(1024)(128)(4,1)}), s8[4194304]{0:T(1024)(128)(4,1)S(1)}, s32[]{:S(2)}) async-start(s8[9437184]{0:T(1024)(128)(4,1)} %bitcast.12), calls=%async_computation.1 | async-start | bytes 8388608
  47.6 12.5 %collective-permute-start.8 = (bf16[400,384]{1,0:T(8,128)(2,1)S(1)}, bf16[400,384]{1,0:T(8,128)(2,1)S(1)}, u32[]{:S(2)}, u32[]{:S(2)}) collective-permute-start(bf16[400,384]{1,0:T(8,128)(2,1)S(1)} %far.4), channel_id=1, source_target_pairs={{10,2},{11,3},{12,4},{13,5},{2,10},{3,11},{4,12},{5,13},{26,18},{2... | collective-permute-start | bytes 921608 | tf_op jit(solution)/shard_map/ppermute | solution.py:313
  51.0 14.3 %collective-permute-start.10 = (bf16[400,384]{1,0:T(8,128)(2,1)S(1)}, bf16[400,384]{1,0:T(8,128)(2,1)S(1)}, u32[]{:S(2)}, u32[]{:S(2)}) collective-permute-start(bf16[400,384]{1,0:T(8,128)(2,1)S(1)} %far.5), channel_id=1, source_target_pairs={{10,2},{11,3},{12,4},{13,5},{2,10},{3,11},{4,12},{5,13},{26,18},{2... | collective-permute-start | bytes 921608 | tf_op jit(solution)/shard_map/ppermute | solution.py:313
  55.3 7.6 %slice-start.2 = ((s8[9437184]{0:T(1024)(128)(4,1)}), s8[1048576]{0:T(1024)(128)(4,1)S(1)}, s32[]{:S(2)}) async-start(s8[9437184]{0:T(1024)(128)(4,1)} %bitcast.12), calls=%async_computation.2 | async-start | bytes 2097152
  60.8 2.1 %collective-permute-start.9 = (bf16[192,384]{1,0:T(8,128)(2,1)S(1)}, bf16[192,384]{1,0:T(8,128)(2,1)S(1)}, u32[]{:S(2)}, u32[]{:S(2)}) collective-permute-start(bf16[192,384]{1,0:T(8,128)(2,1)S(1)} %get-tuple-element.42), channel_id=1, source_target_pairs={{0,1},{1,0},{2,3},{3,2},{4,5},{5,4},{6,7},{7,6},{8,9},{9,8},{10,11... | collective-permute-start | bytes 442376 | tf_op jit(solution)/shard_map/ppermute | solution.py:340
  66.0 2.4 %collective-permute-start.11 = (bf16[192,384]{1,0:T(8,128)(2,1)S(1)}, bf16[192,384]{1,0:T(8,128)(2,1)S(1)}, u32[]{:S(2)}, u32[]{:S(2)}) collective-permute-start(bf16[192,384]{1,0:T(8,128)(2,1)S(1)} %get-tuple-element.45), channel_id=1, source_target_pairs={{0,1},{1,0},{2,3},{3,2},{4,5},{5,4},{6,7},{7,6},{8,9},{9,8},{10,11... | collective-permute-start | bytes 442376 | tf_op jit(solution)/shard_map/ppermute | solution.py:340
